TPU v7x, 256 devices: a whole 4x4x8 slice. The times are simulated.
256 devices in a mesh: table: 32 (over y, z), dp: 8 (over x, core).
Axes of the slice: x: 4, y: 4, z: 8, core: 2. Of those that a mesh axis runs over, the one named last changes fastest.
Arguments:
- dense_input: bfloat16 [32768, 512], P(('table', 'dp')), may hold values from -6 to 6
- bottom_weight: bfloat16 [512, 512], replicated, may hold values from -0.059814453 to 0.059814453
- cold_table: bfloat16 [1048576, 64], P('table'), may hold values from -0.8984375 to 0.8984375
- projection: bfloat16 [256, 512], replicated, may hold values from -0.375 to 0.375
- hot_table: bfloat16 [1024, 512], replicated, may hold values from -0.41992188 to 0.41992188
- cold_owner: int32 [32768, 7, 4, 1], P(('table', 'dp')), may hold values from 0 to 31; in each aligned block of 3584 rows (0 to 3583, 3584 to 7167, ..., all dimensions but the last counted through in order) at most 224 rows name the same one
- cold_local: int32 [32768, 7, 4], P(('table', 'dp')), may hold values from 0 to 32767
- cold_band: int32 [32768, 7, 4], P(('table', 'dp')), may hold values from 0 to 3
- hot_unique: int32 [65536], P(('table', 'dp')), may hold values from 0 to 1023, as said below
- hot_map: int32 [32768, 8, 4], P(('table', 'dp')), may hold values from 0 to 255
- grad_inter: float32 [32768, 256], P(('table', 'dp')), may hold values from -0.3 to 0.3
Outputs:
- interactions: float32 [32768, 256], P(('table', 'dp'))
- cold_grad: float32 [1048576, 64], P(('table', 'dp'))
- hot_grad: float32 [1024, 512], P('table')
- projection_grad: float32 [256, 512], P('table')
- bottom_grad: float32 [512, 512], P('table')
Inputs may be any that keep to these rules, and one draw needn't show every extreme that they name: `cold_owner`: among the 3584 cold lookups of one device (aligned blocks of samples in order), no shard is named more than 224 times, a bound that some block reaches. `hot_unique`: the 256 ids in each device's block are distinct. `hot_map`: positions refer to the list of the device that holds the sample.
All inputs are finite; a program needn't handle non-finite values.
Results may differ from a plain program's by a relative error of at most 0.0052.
Values may be sent and summed in bfloat16 or wider, within the bound.
No kernel may reach another device: no remote copies, remote signals or barrier semaphores. Data moves between devices by JAX's collectives and lax.ppermute only.
A program may use at most 128 MiB of HBM per device.

v0:
```python
import jax
import jax.numpy as jnp
from jax import lax
from jax.sharding import PartitionSpec as P


def silu_slope(pre):
    sigma = jax.nn.sigmoid(pre)
    return sigma * (1.0 + pre * (1.0 - sigma))


def shards(
    dense_input,
    bottom_weight,
    cold_table,
    projection,
    hot_table,
    cold_owner,
    cold_local,
    cold_band,
    hot_unique,
    hot_map,
    grad_inter,
):
    batch_rows = dense_input.shape[0]
    cold_feats = cold_local.shape[1]
    bag_size = cold_local.shape[2]
    hot_feats = hot_map.shape[1]
    tables = lax.axis_size("table")
    rows_dev = cold_table.shape[0]
    cold_width = cold_table.shape[1]
    hidden = projection.shape[1]
    band_count = projection.shape[0] // cold_width
    unique_count = hot_unique.shape[0]
    feats = 1 + cold_feats + hot_feats
    lookups = batch_rows * cold_feats * bag_size
    capacity = 2 * lookups // tables
    highest = lax.Precision.HIGHEST
    owner_ids = cold_owner.reshape(lookups)
    local_rows = cold_local.reshape(lookups)
    owner_hits = (owner_ids[:, None] == jnp.arange(tables, dtype=jnp.int32)[None, :]).astype(
        jnp.int32
    )
    running = jnp.cumsum(owner_hits, axis=0)
    slot_ids = jnp.sum((running - 1) * owner_hits, axis=1)
    position = owner_ids * capacity + slot_ids
    send_ids = (
        jnp.zeros((tables * capacity,), jnp.int32)
        .at[position]
        .set(local_rows)
        .reshape(tables, capacity)
    )
    asked = lax.all_to_all(send_ids, "table", split_axis=0, concat_axis=0, tiled=True)
    fetched = cold_table[asked]
    received = lax.all_to_all(fetched, "table", split_axis=0, concat_axis=0, tiled=True)
    arrived = received.reshape(tables * capacity, cold_width)[position].reshape(
        batch_rows * cold_feats, bag_size, cold_width
    )
    pre = jnp.dot(dense_input, bottom_weight, preferred_element_type=jnp.float32)
    bottom = jax.nn.silu(pre).astype(jnp.bfloat16)
    unique_rows = hot_table[hot_unique]
    counts = jnp.sum(
        (
            hot_map.reshape(batch_rows * hot_feats, bag_size)[:, :, None]
            == jnp.arange(unique_count, dtype=jnp.int32)
        ).astype(jnp.int32),
        axis=1,
    ).astype(jnp.bfloat16)
    hot_emb = jnp.dot(counts, unique_rows, preferred_element_type=jnp.float32).astype(jnp.bfloat16)
    band_mask = (
        cold_band.reshape(batch_rows * cold_feats, bag_size)[..., None]
        == jnp.arange(band_count, dtype=jnp.int32)
    ).astype(jnp.bfloat16)
    pooled = jnp.einsum(
        "qln,qlc->qnc", band_mask, arrived, preferred_element_type=jnp.float32
    ).astype(jnp.bfloat16)
    pooled = pooled.reshape(batch_rows * cold_feats, band_count * cold_width)
    cold_emb = jnp.dot(pooled, projection, preferred_element_type=jnp.float32).astype(jnp.bfloat16)
    stack = jnp.concatenate(
        [
            bottom[:, None, :],
            cold_emb.reshape(batch_rows, cold_feats, hidden),
            hot_emb.reshape(batch_rows, hot_feats, hidden),
        ],
        axis=1,
    )
    inter = jnp.einsum("bfe,bge->bfg", stack, stack, preferred_element_type=jnp.float32)
    grad_block = grad_inter.reshape(batch_rows, feats, feats)
    sym = grad_block + jnp.swapaxes(grad_block, 1, 2)
    d_stack = jnp.einsum("bfg,bge->bfe", sym, stack.astype(jnp.float32), precision=highest).astype(
        jnp.bfloat16
    )
    d_cold = d_stack[:, 1 : 1 + cold_feats].reshape(batch_rows * cold_feats, hidden)
    d_pool = jnp.einsum("qo,ko->qk", d_cold, projection, preferred_element_type=jnp.float32).astype(
        jnp.bfloat16
    )
    d_rows = jnp.einsum(
        "qln,qnc->qlc",
        band_mask,
        d_pool.reshape(batch_rows * cold_feats, band_count, cold_width),
        preferred_element_type=jnp.float32,
    ).astype(jnp.bfloat16)
    grad_slots = (
        jnp.zeros((tables * capacity, cold_width), jnp.bfloat16)
        .at[position]
        .set(d_rows.reshape(lookups, cold_width))
        .reshape(tables, capacity, cold_width)
    )
    returned = lax.all_to_all(grad_slots, "table", split_axis=0, concat_axis=0, tiled=True)
    cold_sum = (
        jnp.zeros((rows_dev, cold_width), jnp.float32)
        .at[asked.reshape(-1)]
        .add(returned.reshape(-1, cold_width).astype(jnp.float32))
    )
    cold_grad = lax.psum_scatter(cold_sum, "dp", scatter_dimension=0, tiled=True)
    d_pre = (d_stack[:, 0].astype(jnp.float32) * silu_slope(pre)).astype(jnp.bfloat16)
    bottom_part = jnp.einsum("bi,bo->io", dense_input, d_pre, preferred_element_type=jnp.float32)
    proj_part = jnp.einsum("qk,qo->ko", pooled, d_cold, preferred_element_type=jnp.float32)
    d_hot = d_stack[:, 1 + cold_feats :].reshape(batch_rows * hot_feats, hidden)
    d_unique = jnp.einsum("qu,qo->uo", counts, d_hot, preferred_element_type=jnp.float32)
    hot_part = jnp.zeros((hot_table.shape[0], hidden), jnp.float32).at[hot_unique].add(d_unique)
    summed = lax.psum((hot_part, proj_part, bottom_part), "dp")
    hot_grad, projection_grad, bottom_grad = (
        lax.psum_scatter(summed[0], "table", scatter_dimension=0, tiled=True),
        lax.psum_scatter(summed[1], "table", scatter_dimension=0, tiled=True),
        lax.psum_scatter(summed[2], "table", scatter_dimension=0, tiled=True),
    )
    return (
        inter.reshape(batch_rows, feats * feats),
        cold_grad,
        hot_grad,
        projection_grad,
        bottom_grad,
    )


def solution(mesh):
    placed = (
        P(("table", "dp"), None),
        P(),
        P("table", None),
        P(),
        P(),
        P(("table", "dp"), None, None, None),
        P(("table", "dp"), None, None),
        P(("table", "dp"), None, None),
        P(("table", "dp")),
        P(("table", "dp"), None, None),
        P(("table", "dp"), None),
    )
    return jax.shard_map(
        shards,
        mesh=mesh,
        in_specs=placed,
        out_specs=(
            P(("table", "dp"), None),
            P(("table", "dp"), None),
            P("table", None),
            P("table", None),
            P("table", None),
        ),
        check_vma=False,
    )
```

profile of v0, /device:TPU:8, one launch (start us, length us, event | category | flops | bytes accessed | tf_op | source)
XLA Modules:
  0.0 966.7 jit_solution(3687475771546508554)
XLA Ops:
  7.2 0.8 broadcast_multiply_fusion
  8.0 1.0 copy.103
  9.4 0.3 copy.102
  9.7 0.2 mul.35
  10.0 9.2 reduce-window.6
  19.2 0.8 slice_reduce_fusion
  20.4 0.3 copy.105
  20.9 0.3 fusion.20
  21.2 13.7 %scatter_custom_fusion = s32[7168]{0:T(1024)S(1)} fusion(s32[3584]{0:T(1024)S(1)} %fusion.28, s32[3584]{0:T(1024)S(1)} %reshape.213, s32[]{:T(128)} %constant.10.clone.1), kind=kCustom, calls=%fused_computation.59 | custom fusion | bytes 28676 | tf_op jit(solution)/shard_map/scatter | solution.py:50
  34.9 0.7 all_to_all.14
  35.6 11.7 %all-to-all-start = ((s32[32,1,224]{2,1,0:T(1,128)}), s32[32,1,224]{2,1,0:T(1,128)S(1)}, u32[]{:S(2)}, u32[]{:S(2)}) async-start(s32[32,1,224]{2,1,0:T(1,128)} %all_to_all.14), calls=%async_computation | async-start | bytes 65536 | tf_op jit(solution)/shard_map/all_to_all | solution.py:53
  47.3 8.4 copy.106
  55.7 0.3 all-to-all-done
  56.2 23.6 %gather_fusion = bf16[7168,64]{1,0:T(8,128)(2,1)S(1)} fusion(bf16[32768,64]{1,0:T(8,128)(2,1)} %copy.106, s32[7168]{0:T(1024)S(1)} %broadcast_clamp_fusion), kind=kCustom, calls=%fused_computation | custom fusion | bytes 1863680 | tf_op jit(solution)/shard_map/gather | solution.py:54
  79.9 1.6 copy.107
  81.5 9.7 %all-to-all-start.1 = ((bf16[32,224,64]{1,2,0:T(8,128)(2,1)}), bf16[32,224,64]{1,2,0:T(8,128)(2,1)}, u32[]{:S(2)}, u32[]{:S(2)}) async-start(bf16[32,224,64]{1,2,0:T(8,128)(2,1)} %copy.107), calls=%async_computation.1 | async-start | bytes 2097152 | tf_op jit(solution)/shard_map/all_to_all | solution.py:55
  91.2 0.2 reduce-scatter.9.cloned.1.call-start
  91.5 0.2 fusion.34
  91.8 0.7 copy-done.5
  93.0 0.2 eq.55
  93.5 1.0 copy.101
  94.5 1.4 copy.116
  95.9 1.2 gather_fusion.2
  97.1 1.5 convert_reduce_fusion
  98.6 1.4 fusion.6
  100.0 17.0 %all-to-all-done.1 = bf16[32,224,64]{1,2,0:T(8,128)(2,1)} async-done(((bf16[32,224,64]{1,2,0:T(8,128)(2,1)}), bf16[32,224,64]{1,2,0:T(8,128)(2,1)}, u32[]{:S(2)}, u32[]{:S(2)}) %all-to-all-start.1) | async-done | bytes 917536 | tf_op jit(solution)/shard_map/all_to_all | solution.py:55
  117.1 1.9 copy.108
  119.0 8.1 gather_fusion.1
  127.0 4.1 fusion.4
  131.1 1.1 copy.110
  132.2 0.4 convolution_convert_fusion.1
  132.7 1.3 reshape.173
  133.9 4.1 fusion.16
  138.0 1.2 copy.140
  139.3 1.7 fusion.7
  140.9 4.0 scatter_custom_fusion.3
  145.0 0.3 reduce-scatter.13.cloned.1.call-start
  145.3 1.3 convolution_bitcast_fusion
  146.6 2.5 copy.129
  149.4 0.5 copy.118
  150.0 0.3 reshape.178
  150.3 0.5 convolution_convert_fusion.2
  150.8 1.1 copy.119
  151.9 3.8 fusion.5
  155.7 10.5 %scatter_custom_fusion.1 = bf16[7168,64]{1,0:T(8,128)(2,1)S(1)} fusion(s32[3584]{0:T(1024)S(1)} %fusion.28, bf16[3584,64]{1,0:T(8,128)(2,1)} %bitcast.83, bf16[]{:T(256)} %constant.17.clone.1), kind=kCustom, calls=%fused_computation.28 | custom fusion | bytes 918016 | tf_op jit(solution)/shard_map/scatter | solution.py:106
  166.2 1.6 copy.120
  167.8 7.3 all-to-all-start.2
  175.2 1.2 fusion.35
  176.6 26.2 %all-to-all-done.2 = bf16[32,224,64]{1,2,0:T(8,128)(2,1)S(1)} async-done(((bf16[32,224,64]{1,2,0:T(8,128)(2,1)}), bf16[32,224,64]{1,2,0:T(8,128)(2,1)S(1)}, u32[]{:S(2)}, u32[]{:S(2)}) %all-to-all-start.2) | async-done | bytes 917536 | tf_op jit(solution)/shard_map/all_to_all | solution.py:109
  202.8 2.2 copy.128
  205.1 51.4 %scatter_custom_fusion.2 = f32[32768,64]{1,0:T(8,128)} fusion(s32[7168]{0:T(1024)S(1)} %bitcast.82, f32[7168,64]{1,0:T(8,128)} %bitcast.75, f32[]{:T(128)} %constant.5.clone.1), kind=kCustom, calls=%fused_computation.7 | custom fusion | flops 458752 | bytes 8389120 | tf_op jit(solution)/shard_map/scatter-add | solution.py:113
  256.5 107.0 %reduce-scatter.9.cloned.1.call-done = f32[32,512]{1,0:T(8,128)} async-done(((f32[1024,512]{1,0:T(8,128)}), f32[32,512]{1,0:T(8,128)}) %reduce-scatter.9.cloned.1.call-update) | async-done | bytes 65552 | tf_op jit(solution)/shard_map/reduce_scatter | solution.py:124
  363.6 1.6 fusion.17
  365.2 0.4 copy.113
  365.6 0.8 copy.124
  366.4 214.3 %reduce-scatter.13.cloned.1.call-done = f32[16,512]{1,0:T(8,128)} async-done(((f32[512,512]{1,0:T(8,128)}), f32[16,512]{1,0:T(8,128)}) %reduce-scatter.13.cloned.1.call-update) | async-done | bytes 32784
  580.6 0.9 copy.130
  581.5 215.1 %reduce-scatter.11.cloned.1.call-done = f32[8,512]{1,0:T(8,128)} async-done(((f32[256,512]{1,0:T(8,128)}), f32[8,512]{1,0:T(8,128)}) %reduce-scatter.11.cloned.1.call-update) | async-done | bytes 16400 | tf_op jit(solution)/shard_map/reduce_scatter | solution.py:125
  796.6 28.0 %all-reduce = (f32[8,512]{1,0:T(8,128)}, f32[16,512]{0,1:T(8,128)S(1)}) all-reduce(f32[8,512]{1,0:T(8,128)} %reduce-scatter.11.cloned.1.call-done, f32[16,512]{0,1:T(8,128)S(1)} %copy.130), channel_id=1, replica_groups=mesh['table'=32,'dp'=8] {'dp'}, use_global_device_ids=true, to_apply=%region_11.12 | all-reduce | flops 12288 | bytes 98304 | tf_op jit(solution)/shard_map/psum | solution.py:122
  824.6 0.7 copy.126
  825.3 68.3 %reduce-scatter.7.cloned.1.call-done = f32[4096,64]{1,0:T(8,128)} async-done(((f32[32768,64]{1,0:T(8,128)}), f32[4096,64]{1,0:T(8,128)}) %reduce-scatter.7.cloned.1.call-update) | async-done | bytes 1048592 | tf_op jit(solution)/shard_map/reduce_scatter | solution.py:115
  893.6 3.1 copy.125
  896.7 62.0 %all-reduce.3.cloned.1.call-done = f32[32,512]{1,0:T(8,128)} async-done(((f32[32,512]{1,0:T(8,128)}), f32[32,512]{1,0:T(8,128)}) %all-reduce.3.cloned.1.call-update) | async-done | bytes 65552 | tf_op jit(solution)/shard_map/psum | solution.py:122
  958.7 1.5 copy.142
  (72 shorter events, 2.8 us)
Async XLA Ops:
  7.2 88.8 %copy-start = (bf16[1024,512]{1,0:T(8,128)(2,1)S(1)}, bf16[1024,512]{1,0:T(8,128)(2,1)}, u32[]{:S(2)}) copy-start(bf16[1024,512]{1,0:T(8,128)(2,1)} %param.15) | copy-start | bytes 3145732
  9.4 11.0 %copy-start.17 = (s32[128,7,4]{0,2,1:T(4,128)S(1)}, s32[128,7,4]{0,2,1:T(4,128)}, u32[]{:S(2)}) copy-start(s32[128,7,4]{0,2,1:T(4,128)} %param.17) | copy-start | bytes 43012
  35.6 20.4 %all-to-all-start = ((s32[32,1,224]{2,1,0:T(1,128)}), s32[32,1,224]{2,1,0:T(1,128)S(1)}, u32[]{:S(2)}, u32[]{:S(2)}) async-start(s32[32,1,224]{2,1,0:T(1,128)} %all_to_all.14), calls=%async_computation | async-start | bytes 65536 | tf_op jit(solution)/shard_map/all_to_all | solution.py:53
  79.8 11.7 %copy-start.9 = (bf16[512,512]{1,0:T(8,128)(2,1)S(1)}, bf16[512,512]{1,0:T(8,128)(2,1)}, u32[]{:S(2)}) copy-start(bf16[512,512]{1,0:T(8,128)(2,1)} %param.12) | copy-start | bytes 1572868
  81.5 9.9 %copy-start.15 = (f32[128,256]{1,0:T(8,128)S(1)}, f32[128,256]{1,0:T(8,128)}, u32[]{:S(2)}) copy-start(f32[128,256]{1,0:T(8,128)} %param.21) | copy-start | bytes 393220
  81.5 10.1 %copy-start.13 = (bf16[128,512]{1,0:T(8,128)(2,1)S(1)}, bf16[128,512]{1,0:T(8,128)(2,1)}, u32[]{:S(2)}) copy-start(bf16[128,512]{1,0:T(8,128)(2,1)} %param.11) | copy-start | bytes 393220
  81.5 11.3 %copy-start.18 = (s32[128,7,4]{0,2,1:T(4,128)S(1)}, s32[128,7,4]{0,2,1:T(4,128)}, u32[]{:S(2)}) copy-start(s32[128,7,4]{0,2,1:T(4,128)} %param.18) | copy-start | bytes 43012
  81.5 11.7 %copy-start.16 = (s32[128,8,4]{0,2,1:T(4,128)S(1)}, s32[128,8,4]{0,2,1:T(4,128)}, u32[]{:S(2)}) copy-start(s32[128,8,4]{0,2,1:T(4,128)} %param.20) | copy-start | bytes 49156
  81.5 35.6 %all-to-all-start.1 = ((bf16[32,224,64]{1,2,0:T(8,128)(2,1)}), bf16[32,224,64]{1,2,0:T(8,128)(2,1)}, u32[]{:S(2)}, u32[]{:S(2)}) async-start(bf16[32,224,64]{1,2,0:T(8,128)(2,1)} %copy.107), calls=%async_computation.1 | async-start | bytes 2097152 | tf_op jit(solution)/shard_map/all_to_all | solution.py:55
  91.2 272.3 %reduce-scatter.9.cloned.1.call-start = ((), (), s32[]{:S(2)}) async-start(), calls=%async_computation.8 | async-start | bytes 2162688 | tf_op jit(solution)/shard_map/reduce_scatter | solution.py:124
  91.8 0.7 copy-start.5
  92.5 3.4 copy-start.19
  92.8 41.1 %copy-start.11 = (bf16[128,1,512]{2,1,0:T(2,128)(2,1)}, bf16[128,1,512]{2,1,0:T(2,128)(2,1)S(1)}, u32[]{:S(2)}) copy-start(bf16[128,1,512]{2,1,0:T(2,128)(2,1)S(1)} %copy.112) | copy-start | bytes 393220
  127.0 5.2 copy-start.4
  132.2 1.7 copy-start.2
  140.9 4.3 copy-start.6
  140.9 4.3 copy-start.14
  145.0 435.6 %reduce-scatter.13.cloned.1.call-start = ((), (), s32[]{:S(2)}) async-start(), calls=%async_computation.11 | async-start | bytes 1081344
  150.0 1.9 copy-start.10
  166.2 9.0 copy-start.3
  167.8 35.0 %all-to-all-start.2 = ((bf16[32,224,64]{1,2,0:T(8,128)(2,1)}), bf16[32,224,64]{1,2,0:T(8,128)(2,1)S(1)}, u32[]{:S(2)}, u32[]{:S(2)}) async-start(bf16[32,224,64]{1,2,0:T(8,128)(2,1)} %copy.120), calls=%async_computation.2 | async-start | bytes 2097152 | tf_op jit(solution)/shard_map/all_to_all | solution.py:109
  175.2 621.4 %reduce-scatter.11.cloned.1.call-start = ((), (), s32[]{:S(2)}) async-start(), calls=%async_computation.10 | async-start | bytes 540672 | tf_op jit(solution)/shard_map/reduce_scatter | solution.py:125
  176.5 717.1 %reduce-scatter.7.cloned.1.call-start = ((), (), s32[]{:S(2)}) async-start(), calls=%async_computation.7 | async-start | bytes 18874368 | tf_op jit(solution)/shard_map/reduce_scatter | solution.py:115
  256.4 107.1 %copy-start.7 = (bf16[128,8,512]{2,1,0:T(8,128)(2,1)S(1)}, bf16[128,8,512]{2,1,0:T(8,128)(2,1)}, u32[]{:S(2)}) copy-start(bf16[128,8,512]{2,1,0:T(8,128)(2,1)} %fusion.6) | copy-start | bytes 3145732
  256.4 107.1 %copy-start.8 = (bf16[128,7,512]{2,1,0:T(8,128)(2,1)S(1)}, bf16[128,7,512]{2,1,0:T(8,128)(2,1)}, u32[]{:S(2)}) copy-start(bf16[128,7,512]{2,1,0:T(8,128)(2,1)} %reshape.173) | copy-start | bytes 2752516
  256.4 107.1 %copy-start.12 = (bf16[128,1,512]{2,1,0:T(2,128)(2,1)S(1)}, bf16[128,1,512]{2,1,0:T(2,128)(2,1)}, u32[]{:S(2)}) copy-start(bf16[128,1,512]{2,1,0:T(2,128)(2,1)} %copy-done.11) | copy-start | bytes 393220
  256.4 702.3 %all-reduce.3.cloned.1.call-start = ((), (), s32[]{:S(2)}) async-start(), calls=%async_computation.9 | async-start | bytes 131072 | tf_op jit(solution)/shard_map/psum | solution.py:122
  365.6 594.6 %copy-start.1 = (bf16[1024,512]{1,0:T(8,128)(2,1)S(1)}, bf16[1024,512]{1,0:T(8,128)(2,1)}, u32[]{:S(2)}) copy-start(bf16[1024,512]{1,0:T(8,128)(2,1)} %param.15) | copy-start | bytes 3145732
Sparse Core Ops, SparseCore 0:
  145.1 218.3 reduce-scatter.8
  367.8 212.7 reduce-scatter.12
  584.9 211.6 reduce-scatter.10
  799.0 94.4 reduce-scatter.6
  895.7 62.9 all-reduce.2
where the time goes:
time: 968 us; the launch traced here: 967 us
  waiting for transfers between devices  710 us (73%)
  local copies, waits for them, and re-layouts  96.3 us (10%)
  other arithmetic  68.1 us (7%)
  starting transfers between devices  29.3 us (3%)
  blocking collectives  28 us (3%)
  matrix products  20.4 us (2%)
  between operations  14.3 us (1%)
    reduce_scatter x1, waiting for transfers between devices, shards(): lax.psum_scatter(summed[1], 'table', scatter_dimension=0, tiled=True)  215 us
    unnamed x6, waiting for transfers between devices  214 us
    reduce_scatter x1, waiting for transfers between devices, shards(): lax.psum_scatter(summed[0], 'table', scatter_dimension=0, tiled=True)  107 us
    reduce_scatter x1, waiting for transfers between devices, shards(): lax.psum_scatter(cold_sum, 'dp', scatter_dimension=0, tiled=True)  68.3 us
    psum x1, waiting for transfers between devices, shards(): summed = lax.psum((hot_part, proj_part, bottom_part), 'dp')  62 us
    scatter-add x1, other arithmetic, shards(): cold_sum = jnp.zeros((rows_dev, cold_width), jnp.float32).at[asked.reshap...  51.4 us
    psum x1, blocking collectives, shards(): summed = lax.psum((hot_part, proj_part, bottom_part), 'dp')  28 us
    all_to_all x1, waiting for transfers between devices, shards(): lax.all_to_all(grad_slots, 'table', split_axis=0, concat_axis=0, tiled=True)  26.2 us
  transfers between devices with their start and end apart: 8, of which 8 were waited for; matrix products, arithmetic and copies ran while one was open for 10% of the time, Pallas kernels for 0%

commit v1 on v0

--- a/solution.py
+++ b/solution.py
@@ -7,6 +7,24 @@
 def silu_slope(pre):
     sigma = jax.nn.sigmoid(pre)
     return sigma * (1.0 + pre * (1.0 - sigma))
+
+
+def spread_sum(parts):
+    core = lax.axis_index("dp") % 2
+    pairs = parts.reshape((4, 2) + parts.shape[1:])
+    kept = lax.dynamic_index_in_dim(pairs, core, 1, keepdims=False)
+    given = lax.dynamic_index_in_dim(pairs, 1 - core, 1, keepdims=False)
+    taken = lax.ppermute(given.astype(jnp.bfloat16), "dp", [(i, i ^ 1) for i in range(8)])
+    both = kept + taken.astype(jnp.float32)
+    moved = lax.all_to_all(
+        both.astype(jnp.bfloat16),
+        "dp",
+        split_axis=0,
+        concat_axis=0,
+        tiled=True,
+        axis_index_groups=[[0, 2, 4, 6], [1, 3, 5, 7]],
+    )
+    return jnp.sum(moved.astype(jnp.float32), axis=0)
 
 
 def shards(
@@ -112,19 +130,38 @@
         .at[asked.reshape(-1)]
         .add(returned.reshape(-1, cold_width).astype(jnp.float32))
     )
-    cold_grad = lax.psum_scatter(cold_sum, "dp", scatter_dimension=0, tiled=True)
+    cold_grad = spread_sum(cold_sum.reshape(8, rows_dev // 8, cold_width)).reshape(
+        rows_dev // 8, cold_width
+    )
     d_pre = (d_stack[:, 0].astype(jnp.float32) * silu_slope(pre)).astype(jnp.bfloat16)
     bottom_part = jnp.einsum("bi,bo->io", dense_input, d_pre, preferred_element_type=jnp.float32)
     proj_part = jnp.einsum("qk,qo->ko", pooled, d_cold, preferred_element_type=jnp.float32)
     d_hot = d_stack[:, 1 + cold_feats :].reshape(batch_rows * hot_feats, hidden)
     d_unique = jnp.einsum("qu,qo->uo", counts, d_hot, preferred_element_type=jnp.float32)
     hot_part = jnp.zeros((hot_table.shape[0], hidden), jnp.float32).at[hot_unique].add(d_unique)
-    summed = lax.psum((hot_part, proj_part, bottom_part), "dp")
-    hot_grad, projection_grad, bottom_grad = (
-        lax.psum_scatter(summed[0], "table", scatter_dimension=0, tiled=True),
-        lax.psum_scatter(summed[1], "table", scatter_dimension=0, tiled=True),
-        lax.psum_scatter(summed[2], "table", scatter_dimension=0, tiled=True),
-    )
+    parts = [
+        part.reshape(tables, part.shape[0] // tables, hidden)
+        for part in (hot_part, proj_part, bottom_part)
+    ]
+    sizes = [part.shape[1] for part in parts]
+    joined = jnp.concatenate(parts, axis=1)
+    share = joined.shape[1] // 8
+    split = jnp.swapaxes(joined.reshape(tables, 8, share, hidden), 0, 1)
+    mine = spread_sum(split)
+    across = lax.all_to_all(
+        mine.astype(jnp.bfloat16), "table", split_axis=0, concat_axis=0, tiled=True
+    )
+    total = jnp.sum(across.astype(jnp.float32), axis=0)
+    whole = lax.all_to_all(
+        jnp.broadcast_to(total[None], (8,) + total.shape),
+        "dp",
+        split_axis=0,
+        concat_axis=0,
+        tiled=True,
+    ).reshape(8 * share, hidden)
+    hot_grad = whole[: sizes[0]]
+    projection_grad = whole[sizes[0] : sizes[0] + sizes[1]]
+    bottom_grad = whole[sizes[0] + sizes[1] :]
     return (
         inter.reshape(batch_rows, feats * feats),
         cold_grad,

time: 968 us -> 360 us (0.37)
  waiting for transfers between devices: 710 us -> 50.3 us
  local copies, waits for them, and re-layouts: 96.3 us -> 137 us
  starting transfers between devices: 29.3 us -> 44.3 us
  between operations: 14.3 us -> 1.75 us
  other arithmetic: 68.1 us -> 78.4 us
  blocking collectives: 28 us -> 18.2 us
    reduce_scatter x3 -> x0, waiting for transfers between devices: 390 us -> none  [the longest x1 215 us: shards(): lax.psum_scatter(summed[1], 'table', scatter_dimension=0, tiled=True)]
    unnamed x6 -> x0, waiting for transfers between devices: 214 us -> none
    psum x1 -> x0, waiting for transfers between devices: 62 us -> none  [shards(): summed = lax.psum((hot_part, proj_part, bottom_part), 'dp')]
    psum x1 -> x0, blocking collectives: 28 us -> none  [shards(): summed = lax.psum((hot_part, proj_part, bottom_part), 'dp')]
    all_to_all x0 -> x3, waiting for transfers between devices: none -> 19.1 us  [the longest x1 17.8 us: spread_sum(): lax.all_to_all(both.astype(jnp.bfloat16), 'dp', split_axis=0, concat_axis...]
    all_to_all x0 -> x1, blocking collectives: none -> 18.2 us  [spread_sum(): lax.all_to_all(both.astype(jnp.bfloat16), 'dp', split_axis=0, concat_axis...]
    all_to_all x0 -> x3, starting transfers between devices: none -> 15 us  [the longest x1 7.77 us: shards(): lax.all_to_all(mine.astype(jnp.bfloat16), 'table', split_axis=0, concat_a...]
    dynamic_slice x0 -> x2, local copies, waits for them, and re-layouts: none -> 13.9 us  [spread_sum(): kept = lax.dynamic_index_in_dim(pairs, core, 1, keepdims=False)]
  transfers between devices with their start and end apart: 8 -> 8, of which waited for: 8 -> 5; matrix products, arithmetic and copies ran while one was open for 10% -> 38% of each run, Pallas kernels for 0% -> 0%
where the time goes in v1:
time: 360 us; the launch traced here: 353 us
  local copies, waits for them, and re-layouts  137 us (38%)
  other arithmetic  78.4 us (22%)
  waiting for transfers between devices  50.3 us (14%)
  starting transfers between devices  44.3 us (12%)
  matrix products  23.6 us (7%)
  blocking collectives  18.2 us (5%)
    scatter-add x1, other arithmetic, shards(): cold_sum = jnp.zeros((rows_dev, cold_width), jnp.float32).at[asked.reshap...  52.4 us
    gather x2, local copies, waits for them, and re-layouts, shards(): fetched = cold_table[asked]  25.2 us
    unnamed x50, local copies, waits for them, and re-layouts  24.5 us
    all_to_all x1, blocking collectives, spread_sum(): lax.all_to_all(both.astype(jnp.bfloat16), 'dp', split_axis=0, concat_axis...  18.2 us
    all_to_all x1, waiting for transfers between devices, spread_sum(): lax.all_to_all(both.astype(jnp.bfloat16), 'dp', split_axis=0, concat_axis...  17.8 us
    all_to_all x1, waiting for transfers between devices, shards(): lax.all_to_all(fetched, 'table', split_axis=0, concat_axis=0, tiled=True)  16.3 us
    all_to_all x1, waiting for transfers between devices, shards(): lax.all_to_all(grad_slots, 'table', split_axis=0, concat_axis=0, tiled=True)  14.6 us
    dynamic_slice x2, local copies, waits for them, and re-layouts, spread_sum(): kept = lax.dynamic_index_in_dim(pairs, core, 1, keepdims=False)  13.9 us
  transfers between devices with their start and end apart: 8, of which 5 were waited for; matrix products, arithmetic and copies ran while one was open for 38% of the time, Pallas kernels for 0%

profile of v1, /device:TPU:8, one launch (start us, length us, event | category | flops | bytes accessed | tf_op | source)
XLA Modules:
  0.0 353.1 jit_solution(17802939379561666598)
XLA Ops:
  0.6 0.8 broadcast_multiply_fusion
  1.5 1.0 copy.190
  3.4 9.2 %reduce-window.6 = s32[32,28,128]{2,1,0:T(8,128)S(1)} reduce-window(s32[32,28,128]{2,1,0:T(8,128)S(1)} %fusion.21, s32[]{:T(128)} %constant.32.clone.1), window={size=1x1x128 pad=0_0x0_0x127_0}, to_apply=%region_0.0 | reduce-window | flops 14565376 | bytes 917508 | tf_op jit(solution)/shard_map/reduce-window
  12.7 0.8 slice_reduce_fusion
  14.7 13.7 %scatter_custom_fusion = s32[7168]{0:T(1024)S(1)} fusion(s32[3584]{0:T(1024)S(1)} %fusion.32, s32[3584]{0:T(1024)S(1)} %reshape.238, s32[]{:T(128)} %constant.32.clone.1), kind=kCustom, calls=%fused_computation.70 | custom fusion | bytes 28676 | tf_op jit(solution)/shard_map/scatter | solution.py:68
  28.4 0.7 all_to_all.26
  29.1 11.7 %all-to-all-start = ((s32[32,1,224]{2,1,0:T(1,128)}), s32[32,1,224]{2,1,0:T(1,128)S(1)}, u32[]{:S(2)}, u32[]{:S(2)}) async-start(s32[32,1,224]{2,1,0:T(1,128)} %all_to_all.26), calls=%async_computation | async-start | bytes 65536 | tf_op jit(solution)/shard_map/all_to_all | solution.py:71
  40.8 8.4 %copy.193 = bf16[32768,64]{1,0:T(8,128)(2,1)} copy(bf16[32768,64]{0,1:T(8,128)(2,1)} %param.13) | data formatting | bytes 8388608 | tf_op args[2]
  49.7 23.6 %gather_fusion = bf16[7168,64]{1,0:T(8,128)(2,1)S(1)} fusion(bf16[32768,64]{1,0:T(8,128)(2,1)} %copy.193, s32[7168]{0:T(1024)S(1)} %broadcast_clamp_fusion), kind=kCustom, calls=%fused_computation | custom fusion | bytes 1863680 | tf_op jit(solution)/shard_map/gather | solution.py:72
  73.3 1.6 copy.194
  75.0 10.0 %all-to-all-start.1 = ((bf16[32,224,64]{1,2,0:T(8,128)(2,1)}), bf16[32,224,64]{1,2,0:T(8,128)(2,1)}, u32[]{:S(2)}, u32[]{:S(2)}) async-start(bf16[32,224,64]{1,2,0:T(8,128)(2,1)} %copy.194), calls=%async_computation.1 | async-start | bytes 2097152 | tf_op jit(solution)/shard_map/all_to_all | solution.py:73
  85.5 0.9 copy.199
  87.0 1.0 copy.188
  88.1 1.4 copy.203
  89.5 1.2 gather_fusion.2
  90.7 1.5 convert_reduce_fusion.1
  92.2 1.4 fusion.8
  93.7 0.7 reshape.196
  94.4 16.3 %all-to-all-done.1 = bf16[32,224,64]{1,2,0:T(8,128)(2,1)} async-done(((bf16[32,224,64]{1,2,0:T(8,128)(2,1)}), bf16[32,224,64]{1,2,0:T(8,128)(2,1)}, u32[]{:S(2)}, u32[]{:S(2)}) %all-to-all-start.1) | async-done | bytes 917536 | tf_op jit(solution)/shard_map/all_to_all | solution.py:73
  110.7 1.9 copy.195
  112.6 8.1 %gather_fusion.1 = bf16[3584,64]{1,0:T(8,128)(2,1)} fusion(bf16[7168,64]{1,0:T(8,128)(2,1)S(1)} %bitcast.100, s32[4096]{0:T(1024)S(1)} %pad_clamp_fusion), kind=kCustom, calls=%fused_computation.1 | custom fusion | bytes 931840 | tf_op jit(solution)/shard_map/gather | solution.py:74
  120.6 4.1 %fusion.6 = bf16[896,4,64]{2,1,0:T(4,128)(2,1)S(1)} fusion(bf16[896,4,64]{2,1,0:T(4,128)(2,1)} %bitcast.113, s32[896,4]{1,0:T(8,128)} %copy.188), kind=kOutput, calls=%fused_computation.26 | convolution fusion | flops 2078720 | bytes 931840 | tf_op jit(solution)/shard_map/qln,qlc->qnc/dot_general | solution.py:92
  124.7 1.1 copy.197
  126.3 1.3 reshape.193
  127.6 4.1 %fusion.19 = bf16[128,16,512]{2,1,0:T(8,128)(2,1)S(1)} fusion(f32[128,16,16]{2,1,0:T(8,128)} %copy.203, bf16[128,8,512]{2,1,0:T(8,128)(2,1)} %fusion.8, bf16[128,7,512]{2,1,0:T(8,128)(2,1)} %reshape.193, bf16[128,1,512]{2,1,0:T(2,128)(2,1)S(1)} %copy-done.12), kind=kOutput, calls=%fused_computation.41 | convolution fusion | flops 207618048 | bytes 4325376 | tf_op jit(solution)/shard_map/bfg,bge->bfe/dot_general | solution.py:108
  131.6 1.2 copy.239
  132.8 1.7 fusion.27
  135.1 1.2 reshape.269
  136.3 1.2 reshape.198
  137.6 1.7 fusion.9
  139.7 1.3 copy.206
  141.0 3.8 %fusion.7 = bf16[896,4,64]{2,1,0:T(4,128)(2,1)} fusion(bf16[896,4,64]{2,1,0:T(4,128)(2,1)S(1)} %copy.206, s32[896,4]{1,0:T(8,128)S(1)} %copy-done.11), kind=kOutput, calls=%fused_computation.27 | convolution fusion | flops 2078720 | bytes 931840 | tf_op jit(solution)/shard_map/qln,qnc->qlc/dot_general | solution.py:115
  144.9 10.5 %scatter_custom_fusion.1 = bf16[7168,64]{1,0:T(8,128)(2,1)S(1)} fusion(s32[3584]{0:T(1024)S(1)} %fusion.32, bf16[3584,64]{1,0:T(8,128)(2,1)} %bitcast.118, bf16[]{:T(256)} %constant.61.clone.1), kind=kCustom, calls=%fused_computation.37 | custom fusion | bytes 918016 | tf_op jit(solution)/shard_map/scatter | solution.py:124
  155.4 1.6 copy.208
  157.0 7.4 %all-to-all-start.2 = ((bf16[32,224,64]{1,2,0:T(8,128)(2,1)}), bf16[32,224,64]{1,2,0:T(8,128)(2,1)S(1)}, u32[]{:S(2)}, u32[]{:S(2)}) async-start(bf16[32,224,64]{1,2,0:T(8,128)(2,1)} %copy.208), calls=%async_computation.2 | async-start | bytes 2097152 | tf_op jit(solution)/shard_map/all_to_all | solution.py:127
  164.5 1.3 fusion.39
  165.7 3.1 scatter_custom_fusion.3
  168.8 1.7 pad_maximum_fusion
  170.6 2.1 copy.215
  172.7 1.9 copy-done.2
  174.6 1.1 fusion.14
  175.7 14.6 %all-to-all-done.2 = bf16[32,224,64]{1,2,0:T(8,128)(2,1)S(1)} async-done(((bf16[32,224,64]{1,2,0:T(8,128)(2,1)}), bf16[32,224,64]{1,2,0:T(8,128)(2,1)S(1)}, u32[]{:S(2)}, u32[]{:S(2)}) %all-to-all-start.2) | async-done | bytes 917536 | tf_op jit(solution)/shard_map/all_to_all | solution.py:127
  190.3 2.4 copy.222
  192.8 52.4 %scatter_custom_fusion.2 = f32[32768,64]{1,0:T(8,128)} fusion(s32[7168]{0:T(1024)S(1)} %bitcast.117, f32[7168,64]{1,0:T(8,128)} %bitcast.108, f32[]{:T(128)} %constant.60.clone.1), kind=kCustom, calls=%fused_computation.8 | custom fusion | flops 458752 | bytes 8389120 | tf_op jit(solution)/shard_map/scatter-add | solution.py:131
  245.2 5.8 %dynamic-slice_convert_fusion = bf16[4,1,4096,64]{3,2,1,0:T(8,128)(2,1)} fusion(f32[4,2,4096,64]{3,2,1,0:T(8,128)} %bitcast.98, s32[]{:T(128)S(6)} %select_n.61), kind=kLoop, calls=%fused_computation.7 | loop fusion | bytes 4194308 | tf_op jit(solution)/shard_map/convert_element_type | solution.py:17
  251.1 11.9 %copy.230 = bf16[4,1,4096,64]{2,1,0,3:T(2,128)(2,1)} copy(bf16[4,1,4096,64]{3,2,1,0:T(8,128)(2,1)} %dynamic-slice_convert_fusion) | data formatting | bytes 4194304
  262.9 4.5 %copy.240 = bf16[4,1,4096,64]{2,3,1,0:T(8,128)(2,1)S(1)} copy(bf16[4,1,4096,64]{2,1,0,3:T(2,128)(2,1)} %copy.230) | data formatting | bytes 4194304 | tf_op jit(solution)/shard_map/convert_element_type | solution.py:17
  267.6 2.1 fusion.3
  269.7 18.2 %all_to_all.42 = bf16[4,32,7,512]{3,1,2,0:T(8,128)(2,1)S(1)} all-to-all(bf16[4,32,7,512]{3,1,2,0:T(8,128)(2,1)S(1)} %fusion.3), channel_id=1, replica_groups={{0,2,4,6},{1,3,5,7},{8,10,12,14},{9,11,13,15},{16,18,20,22},{17,19,21,2..., dimensions={0} | all-to-all | bytes 1835008 | tf_op jit(solution)/shard_map/all_to_all | solution.py:19
  288.0 0.9 copy.217
  288.9 7.8 %all-to-all-start.5 = ((bf16[32,7,512]{2,1,0:T(8,128)(2,1)}), bf16[32,7,512]{2,1,0:T(8,128)(2,1)S(1)}, u32[]{:S(2)}, u32[]{:S(2)}) async-start(bf16[32,7,512]{2,1,0:T(8,128)(2,1)} %copy.217), calls=%async_computation.5 | async-start | bytes 524288 | tf_op jit(solution)/shard_map/all_to_all | solution.py:151
  296.7 7.2 %constant_dynamic-slice_fusion = f32[4,1,4096,64]{3,2,1,0:T(8,128)} fusion(f32[4,2,4096,64]{3,2,1,0:T(8,128)} %bitcast.99, s32[]{:T(128)S(6)} %select_n.60), kind=kLoop, calls=%fused_computation.75 | loop fusion | bytes 8388612 | tf_op jit(solution)/shard_map/jit(dynamic_index_in_dim)/dynamic_slice | solution.py:15
  303.8 6.8 %copy.212 = f32[4,1,4096,64]{2,3,1,0:T(8,128)} copy(f32[4,1,4096,64]{3,2,1,0:T(8,128)} %constant_dynamic-slice_fusion) | data formatting | bytes 8388608 | tf_op jit(solution)/shard_map/jit(dynamic_index_in_dim)/dynamic_slice | solution.py:15
  310.7 0.7 broadcast_in_dim.17
  311.3 3.4 all-to-all-start.6
  314.7 4.8 %fusion.2 = bf16[4,4096,64]{1,2,0:T(8,128)(2,1)} fusion(f32[4,1,4096,64]{2,3,1,0:T(8,128)} %copy.212, bf16[4,4096,64]{1,2,0:T(8,128)(2,1)} %collective-permute-done), kind=kLoop, calls=%fused_computation.11 | loop fusion | flops 3145728 | bytes 8388608 | tf_op jit(solution)/shard_map/convert_element_type | solution.py:20
  319.5 1.3 all-to-all-done.6
  320.8 3.9 %all-to-all-start.3 = ((bf16[4,4096,64]{1,2,0:T(8,128)(2,1)}), bf16[4,4096,64]{1,2,0:T(8,128)(2,1)S(1)}, u32[]{:S(2)}, u32[]{:S(2)}) async-start(bf16[4,4096,64]{1,2,0:T(8,128)(2,1)} %fusion.2), calls=%async_computation.3 | async-start | bytes 4194304 | tf_op jit(solution)/shard_map/all_to_all | solution.py:19
  324.7 4.4 %fusion.20 = f32[128,16,16]{2,1,0:T(8,128)} fusion(bf16[128,8,512]{2,1,0:T(8,128)(2,1)S(1)} %copy-done.9, bf16[128,7,512]{2,1,0:T(8,128)(2,1)} %reshape.193, bf16[128,1,512]{2,1,0:T(2,128)(2,1)} %copy.199), kind=kOutput, calls=%fused_computation.42 | convolution fusion | flops 39845888 | bytes 2228224 | tf_op jit(solution)/shard_map/bfe,bge->bfg/dot_general | solution.py:105
  329.1 1.7 copy.200
  330.8 0.8 copy.218
  332.8 0.6 slice.43
  333.5 17.8 %all-to-all-done.3 = bf16[4,4096,64]{1,2,0:T(8,128)(2,1)S(1)} async-done(((bf16[4,4096,64]{1,2,0:T(8,128)(2,1)}), bf16[4,4096,64]{1,2,0:T(8,128)(2,1)S(1)}, u32[]{:S(2)}, u32[]{:S(2)}) %all-to-all-start.3) | async-done | bytes 2097184 | tf_op jit(solution)/shard_map/all_to_all | solution.py:19
  351.3 1.3 convert_reduce_fusion
  (85 shorter events, 7.0 us)
Async XLA Ops:
  0.6 88.9 %copy-start = (bf16[1024,512]{1,0:T(8,128)(2,1)S(1)}, bf16[1024,512]{1,0:T(8,128)(2,1)}, u32[]{:S(2)}) copy-start(bf16[1024,512]{1,0:T(8,128)(2,1)} %param.15) | copy-start | bytes 3145732
  2.8 11.0 %copy-start.17 = (s32[128,7,4]{0,2,1:T(4,128)S(1)}, s32[128,7,4]{0,2,1:T(4,128)}, u32[]{:S(2)}) copy-start(s32[128,7,4]{0,2,1:T(4,128)} %param.17) | copy-start | bytes 43012
  29.1 20.4 %all-to-all-start = ((s32[32,1,224]{2,1,0:T(1,128)}), s32[32,1,224]{2,1,0:T(1,128)S(1)}, u32[]{:S(2)}, u32[]{:S(2)}) async-start(s32[32,1,224]{2,1,0:T(1,128)} %all_to_all.26), calls=%async_computation | async-start | bytes 65536 | tf_op jit(solution)/shard_map/all_to_all | solution.py:71
  73.3 11.7 %copy-start.14 = (f32[128,256]{1,0:T(8,128)S(1)}, f32[128,256]{1,0:T(8,128)}, u32[]{:S(2)}) copy-start(f32[128,256]{1,0:T(8,128)} %param.21) | copy-start | bytes 393220
  73.3 11.8 %copy-start.13 = (bf16[128,512]{1,0:T(8,128)(2,1)S(1)}, bf16[128,512]{1,0:T(8,128)(2,1)}, u32[]{:S(2)}) copy-start(bf16[128,512]{1,0:T(8,128)(2,1)} %param.11) | copy-start | bytes 393220
  74.9 10.2 %copy-start.10 = (bf16[512,512]{1,0:T(8,128)(2,1)S(1)}, bf16[512,512]{1,0:T(8,128)(2,1)}, u32[]{:S(2)}) copy-start(bf16[512,512]{1,0:T(8,128)(2,1)} %param.12) | copy-start | bytes 1572868
  74.9 11.4 %copy-start.18 = (s32[128,7,4]{0,2,1:T(4,128)S(1)}, s32[128,7,4]{0,2,1:T(4,128)}, u32[]{:S(2)}) copy-start(s32[128,7,4]{0,2,1:T(4,128)} %param.18) | copy-start | bytes 43012
  75.0 11.8 %copy-start.16 = (s32[128,8,4]{0,2,1:T(4,128)S(1)}, s32[128,8,4]{0,2,1:T(4,128)}, u32[]{:S(2)}) copy-start(s32[128,8,4]{0,2,1:T(4,128)} %param.20) | copy-start | bytes 49156
  75.0 35.7 %all-to-all-start.1 = ((bf16[32,224,64]{1,2,0:T(8,128)(2,1)}), bf16[32,224,64]{1,2,0:T(8,128)(2,1)}, u32[]{:S(2)}, u32[]{:S(2)}) async-start(bf16[32,224,64]{1,2,0:T(8,128)(2,1)} %copy.194), calls=%async_computation.1 | async-start | bytes 2097152 | tf_op jit(solution)/shard_map/all_to_all | solution.py:73
  85.4 4.1 %copy-start.20 = (s32[256]{0:T(256)S(1)}, s32[256]{0:T(256)}, u32[]{:S(2)}) copy-start(s32[256]{0:T(256)} %param.19) | copy-start | bytes 3076
  89.5 2.7 copy-start.19
  120.6 5.2 %copy-start.8 = (bf16[256,512]{1,0:T(8,128)(2,1)S(1)}, bf16[256,512]{1,0:T(8,128)(2,1)}, u32[]{:S(2)}) copy-start(bf16[256,512]{1,0:T(8,128)(2,1)} %param.14) | copy-start | bytes 786436
  125.8 5.8 %copy-start.4 = (bf16[896,4,64]{0,2,1:T(8,128)(2,1)}, bf16[896,4,64]{0,2,1:T(8,128)(2,1)S(1)}, u32[]{:S(2)}) copy-start(bf16[896,4,64]{0,2,1:T(8,128)(2,1)S(1)} %copy.197) | copy-start | bytes 1376260
  125.8 1.7 copy-start.12
  132.8 1.7 copy-start.3
  135.1 2.5 slice-start
  137.6 1.7 copy-start.6
  139.2 1.8 copy-start.11
  155.4 9.1 %copy-start.5 = (bf16[896,4,64]{0,2,1:T(8,128)(2,1)S(1)}, bf16[896,4,64]{0,2,1:T(8,128)(2,1)}, u32[]{:S(2)}) copy-start(bf16[896,4,64]{0,2,1:T(8,128)(2,1)} %copy-done.4) | copy-start | bytes 1376260
  157.0 7.5 %copy-start.7 = (bf16[896,512,1]{1,0,2:T(8,128)(2,1)S(1)}, bf16[896,512,1]{1,0,2:T(8,128)(2,1)}, u32[]{:S(2)}) copy-start(bf16[896,512,1]{1,0,2:T(8,128)(2,1)} %reshape.269) | copy-start | bytes 2752516
  157.0 33.3 %all-to-all-start.2 = ((bf16[32,224,64]{1,2,0:T(8,128)(2,1)}), bf16[32,224,64]{1,2,0:T(8,128)(2,1)S(1)}, u32[]{:S(2)}, u32[]{:S(2)}) async-start(bf16[32,224,64]{1,2,0:T(8,128)(2,1)} %copy.208), calls=%async_computation.2 | async-start | bytes 2097152 | tf_op jit(solution)/shard_map/all_to_all | solution.py:127
  170.6 5.1 %copy-start.15 = (s32[7168,1]{0,1:T(1,128)S(1)}, s32[7168,1]{0,1:T(1,128)}, u32[]{:S(2)}) copy-start(s32[7168,1]{0,1:T(1,128)} %reshape.196) | copy-start | bytes 86020
  172.7 1.9 copy-start.2
  175.7 91.9 %collective-permute-start.1 = (bf16[4,32,7,512]{3,1,2,0:T(8,128)(2,1)}, bf16[4,32,7,512]{3,1,2,0:T(8,128)(2,1)}, u32[]{:S(2)}, u32[]{:S(2)}) collective-permute-start(bf16[4,32,7,512]{3,1,2,0:T(8,128)(2,1)} %fusion.14), channel_id=1, source_target_pairs={{0,1},{1,0},{2,3},{3,2},{4,5},{5,4},{6,7},{7,6},{8,9},{9,8},{10,11... | collective-permute-start | bytes 2752520 | tf_op jit(solution)/shard_map/ppermute | solution.py:17
  267.5 47.3 %collective-permute-start = (bf16[4,4096,64]{1,2,0:T(8,128)(2,1)S(1)}, bf16[4,4096,64]{1,2,0:T(8,128)(2,1)}, u32[]{:S(2)}, u32[]{:S(2)}) collective-permute-start(bf16[4,4096,64]{1,2,0:T(8,128)(2,1)S(1)} %bitcast.109), channel_id=1, source_target_pairs={{0,1},{1,0},{2,3},{3,2},{4,5},{5,4},{6,7},{7,6},{8,9},{9,8},{10,11... | collective-permute-start | bytes 6291464 | tf_op jit(solution)/shard_map/ppermute | solution.py:17
  288.9 21.7 %all-to-all-start.5 = ((bf16[32,7,512]{2,1,0:T(8,128)(2,1)}), bf16[32,7,512]{2,1,0:T(8,128)(2,1)S(1)}, u32[]{:S(2)}, u32[]{:S(2)}) async-start(bf16[32,7,512]{2,1,0:T(8,128)(2,1)} %copy.217), calls=%async_computation.5 | async-start | bytes 524288 | tf_op jit(solution)/shard_map/all_to_all | solution.py:151
  311.3 9.4 %all-to-all-start.6 = ((f32[8,7,512]{2,1,0:T(8,128)}), f32[8,7,512]{2,1,0:T(8,128)S(1)}, u32[]{:S(2)}, u32[]{:S(2)}) async-start(f32[8,7,512]{2,1,0:T(8,128)} %broadcast_in_dim.17), calls=%async_computation.6 | async-start | bytes 262144 | tf_op jit(solution)/shard_map/all_to_all | solution.py:155
  319.5 5.2 %copy-start.9 = (bf16[128,8,512]{2,1,0:T(8,128)(2,1)S(1)}, bf16[128,8,512]{2,1,0:T(8,128)(2,1)}, u32[]{:S(2)}) copy-start(bf16[128,8,512]{2,1,0:T(8,128)(2,1)} %fusion.8) | copy-start | bytes 3145732
  320.8 30.5 %all-to-all-start.3 = ((bf16[4,4096,64]{1,2,0:T(8,128)(2,1)}), bf16[4,4096,64]{1,2,0:T(8,128)(2,1)S(1)}, u32[]{:S(2)}, u32[]{:S(2)}) async-start(bf16[4,4096,64]{1,2,0:T(8,128)(2,1)} %fusion.2), calls=%async_computation.3 | async-start | bytes 4194304 | tf_op jit(solution)/shard_map/all_to_all | solution.py:19
  329.1 23.4 %copy-start.1 = (bf16[1024,512]{1,0:T(8,128)(2,1)S(1)}, bf16[1024,512]{1,0:T(8,128)(2,1)}, u32[]{:S(2)}) copy-start(bf16[1024,512]{1,0:T(8,128)(2,1)} %param.15) | copy-start | bytes 3145732

commit v2 on v0

v2 whole, which is shorter than its diff:
```python
import functools

import jax
import jax.numpy as jnp
from jax import lax
from jax.experimental import pallas as pl
from jax.experimental.pallas import tpu as pltpu
from jax.sharding import PartitionSpec as P

F32 = jnp.float32
BF16 = jnp.bfloat16
LANES = 128
NT = (((1,), (1,)), ((), ()))
TN = (((0,), (0,)), ((), ()))
MIB = 1 << 20


def dot(a, b, dims=(((1,), (0,)), ((), ()))):
    return lax.dot_general(a, b, dims, preferred_element_type=F32)


def split_two(v):
    high = v.astype(BF16)
    return high, (v - high.astype(F32)).astype(BF16)


def iota(shape, dim):
    return lax.broadcasted_iota(jnp.int32, shape, dim)


def call(kernel, outs, scratch=(), specs=None, vmem=16, us=1, grid=None, out_specs=None):
    args = {} if specs is None else {"in_specs": specs}
    if grid is not None:
        args["grid"] = grid
    if out_specs is not None:
        args["out_specs"] = out_specs
    return pl.pallas_call(
        kernel,
        out_shape=outs,
        scratch_shapes=list(scratch),
        compiler_params=pltpu.CompilerParams(vmem_limit_bytes=vmem * MIB),
        cost_estimate=pl.CostEstimate(
            flops=us * 1_100_000_000, bytes_accessed=MIB, transcendentals=0
        ),
        **args,
    )


SMEM = pl.BlockSpec(memory_space=pltpu.SMEM)
VMEM = pl.BlockSpec(memory_space=pltpu.VMEM)


def prep_kernel(tables, pairs, owner_ref, local_ref, ids_ref, pos_ref):
    steps = owner_ref.shape[0]
    row, col = iota((LANES, 2 * LANES), 0), iota((LANES, 2 * LANES), 1)
    tri = jnp.where((row < col) | (col >= LANES), 1.0, 0.0).astype(BF16)
    table_row = iota((tables, LANES), 0)
    slot_row = iota((2 * LANES, LANES), 0)
    hits = [
        jnp.where(owner_ref[j : j + 1, :] == table_row, 1.0, 0.0) for j in range(steps)
    ]
    sums = dot(jnp.concatenate(hits, axis=0).astype(BF16), tri)
    carry = jnp.zeros((tables, LANES), F32)
    left, right = [], []
    for j in range(steps):
        part = sums[j * tables : (j + 1) * tables]
        slot = jnp.sum(hits[j] * (part[:, :LANES] + carry), axis=0, keepdims=True)
        slot = slot.astype(jnp.int32)
        carry = carry + part[:, LANES:]
        upper = jnp.where(slot >= pairs, 1, 0)
        pos_ref[j : j + 1, :] = (
            upper * (tables * pairs - pairs) + owner_ref[j : j + 1, :] * pairs + slot
        )
        local = local_ref[j : j + 1, :]
        code = (((local >> 11) & 1) << 14) | ((local >> 12) << 11) | (local & 2047)
        high, low = (code >> 8).astype(F32), (code & 255).astype(F32)
        left.append(jnp.concatenate([hits[j] * high, hits[j] * low], axis=0).astype(BF16))
        right.append(jnp.where(slot + upper * (LANES - pairs) == slot_row, 1.0, 0.0).astype(BF16))
    placed = dot(jnp.concatenate(left, axis=1), jnp.concatenate(right, axis=1), NT)
    ids_ref[...] = (placed[:tables] * 256.0 + placed[tables:]).astype(jnp.int32)


def pack_kernel(table_ref, packed_ref):
    half = table_ref.shape[1] // 2
    both = jnp.concatenate([table_ref[:, :half], table_ref[:, half:]], axis=0)
    packed_ref[...] = both.astype(F32).T


def lane_is_low(shape):
    return iota(shape, len(shape) - 1) < 64


def gather_kernel(ids_ref, vec_ref, packed_ref, out_ref, got_a, got_b):
    tables, pairs, _ = out_ref.shape
    step = pairs // 2

    def one(part, source):
        first = source * (2 * LANES) + part * step
        base = pl.multiple_of(source * pairs + part * step, 8)
        read_a = [packed_ref[pl.ds(ids_ref[first + u], 1), :] for u in range(step)]
        read_b = [packed_ref[pl.ds(ids_ref[first + LANES + u], 1), :] for u in range(step)]
        for u in range(step):
            got_a[pl.ds(base + u, 1), :] = read_a[u]
            got_b[pl.ds(base + u, 1), :] = read_b[u]
        return source

    def per_source(source, carry):
        lax.fori_loop(0, 2, one, source)
        return carry

    lax.fori_loop(0, tables, per_source, 0)
    upper = (vec_ref[...] >> 14).astype(F32).T
    low = lane_is_low((pairs, LANES))
    for k in range(tables):
        a = got_a[k * pairs : (k + 1) * pairs, :]
        b = got_b[k * pairs : (k + 1) * pairs, :]
        up_a = upper[:pairs, k : k + 1] > 0.5
        up_b = upper[LANES : LANES + pairs, k : k + 1] > 0.5
        a = jnp.where(up_a, pltpu.roll(a, 64, 1), a)
        b = jnp.where(up_b, b, pltpu.roll(b, 64, 1))
        out_ref[k] = jnp.where(low, a, b).astype(BF16)


def front_kernel(
    dense_ref,
    weight_ref,
    hot_ref,
    unique_ref,
    map_ref,
    grad_ref,
    pre_ref,
    bottom_ref,
    emb_ref,
    counts_ref,
    high_ref,
    low_ref,
):
    batch = dense_ref.shape[0]
    hot_feats, bag = map_ref.shape[0], map_ref.shape[1]
    unique = unique_ref.shape[0]
    feats = high_ref.shape[0]
    pre = dot(dense_ref[...], weight_ref[...])
    pre_ref[...] = pre
    bottom_ref[...] = jax.nn.silu(pre).astype(BF16)
    picks = jnp.where(unique_ref[...] == iota((unique, hot_ref.shape[0]), 1), 1.0, 0.0)
    rows = dot(picks.astype(BF16), hot_ref[...]).astype(BF16)
    place = iota((unique, batch), 0)
    for h in range(hot_feats):
        count = jnp.zeros((unique, batch), F32)
        for l in range(bag):
            count += jnp.where(map_ref[h, l : l + 1, :] == place, 1.0, 0.0)
        counts_ref[:, h * batch : (h + 1) * batch] = count.astype(BF16)
        emb_ref[h] = dot(count.T.astype(BF16), rows).astype(BF16)
    grad = grad_ref[...]
    grad_high, grad_low = split_two(grad)
    square = feats * feats
    at = iota((square, square), 0)
    other = iota((square, square), 1) // feats
    same = iota((batch, square), 0) % feats == iota((batch, square), 1) % feats
    for f in range(feats):
        pick = jnp.where(at == f * feats + other, 1.0, 0.0) + jnp.where(
            at == other * feats + f, 1.0, 0.0
        )
        pick = pick.astype(BF16)
        spread = jnp.where(same, dot(grad_high, pick) + dot(grad_low, pick), 0.0)
        high_ref[f], low_ref[f] = split_two(spread)


def main_kernel(
    pos_ref,
    rows_ref,
    band_ref,
    proj_ref,
    bottom_ref,
    hot_ref,
    high_ref,
    low_ref,
    slots_ref,
    d_ref,
    cold_ref,
    pooled_ref,
    wide,
    lookups,
    stack,
):
    tables, pairs, _ = rows_ref.shape
    feats, batch, hidden = stack.shape
    cold_feats = cold_ref.shape[0]
    bag = band_ref.shape[0] // cold_feats
    half = tables * pairs
    low = lane_is_low((pairs, LANES))
    for k in range(tables):
        x = rows_ref[k].astype(F32)
        r = pltpu.roll(x, 64, 1)
        wide[k * pairs : (k + 1) * pairs, :] = jnp.where(low, x, r)
        wide[half + k * pairs : half + (k + 1) * pairs, :] = jnp.where(low, r, x)

    def fetch(i, carry):
        base = pl.multiple_of(i * 16, 16)
        got = [wide[pl.ds(pos_ref[base + u], 1), :] for u in range(16)]
        for u in range(16):
            lookups[pl.ds(base + u, 1), :] = got[u]
        return carry

    lax.fori_loop(0, lookups.shape[0] // 16, fetch, 0)
    band = band_ref[...].astype(F32).T
    side = jnp.where(lane_is_low((batch, LANES)), 0.0, 1.0)
    stack[0] = bottom_ref[...]
    for h in range(feats - 1 - cold_feats):
        stack[1 + cold_feats + h] = hot_ref[h]
    for f in range(cold_feats):
        first = jnp.zeros((batch, LANES), F32)
        second = jnp.zeros((batch, LANES), F32)
        for l in range(bag):
            j = f * bag + l
            x = lookups[j * batch : (j + 1) * batch, :]
            b = band[:, j : j + 1] - side
            first += jnp.where(b == 0.0, x, 0.0)
            second += jnp.where(b == 2.0, x, 0.0)
        pooled = jnp.concatenate([first, second], axis=1).astype(BF16)
        pooled_ref[f] = pooled
        emb = dot(pooled, proj_ref[...]).astype(BF16)
        cold_ref[f] = emb
        stack[1 + f] = emb
    for g in range(batch // 16):
        at = slice(g * 16, (g + 1) * 16)
        x = stack[:, at, :].reshape(feats * 16, hidden)
        high = high_ref[:, at, :].reshape(feats * 16, feats * 16)
        rest = low_ref[:, at, :].reshape(feats * 16, feats * 16)
        d = (dot(high, x) + dot(rest, x)).astype(BF16)
        d_ref[:, at, :] = d.reshape(feats, 16, hidden)
    low = lane_is_low((batch, LANES))
    for f in range(cold_feats):
        d_pool = dot(d_ref[1 + f], proj_ref[...], NT).astype(BF16).astype(F32)
        first, second = d_pool[:, :LANES], d_pool[:, LANES:]
        first_r, second_r = pltpu.roll(first, 64, 1), pltpu.roll(second, 64, 1)
        each = [
            jnp.where(low, first, first_r),
            jnp.where(low, first_r, first),
            jnp.where(low, second, second_r),
            jnp.where(low, second_r, second),
        ]
        for l in range(bag):
            j = f * bag + l
            b = jnp.broadcast_to(band[:, j : j + 1], (batch, LANES))
            x = jnp.where(b < 0.5, each[0], each[1])
            y = jnp.where(b < 2.5, each[2], each[3])
            lookups[j * batch : (j + 1) * batch, :] = jnp.where(b < 1.5, x, y)
    wide[...] = jnp.zeros(wide.shape, F32)

    def place(i, carry):
        base = pl.multiple_of(i * 16, 16)
        got = [lookups[pl.ds(base + u, 1), :] for u in range(16)]
        for u in range(16):
            wide[pl.ds(pos_ref[base + u], 1), :] = got[u]
        return carry

    lax.fori_loop(0, lookups.shape[0] // 16, place, 0)
    low = lane_is_low((pairs, LANES))
    for k in range(tables):
        a = wide[k * pairs : (k + 1) * pairs, :]
        b = wide[half + k * pairs : half + (k + 1) * pairs, :]
        slots_ref[k] = jnp.where(low, a, b).astype(BF16)


def silu_slope(pre):
    sigma = jax.nn.sigmoid(pre)
    return sigma * (1.0 + pre * (1.0 - sigma))


def back_kernel(
    place_ref,
    d_ref,
    pre_ref,
    dense_ref,
    pooled_ref,
    counts_ref,
    unique_ref,
    kept_ref,
    given_ref,
    parts,
):
    feats, batch, hidden = d_ref.shape
    cold_feats = pooled_ref.shape[0]
    hot_feats = feats - 1 - cold_feats
    tables = parts.shape[2] // 32
    cuts = hidden // LANES
    slope = silu_slope(pre_ref[...])
    d_pre = (d_ref[0].astype(F32) * slope).astype(BF16)
    bottom = dot(dense_ref[...], d_pre, TN)
    d_cold = d_ref[1 : 1 + cold_feats].reshape(cold_feats * batch, hidden)
    pooled = pooled_ref[...].reshape(cold_feats * batch, pooled_ref.shape[2])
    proj = dot(pooled, d_cold, TN)
    d_hot = d_ref[1 + cold_feats :].reshape(hot_feats * batch, hidden)
    high, rest = split_two(dot(counts_ref[...], d_hot))
    hot_rows = tables * 32
    picks = jnp.where(
        iota((hot_rows, unique_ref.shape[1]), 0) == unique_ref[...], 1.0, 0.0
    ).astype(BF16)
    hot = dot(picks, high) + dot(picks, rest)
    for c in range(cuts):
        at = slice(c * LANES, (c + 1) * LANES)
        parts[0, c] = hot[:, at]
        parts[1, c] = jnp.concatenate(
            [
                bottom[:, at].reshape(tables, 16, LANES),
                proj[:, at].reshape(tables, 8, LANES),
                jnp.zeros((tables, 8, LANES), F32),
            ],
            axis=1,
        ).reshape(hot_rows, LANES)
    core = place_ref[1]
    for k in range(cuts):
        chunk = (place_ref[0] + k) % cuts
        kept_ref[k] = parts[core, chunk]
        given_ref[k] = parts[1 - core, chunk].astype(BF16)


def inter_kernel(bottom_ref, cold_ref, hot_ref, inter_ref, stack, grams):
    feats, batch, hidden = stack.shape
    cold_feats = cold_ref.shape[0]
    stack[0] = bottom_ref[...]
    for f in range(cold_feats):
        stack[1 + f] = cold_ref[f]
    for h in range(hot_ref.shape[0]):
        stack[1 + cold_feats + h] = hot_ref[h]
    square = feats * feats
    same = iota((square, square), 0) % feats == iota((square, square), 1) % feats
    for g in range(batch // 16):
        at = slice(g * 16, (g + 1) * 16)
        x = stack[:, at, :].reshape(feats * 16, hidden)
        grams[:, at, :] = jnp.where(same, dot(x, x, NT), 0.0).reshape(feats, 16, square)
    total = jnp.zeros((batch, square), F32)
    other = iota((square, square), 0) // feats
    to = iota((square, square), 1)
    for f in range(feats):
        pick = jnp.where(to == f * feats + other, 1.0, 0.0).astype(BF16)
        high, rest = split_two(grams[f])
        total += dot(high, pick) + dot(rest, pick)
    inter_ref[...] = total


def add_kernel(
    place_ref,
    ids_ref,
    vec_ref,
    rows_ref,
    kept_ref,
    given_ref,
    kept_own_ref,
    given_own_ref,
    val_a,
    val_b,
    *sums,
):
    tables, pairs, _ = rows_ref.shape
    for part in sums:
        part[...] = jnp.zeros(part.shape, F32)
    upper = (vec_ref[...] >> 14).astype(F32).T
    low = lane_is_low((pairs, LANES))
    side = jnp.where(low, 0.0, 1.0)
    for k in range(tables):
        x = rows_ref[k].astype(F32)
        r = pltpu.roll(x, 64, 1)
        at = slice(k * pairs, (k + 1) * pairs)
        up_a, up_b = upper[:pairs, k : k + 1], upper[LANES : LANES + pairs, k : k + 1]
        val_a[at, :] = jnp.where(up_a == side, jnp.where(low, x, r), 0.0)
        val_b[at, :] = jnp.where(up_b == side, jnp.where(low, r, x), 0.0)
    half = tables // 2

    def one(group, source):
        first = source * (2 * LANES) + group * 8
        base = pl.multiple_of(source * pairs + group * 8, 8)
        for u in range(8):
            spots = [
                ids_ref[first + half * which * 2 * LANES + side * LANES + u]
                for which in range(2)
                for side in range(2)
            ]
            new = [
                sums[2 * which + side][pl.ds(spots[2 * which + side], 1), :]
                + val[pl.ds(base + half * which * pairs + u, 1), :]
                for which in range(2)
                for side, val in enumerate((val_a, val_b))
            ]
            for part, spot, value in zip(sums, spots, new):
                part[pl.ds(spot, 1), :] = value
        return source

    def per_source(source, carry):
        lax.fori_loop(0, pairs // 8, one, source)
        return carry

    lax.fori_loop(0, half, per_source, 0)
    core = place_ref[1]
    size = kept_own_ref.shape[0]
    half = size // 2
    for k in range(4):
        chunk = 2 * ((place_ref[0] + k) % 4)
        for h in range(2):
            mine = pl.ds(pl.multiple_of((chunk + core) * size + h * half, half), half)
            other = pl.ds(pl.multiple_of((chunk + 1 - core) * size + h * half, half), half)
            keep = functools.reduce(jnp.add, [part[mine, :] for part in sums])
            give = functools.reduce(jnp.add, [part[other, :] for part in sums]).astype(BF16)
            if k == 0:
                kept_own_ref[h * half : (h + 1) * half, :] = keep
                given_own_ref[h * half : (h + 1) * half, :] = give
            else:
                kept_ref[k - 1, h] = keep.astype(BF16)
                given_ref[k - 1, h] = give


def pair_kernel(kept_ref, taken_ref, up_ref, down_ref, next_up_ref, next_down_ref):
    def total(k, h):
        return (kept_ref[k, h].astype(F32) + taken_ref[k, h].astype(F32)).astype(BF16)

    up_ref[0] = total(1, 0)
    up_ref[1] = total(0, 1)
    down_ref[0] = total(1, 1)
    down_ref[1] = total(2, 0)
    next_up_ref[...] = total(0, 0)
    next_down_ref[...] = total(2, 1)


def last_kernel(kept_ref, taken_ref, low_ref, high_ref, far_low_ref, far_high_ref, out_ref):
    half = low_ref.shape[0]
    total = kept_ref[...] + taken_ref[...].astype(F32)
    low = total[:half] + low_ref[...].astype(F32) + far_low_ref[...].astype(F32)
    high = total[half:] + high_ref[...].astype(F32) + far_high_ref[...].astype(F32)
    wide = jnp.concatenate([low, high], axis=0).T
    out_ref[...] = jnp.concatenate([wide[:64], wide[64:]], axis=1)


def to_other_core(x):
    return lax.ppermute(x, "dp", [(i, i ^ 1) for i in range(8)])


def along_x(x, steps):
    return lax.ppermute(x, "dp", [(i, (i + 2 * steps) % 8) for i in range(8)])


def exchange(x, axis):
    return lax.all_to_all(x, axis, split_axis=0, concat_axis=0, tiled=True)


def shards(
    dense_input,
    bottom_weight,
    cold_table,
    projection,
    hot_table,
    cold_owner,
    cold_local,
    cold_band,
    hot_unique,
    hot_map,
    grad_inter,
):
    batch, hidden = dense_input.shape
    cold_feats, bag = cold_local.shape[1], cold_local.shape[2]
    hot_feats = hot_map.shape[1]
    feats = 1 + cold_feats + hot_feats
    tables = lax.axis_size("table")
    rows_dev, width = cold_table.shape
    unique = hot_unique.shape[0]
    lookups = batch * cold_feats * bag
    slots = 2 * lookups // tables
    pairs = slots // 2
    bands = projection.shape[0]
    at_dp = lax.axis_index("dp").astype(jnp.int32)
    place = jnp.stack([at_dp // 2, at_dp % 2])

    def by_sample(v):
        return jnp.transpose(v.reshape(batch, cold_feats, bag), (1, 2, 0)).reshape(
            cold_feats * bag, batch
        )

    shape = jax.ShapeDtypeStruct
    ids, pos = call(
        functools.partial(prep_kernel, tables, pairs),
        (shape((tables, 2 * LANES), jnp.int32), shape((cold_feats * bag, batch), jnp.int32)),
    )(by_sample(cold_owner), by_sample(cold_local))
    pos = pos.reshape(lookups)
    asked = exchange(ids, "table")
    row_ids = (asked & (rows_dev // 2 - 1)).reshape(tables * 2 * LANES)
    packed = call(
        pack_kernel,
        shape((rows_dev // 2, LANES), F32),
        grid=(8,),
        specs=[pl.BlockSpec((width, rows_dev // 8), lambda i: (0, i))],
        out_specs=pl.BlockSpec((rows_dev // 16, LANES), lambda i: (i, 0)),
        us=6,
    )(cold_table.T)
    fetched = call(
        gather_kernel,
        shape((tables, pairs, LANES), BF16),
        scratch=[pltpu.VMEM((tables * pairs, LANES), F32)] * 2,
        specs=[SMEM, VMEM, VMEM],
        us=16,
    )(row_ids, asked, packed)
    received = exchange(fetched, "table")
    pre, bottom, hot_emb, counts, high, low = call(
        front_kernel,
        (
            shape((batch, hidden), F32),
            shape((batch, hidden), BF16),
            shape((hot_feats, batch, hidden), BF16),
            shape((unique, hot_feats * batch), BF16),
            shape((feats, batch, feats * feats), BF16),
            shape((feats, batch, feats * feats), BF16),
        ),
        us=3,
    )(
        dense_input,
        bottom_weight,
        hot_table,
        hot_unique.reshape(unique, 1),
        jnp.transpose(hot_map, (1, 2, 0)),
        grad_inter,
    )
    slot_grads, d_stack, cold_emb, pooled = call(
        main_kernel,
        (
            shape((tables, pairs, LANES), BF16),
            shape((feats, batch, hidden), BF16),
            shape((cold_feats, batch, hidden), BF16),
            shape((cold_feats, batch, bands), BF16),
        ),
        scratch=[
            pltpu.VMEM((2 * tables * pairs, LANES), F32),
            pltpu.VMEM((lookups, LANES), F32),
            pltpu.VMEM((feats, batch, hidden), BF16),
        ],
        specs=[SMEM] + [VMEM] * 7,
        us=14,
        vmem=20,
    )(pos, received, by_sample(cold_band), projection, bottom, hot_emb, high, low)
    returned = exchange(slot_grads, "table")
    cuts = hidden // LANES
    dense_kept, dense_given = call(
        back_kernel,
        (
            shape((cuts, tables * 32, LANES), F32),
            shape((cuts, tables * 32, LANES), BF16),
        ),
        scratch=[pltpu.VMEM((2, cuts, tables * 32, LANES), F32)],
        specs=[SMEM] + [VMEM] * 6,
        us=4,
        vmem=20,
    )(
        place,
        d_stack,
        pre,
        dense_input,
        pooled,
        counts,
        hot_unique.reshape(1, unique),
    )
    dense_pair = dense_kept + to_other_core(dense_given).astype(F32)
    dense_out = dense_pair[1:].astype(BF16)
    dense_row = dense_pair[0]
    for k, steps in enumerate((1, 2, -1)):
        dense_row += along_x(dense_out[k], steps).astype(F32)
    dense_row = dense_row.astype(BF16).reshape(tables, 32, LANES)
    returned, dense_row = lax.optimization_barrier((returned, dense_row))
    dense_all = exchange(dense_row, "table")

    size = rows_dev // 16
    half = size // 2
    kept, given, kept_own, given_own = call(
        add_kernel,
        (
            shape((3, 2, half, LANES), BF16),
            shape((3, 2, half, LANES), BF16),
            shape((size, LANES), F32),
            shape((size, LANES), BF16),
        ),
        scratch=[pltpu.VMEM((tables * pairs, LANES), F32)] * 2
        + [pltpu.VMEM((rows_dev // 2, LANES), F32)] * 4,
        specs=[SMEM, SMEM, VMEM, VMEM],
        us=20,
        vmem=46,
    )(place, row_ids, asked, returned)
    given, given_own, dense_all = lax.optimization_barrier((given, given_own, dense_all))
    taken = to_other_core(given)
    taken_own = to_other_core(given_own)
    up, down, next_up, next_down = call(
        pair_kernel,
        (
            shape((2, half, LANES), BF16),
            shape((2, half, LANES), BF16),
            shape((half, LANES), BF16),
            shape((half, LANES), BF16),
        ),
        us=2,
    )(kept, taken)
    mine = jnp.sum(dense_all.astype(F32), axis=0)
    (up, down, stack_cold) = lax.optimization_barrier((up, down, cold_emb))
    inter = call(
        inter_kernel,
        shape((batch, feats * feats), F32),
        scratch=[
            pltpu.VMEM((feats, batch, hidden), BF16),
            pltpu.VMEM((feats, batch, feats * feats), F32),
        ],
        us=4,
    )(bottom, stack_cold, hot_emb)
    from_below = along_x(up, 1)
    from_above = along_x(down, -1)
    next_up = (next_up.astype(F32) + from_below[0].astype(F32)).astype(BF16)
    next_down = (next_down.astype(F32) + from_above[0].astype(F32)).astype(BF16)
    far_low = along_x(next_up, 1)
    far_high = along_x(next_down, -1)
    cold_grad = call(last_kernel, shape((width, rows_dev // 8), F32), us=2)(
        kept_own, taken_own, from_above[1], from_below[1], far_low, far_high
    ).T
    theirs = to_other_core(mine)
    both = jnp.where(place[1] == 0, jnp.stack([mine, theirs]), jnp.stack([theirs, mine]))
    ring = jnp.stack([both, along_x(both, -1), along_x(both, 2), along_x(both, 1)])
    whole = jnp.concatenate(
        [lax.dynamic_index_in_dim(ring, (c - place[0]) % cuts, 0, False) for c in range(cuts)],
        axis=2,
    )
    return inter, cold_grad, whole[0], whole[1, 16:24], whole[1, :16]


def solution(mesh):
    placed = (
        P(("table", "dp"), None),
        P(),
        P("table", None),
        P(),
        P(),
        P(("table", "dp"), None, None, None),
        P(("table", "dp"), None, None),
        P(("table", "dp"), None, None),
        P(("table", "dp")),
        P(("table", "dp"), None, None),
        P(("table", "dp"), None),
    )
    return jax.shard_map(
        shards,
        mesh=mesh,
        in_specs=placed,
        out_specs=(
            P(("table", "dp"), None),
            P(("table", "dp"), None),
            P("table", None),
            P("table", None),
            P("table", None),
        ),
        check_vma=False,
    )
```

time: 968 us -> 192 us (0.20)
  waiting for transfers between devices: 710 us -> 52.7 us
  local copies, waits for them, and re-layouts: 96.3 us -> 27.4 us
  other arithmetic: 68.1 us -> 3.92 us
  Pallas kernels: 0 us -> 56 us
  blocking collectives: 28 us -> 0 us
  starting transfers between devices: 29.3 us -> 50.4 us
  matrix products: 20.4 us -> 0 us
  between operations: 14.3 us -> 0.95 us
    reduce_scatter x3 -> x0, waiting for transfers between devices: 390 us -> none  [the longest x1 215 us: shards(): lax.psum_scatter(summed[1], 'table', scatter_dimension=0, tiled=True)]
    unnamed x6 -> x0, waiting for transfers between devices: 214 us -> none
    psum x1 -> x0, waiting for transfers between devices: 62 us -> none  [shards(): summed = lax.psum((hot_part, proj_part, bottom_part), 'dp')]
    pallas_call x0 -> x10, Pallas kernels: none -> 56 us  [the longest x1 19.3 us: shards(): call(add_kernel, (shape((3, 2, half, LANES), BF16), shape((3, 2, half, LA...]
    scatter-add x2 -> x0, other arithmetic: 55.4 us -> none  [the longest x1 51.4 us: shards(): cold_sum = jnp.zeros((rows_dev, cold_width), jnp.float32).at[asked.reshap...]
    gather x4 -> x0, local copies, waits for them, and re-layouts: 34.4 us -> none  [the longest x2 25.2 us: shards(): fetched = cold_table[asked]]
    ppermute x0 -> x14, waiting for transfers between devices: none -> 31.6 us  [the longest x10 28.9 us: along_x(): return lax.ppermute(x, 'dp', [(i, (i + 2 * steps) % 8) for i in range(8)])]
    psum x1 -> x0, blocking collectives: 28 us -> none  [shards(): summed = lax.psum((hot_part, proj_part, bottom_part), 'dp')]
  transfers between devices with their start and end apart: 8 -> 18, of which waited for: 8 -> 13; matrix products, arithmetic and copies ran while one was open for 10% -> 2% of each run, Pallas kernels for 0% -> 14%
where the time goes in v2:
time: 192 us; the launch traced here: 191 us
  Pallas kernels  56 us (29%)
  waiting for transfers between devices  52.7 us (27%)
  starting transfers between devices  50.4 us (26%)
  local copies, waits for them, and re-layouts  27.4 us (14%)
  other arithmetic  3.92 us (2%)
    all_to_all x4, starting transfers between devices, exchange(): return lax.all_to_all(x, axis, split_axis=0, concat_axis=0, tiled=True)  35.1 us
    ppermute x10, waiting for transfers between devices, along_x(): return lax.ppermute(x, 'dp', [(i, (i + 2 * steps) % 8) for i in range(8)])  28.9 us
    unnamed x61, local copies, waits for them, and re-layouts  24.4 us
    all_to_all x4, waiting for transfers between devices, exchange(): return lax.all_to_all(x, axis, split_axis=0, concat_axis=0, tiled=True)  21.2 us
    pallas_call x1, Pallas kernels, shards(): call(add_kernel, (shape((3, 2, half, LANES), BF16), shape((3, 2, half, LA...  19.3 us
    ppermute x10, starting transfers between devices, along_x(): return lax.ppermute(x, 'dp', [(i, (i + 2 * steps) % 8) for i in range(8)])  14.5 us
    pallas_call x1, Pallas kernels, shards(): call(main_kernel, (shape((tables, pairs, LANES), BF16), shape((feats, bat...  13.1 us
    pallas_call x1, Pallas kernels, shards(): call(gather_kernel, shape((tables, pairs, LANES), BF16), scratch=[pltpu.V...  9.83 us
  transfers between devices with their start and end apart: 18, of which 13 were waited for; matrix products, arithmetic and copies ran while one was open for 2% of the time, Pallas kernels for 14%

profile of v2, /device:TPU:8, one launch (start us, length us, event | category | flops | bytes accessed | tf_op | source)
XLA Modules:
  0.0 191.5 jit_solution(13517857149989771780)
XLA Ops:
  0.6 0.7 reshape.105.owner_ref
  1.4 0.7 reshape.106.local_ref
  2.1 1.0 shard_map.147
  3.1 0.6 copy.18
  3.8 11.7 %all-to-all-start = ((s32[32,1,256]{2,1,0:T(1,128)}), s32[32,1,256]{2,1,0:T(1,128)S(1)}, u32[]{:S(2)}, u32[]{:S(2)}) async-start(s32[32,1,256]{2,1,0:T(1,128)} %copy.18), calls=%async_computation | async-start | bytes 65536 | tf_op jit(solution)/shard_map/all_to_all | solution.py:443
  15.5 2.2 %copy-done.1 = bf16[32768,64]{0,1:T(8,128)(2,1)S(1)} copy-done((bf16[32768,64]{0,1:T(8,128)(2,1)S(1)}, bf16[32768,64]{0,1:T(8,128)(2,1)}, u32[]{:S(2)}) %copy-start.1) | copy-done | bytes 4194328
  17.7 2.0 %shard_map.148.packed_ref = f32[16384,128]{1,0:T(8,128)S(1)} custom-call(bf16[64,32768]{1,0:T(8,128)(2,1)S(1)} %bitcast.77), custom_call_target="tpu_custom_call" | custom-call | flops 6600000000 | bytes 1048576 | tf_op jit(solution)/shard_map/pallas_call | solution.py:486
  19.7 3.3 %copy-done.11 = f32[16384,128]{1,0:T(8,128)} copy-done((f32[16384,128]{1,0:T(8,128)}, f32[16384,128]{1,0:T(8,128)S(1)}, u32[]{:S(2)}) %copy-start.11) | copy-done | bytes 8388632
  23.0 1.1 all-to-all-done
  24.2 3.4 %copy-done.12 = f32[16384,128]{1,0:T(8,128)S(1)} copy-done((f32[16384,128]{1,0:T(8,128)S(1)}, f32[16384,128]{1,0:T(8,128)}, u32[]{:S(2)}) %copy-start.12) | copy-done | bytes 8388632
  27.6 9.8 %shard_map.149 = bf16[32,112,128]{2,1,0:T(8,128)(2,1)} custom-call(s32[8192]{0:T(1024)S(1)} %bitcast.72, s32[32,256]{1,0:T(8,128)S(1)} %bitcast.70, f32[16384,128]{1,0:T(8,128)S(1)} %copy-done.12), custom_call_target="tpu_custom_call" | custom-call | flops 17600000000 | bytes 1048576 | tf_op jit(solution)/shard_map/pallas_call | solution.py:494
  37.4 8.6 %all-to-all-start.1 = ((bf16[32,112,128]{2,1,0:T(8,128)(2,1)}), bf16[32,112,128]{2,1,0:T(8,128)(2,1)S(1)}, u32[]{:S(2)}, u32[]{:S(2)}) async-start(bf16[32,112,128]{2,1,0:T(8,128)(2,1)} %shard_map.149), calls=%async_computation.1 | async-start | bytes 1835008 | tf_op jit(solution)/shard_map/all_to_all | solution.py:443
  46.1 0.1 copy.17.unique_ref
  46.4 1.2 copy-done.2
  47.6 2.6 %shard_map.146 = (f32[128,512]{1,0:T(8,128)S(1)}, bf16[128,512]{1,0:T(8,128)(2,1)S(1)}, bf16[8,128,512]{2,1,0:T(8,128)(2,1)S(1)}, bf16[256,1024]{1,0:T(8,128)(2,...) custom-call(bf16[128,512]{1,0:T(8,128)(2,1)S(1)} %copy-done.7, ...), custom_call_target="tpu_custom_call" | custom-call | flops 3300000000 | bytes 1048576 | tf_op jit(solution)/shard_map/pallas_call | solution.py:502
  50.2 1.0 copy-done.15
  51.2 1.0 copy-done.18
  52.2 1.0 copy-done.20
  53.2 0.8 copy-done.22
  54.0 0.7 copy-done.26
  54.7 14.5 %all-to-all-done.1.rows_ref = bf16[32,112,128]{2,1,0:T(8,128)(2,1)S(1)} async-done(((bf16[32,112,128]{2,1,0:T(8,128)(2,1)}), bf16[32,112,128]{2,1,0:T(8,128)(2,1)S(1)}, u32[]{:S(2)}, u32[]{:S(2)}) %all-to-all-start.1) | async-done | bytes 917536 | tf_op jit(solution)/shard_map/all_to_all | solution.py:443
  69.2 1.2 copy-done.16
  70.4 1.2 copy-done.19
  71.7 1.2 copy-done.21
  72.9 0.9 copy-done.27
  73.8 13.1 %shard_map.150 = (bf16[32,112,128]{2,1,0:T(8,128)(2,1)}, bf16[16,128,512]{2,1,0:T(8,128)(2,1)S(1)}, bf16[7,128,512]{2,1,0:T(8,128)(2,1)S(1)}, bf16[7,128,256]{2,1,0:T(8,128)(2,1)S(1)}) custom-call(s32[3584]{0:T(1024)S(1)} %bitcast.79, bf16[32,112,128]{2,1,0:T(8,128)(2,1)S(1)} %all-to-all-done.1.rows_ref, s32[28,128]{1,0:T(8,128)S(1)} %reshape.108.band_ref, ...), custom_call_target="tpu_custom_call" | custom-call | flops 15399999488 | bytes 1048576 | tf_op jit(solution)/shard_map/pallas_call | solution.py:521
  86.9 0.9 copy-done.24
  87.8 3.5 %shard_map.151 = (f32[4,1024,128]{2,1,0:T(8,128)S(1)}, bf16[4,1024,128]{2,1,0:T(8,128)(2,1)}) custom-call(s32[2]{0:T(128)S(1)} %pad_add_fusion.place_ref, bf16[16,128,512]{2,1,0:T(8,128)(2,1)S(1)} %get-tuple-element.42.d_ref, f32[128,512]{1,0:T(8,128)S(1)} %get-tuple-element.43.pre_ref, bf16[128,512]{1,0:T(8,128)(2,1)S(1)} %copy-done.7, ...), custom_call_target="tpu_custom_call" | custom-call | flops 4400000000 | bytes 1048576 | tf_op jit(solution)/shard_map/pallas_call | solution.py:540
  91.3 7.2 %all-to-all-start.2 = ((bf16[32,112,128]{2,1,0:T(8,128)(2,1)}), bf16[32,112,128]{2,1,0:T(8,128)(2,1)S(1)}, u32[]{:S(2)}, u32[]{:S(2)}) async-start(bf16[32,112,128]{2,1,0:T(8,128)(2,1)} %get-tuple-element.41), calls=%async_computation.2 | async-start | bytes 1835008 | tf_op jit(solution)/shard_map/all_to_all | solution.py:443
  98.5 1.5 fusion.6
  100.1 1.6 collective-permute-start.1
  101.6 2.7 %collective-permute-start.2 = (bf16[1024,128]{1,0:T(8,128)(2,1)S(1)}, bf16[1024,128]{1,0:T(8,128)(2,1)S(1)}, u32[]{:S(2)}, u32[]{:S(2)}) collective-permute-start(bf16[1024,128]{1,0:T(8,128)(2,1)S(1)} %get-tuple-element.69), channel_id=1, source_target_pairs={{0,4},{1,5},{2,6},{3,7},{4,0},{5,1},{6,2},{7,3},{8,12},{9,13},{10,... | collective-permute-start | bytes 786440 | tf_op jit(solution)/shard_map/ppermute | solution.py:439
  104.4 1.4 collective-permute-start.3
  105.8 3.7 %collective-permute-done.1 = bf16[1024,128]{1,0:T(8,128)(2,1)S(1)} collective-permute-done((bf16[1024,128]{1,0:T(8,128)(2,1)S(1)}, bf16[1024,128]{1,0:T(8,128)(2,1)S(1)}, u32[]{:S(2)}, u32[]{:S(2)}) %collective-permute-start.1) | collective-permute-done | bytes 262176 | tf_op jit(solution)/shard_map/ppermute | solution.py:439
  109.5 6.6 %collective-permute-done.2 = bf16[1024,128]{1,0:T(8,128)(2,1)S(1)} collective-permute-done((bf16[1024,128]{1,0:T(8,128)(2,1)S(1)}, bf16[1024,128]{1,0:T(8,128)(2,1)S(1)}, u32[]{:S(2)}, u32[]{:S(2)}) %collective-permute-start.2) | collective-permute-done | bytes 262176 | tf_op jit(solution)/shard_map/ppermute | solution.py:439
  116.1 0.9 fusion.3
  117.0 5.5 %all-to-all-done.2.rows_ref = bf16[32,112,128]{2,1,0:T(8,128)(2,1)S(1)} async-done(((bf16[32,112,128]{2,1,0:T(8,128)(2,1)}), bf16[32,112,128]{2,1,0:T(8,128)(2,1)S(1)}, u32[]{:S(2)}, u32[]{:S(2)}) %all-to-all-start.2) | async-done | bytes 917536 | tf_op jit(solution)/shard_map/all_to_all | solution.py:443
  122.5 7.6 %all-to-all-start.3 = ((bf16[32,32,128]{2,1,0:T(8,128)(2,1)}), bf16[32,32,128]{2,1,0:T(8,128)(2,1)S(1)}, u32[]{:S(2)}, u32[]{:S(2)}) async-start(bf16[32,32,128]{2,1,0:T(8,128)(2,1)} %bitcast.17), calls=%async_computation.3 | async-start | bytes 524288 | tf_op jit(solution)/shard_map/all_to_all | solution.py:443
  130.1 19.3 %shard_map.152 = (bf16[3,2,1024,128]{3,2,1,0:T(8,128)(2,1)S(1)}, bf16[3,2,1024,128]{3,2,1,0:T(8,128)(2,1)S(1)}, f32[2048,128]{1,0:T(8,128)S(1)}, bf16[2048,128]{1,0:T(8,128)(2,1)S(1)}) custom-call(s32[2]{0:T(128)S(1)} %pad_add_fusion.place_ref, s32[8192]{0:T(1024)S(1)} %bitcast.73, s32[32,256]{1,0:T(8,128)S(1)} %bitcast.71, ...), custom_call_target="tpu_custom_call" | custom-call | flops 22000001024 | bytes 1048576 | tf_op jit(solution)/shard_map/pallas_call | solution.py:570
  149.4 1.2 copy-done.9
  150.5 1.0 copy-done.13
  151.5 0.8 copy-done.4
  152.4 0.6 collective-permute-start.10
  153.0 0.2 collective-permute-start.5
  153.2 2.6 %collective-permute-done.10 = f32[32,128]{1,0:T(8,128)S(1)} collective-permute-done((f32[32,128]{1,0:T(8,128)S(1)}, f32[32,128]{1,0:T(8,128)S(1)}, u32[]{:S(2)}, u32[]{:S(2)}) %collective-permute-start.10) | collective-permute-done | bytes 16416 | tf_op jit(solution)/shard_map/ppermute | solution.py:435
  155.8 2.8 %collective-permute-start.11 = (f32[2,32,128]{2,1,0:T(8,128)S(1)}, f32[2,32,128]{2,1,0:T(8,128)S(1)}, u32[]{:S(2)}, u32[]{:S(2)}) collective-permute-start(f32[2,32,128]{2,1,0:T(8,128)S(1)} %maximum_select_fusion.1), channel_id=1, source_target_pairs={{0,6},{1,7},{2,0},{3,1},{4,2},{5,3},{6,4},{7,5},{8,14},{9,15},{10,... | collective-permute-start | bytes 98312 | tf_op jit(solution)/shard_map/ppermute | solution.py:439
  158.6 0.8 collective-permute-start.12
  159.4 0.9 collective-permute-start.13
  160.4 3.6 %collective-permute-done.12 = f32[2,32,128]{2,1,0:T(8,128)S(1)} collective-permute-done((f32[2,32,128]{2,1,0:T(8,128)S(1)}, f32[2,32,128]{2,1,0:T(8,128)S(1)}, u32[]{:S(2)}, u32[]{:S(2)}) %collective-permute-start.12) | collective-permute-done | bytes 32800 | tf_op jit(solution)/shard_map/ppermute | solution.py:439
  164.0 0.5 collective-permute-done.13
  164.5 0.6 maximum_bitcast_fusion
  165.2 0.6 slice_bitcast_fusion.8
  165.8 1.4 copy-done.10
  167.2 0.4 shard_map.153
  167.6 0.5 collective-permute-start.6
  168.1 0.6 maximum_bitcast_fusion.1
  168.7 1.6 collective-permute-start.7
  170.3 3.0 %shard_map.154 = f32[128,256]{1,0:T(8,128)} custom-call(bf16[128,512]{1,0:T(8,128)(2,1)S(1)} %copy-done.28, bf16[7,128,512]{2,1,0:T(8,128)(2,1)S(1)} %copy-done.25, bf16[8,128,512]{2,1,0:T(8,128)(2,1)S(1)} %copy-done.17), custom_call_target="tpu_custom_call" | custom-call | flops 4400000000 | bytes 1048576 | tf_op jit(solution)/shard_map/pallas_call | solution.py:599
  173.3 6.7 %collective-permute-done.6 = bf16[2,1024,128]{2,1,0:T(8,128)(2,1)S(1)} collective-permute-done((bf16[2,1024,128]{2,1,0:T(8,128)(2,1)S(1)}, bf16[2,1024,128]{2,1,0:T(8,128)(2,1)S(1)}, u32[]{:S(2)}, u32[]{:S(2)}) %collective-permute-start.6) | collective-permute-done | bytes 524320 | tf_op jit(solution)/shard_map/ppermute | solution.py:439
  180.1 2.1 %collective-permute-start.9 = (bf16[1024,128]{1,0:T(8,128)(2,1)S(1)}, bf16[1024,128]{1,0:T(8,128)(2,1)S(1)}, u32[]{:S(2)}, u32[]{:S(2)}) collective-permute-start(bf16[1024,128]{1,0:T(8,128)(2,1)S(1)} %fusion.4), channel_id=1, source_target_pairs={{0,6},{1,7},{2,0},{3,1},{4,2},{5,3},{6,4},{7,5},{8,14},{9,15},{10,... | collective-permute-start | bytes 786440 | tf_op jit(solution)/shard_map/ppermute | solution.py:439
  182.3 0.2 collective-permute-done.7
  182.7 3.9 %collective-permute-done.9.far_high_ref = bf16[1024,128]{1,0:T(8,128)(2,1)S(1)} collective-permute-done((bf16[1024,128]{1,0:T(8,128)(2,1)S(1)}, bf16[1024,128]{1,0:T(8,128)(2,1)S(1)}, u32[]{:S(2)}, u32[]{:S(2)}) %collective-permute-start.9) | collective-permute-done | bytes 262176 | tf_op jit(solution)/shard_map/ppermute | solution.py:439
  186.6 3.6 %collective-permute-done.8.far_low_ref = bf16[1024,128]{1,0:T(8,128)(2,1)S(1)} collective-permute-done((bf16[1024,128]{1,0:T(8,128)(2,1)S(1)}, bf16[1024,128]{1,0:T(8,128)(2,1)S(1)}, u32[]{:S(2)}, u32[]{:S(2)}) %collective-permute-start.8) | collective-permute-done | bytes 262176 | tf_op jit(solution)/shard_map/ppermute | solution.py:439
  190.2 1.3 shard_map.155
  (66 shorter events, 0.8 us)
Async XLA Ops:
  3.8 20.4 %all-to-all-start = ((s32[32,1,256]{2,1,0:T(1,128)}), s32[32,1,256]{2,1,0:T(1,128)S(1)}, u32[]{:S(2)}, u32[]{:S(2)}) async-start(s32[32,1,256]{2,1,0:T(1,128)} %copy.18), calls=%async_computation | async-start | bytes 65536 | tf_op jit(solution)/shard_map/all_to_all | solution.py:443
  15.5 2.2 %copy-start.1 = (bf16[32768,64]{0,1:T(8,128)(2,1)S(1)}, bf16[32768,64]{0,1:T(8,128)(2,1)}, u32[]{:S(2)}) copy-start(bf16[32768,64]{0,1:T(8,128)(2,1)} %param.13) | copy-start | bytes 12582916
  19.7 3.3 %copy-start.11 = (f32[16384,128]{1,0:T(8,128)}, f32[16384,128]{1,0:T(8,128)S(1)}, u32[]{:S(2)}) copy-start(f32[16384,128]{1,0:T(8,128)S(1)} %shard_map.148.packed_ref) | copy-start | bytes 25165828
  24.2 3.4 %copy-start.12 = (f32[16384,128]{1,0:T(8,128)S(1)}, f32[16384,128]{1,0:T(8,128)}, u32[]{:S(2)}) copy-start(f32[16384,128]{1,0:T(8,128)} %copy-done.11) | copy-start | bytes 25165828
  27.6 18.5 %copy-start = (s32[256]{0:T(256)S(1)}, s32[256]{0:T(256)}, u32[]{:S(2)}) copy-start(s32[256]{0:T(256)} %param.19) | copy-start | bytes 3076
  27.6 18.7 %copy-start.29 = (s32[128,7,4]{0,2,1:T(4,128)S(1)}, s32[128,7,4]{0,2,1:T(4,128)}, u32[]{:S(2)}) copy-start(s32[128,7,4]{0,2,1:T(4,128)} %param.18) | copy-start | bytes 43012
  27.6 18.8 %copy-start.3 = (bf16[512,512]{1,0:T(8,128)(2,1)S(1)}, bf16[512,512]{1,0:T(8,128)(2,1)}, u32[]{:S(2)}) copy-start(bf16[512,512]{1,0:T(8,128)(2,1)} %weight_ref.1) | copy-start | bytes 1572868
  27.6 18.8 %copy-start.6 = (f32[128,256]{1,0:T(8,128)S(1)}, f32[128,256]{1,0:T(8,128)}, u32[]{:S(2)}) copy-start(f32[128,256]{1,0:T(8,128)} %grad_ref.1) | copy-start | bytes 393220
  27.6 18.8 %copy-start.7 = (bf16[128,512]{1,0:T(8,128)(2,1)S(1)}, bf16[128,512]{1,0:T(8,128)(2,1)}, u32[]{:S(2)}) copy-start(bf16[128,512]{1,0:T(8,128)(2,1)} %dense_ref.3) | copy-start | bytes 393220
  27.6 18.8 %copy-start.8 = (s32[128,8,4]{0,2,1:T(4,128)S(1)}, s32[128,8,4]{0,2,1:T(4,128)}, u32[]{:S(2)}) copy-start(s32[128,8,4]{0,2,1:T(4,128)} %param.20) | copy-start | bytes 49156
  37.4 31.8 %all-to-all-start.1 = ((bf16[32,112,128]{2,1,0:T(8,128)(2,1)}), bf16[32,112,128]{2,1,0:T(8,128)(2,1)S(1)}, u32[]{:S(2)}, u32[]{:S(2)}) async-start(bf16[32,112,128]{2,1,0:T(8,128)(2,1)} %shard_map.149), calls=%async_computation.1 | async-start | bytes 1835008 | tf_op jit(solution)/shard_map/all_to_all | solution.py:443
  46.4 1.2 copy-start.2
  47.6 21.6 %copy-start.5 = (bf16[256,512]{1,0:T(8,128)(2,1)S(1)}, bf16[256,512]{1,0:T(8,128)(2,1)}, u32[]{:S(2)}) copy-start(bf16[256,512]{1,0:T(8,128)(2,1)} %proj_ref.1) | copy-start | bytes 786436
  50.2 1.0 copy-start.15
  51.2 1.0 copy-start.18
  52.2 1.0 copy-start.20
  53.2 0.8 copy-start.22
  54.0 0.7 copy-start.26
  69.2 1.2 copy-start.16
  70.4 1.2 copy-start.19
  71.6 1.2 copy-start.21
  72.9 0.9 copy-start.27
  73.8 14.0 %copy-start.23 = (bf16[256,1024]{1,0:T(8,128)(2,1)S(1)}, bf16[256,1024]{1,0:T(8,128)(2,1)}, u32[]{:S(2)}) copy-start(bf16[256,1024]{1,0:T(8,128)(2,1)} %copy-done.22) | copy-start | bytes 1572868
  86.9 0.9 copy-start.24
  91.3 7.2 %collective-permute-start = (bf16[4,1024,128]{2,1,0:T(8,128)(2,1)}, bf16[4,1024,128]{2,1,0:T(8,128)(2,1)}, u32[]{:S(2)}, u32[]{:S(2)}) collective-permute-start(bf16[4,1024,128]{2,1,0:T(8,128)(2,1)} %get-tuple-element.47), channel_id=1, source_target_pairs={{0,1},{1,0},{2,3},{3,2},{4,5},{5,4},{6,7},{7,6},{8,9},{9,8},{10,11... | collective-permute-start | bytes 3145736 | tf_op jit(solution)/shard_map/ppermute | solution.py:435
  91.3 31.2 %all-to-all-start.2 = ((bf16[32,112,128]{2,1,0:T(8,128)(2,1)}), bf16[32,112,128]{2,1,0:T(8,128)(2,1)S(1)}, u32[]{:S(2)}, u32[]{:S(2)}) async-start(bf16[32,112,128]{2,1,0:T(8,128)(2,1)} %get-tuple-element.41), calls=%async_computation.2 | async-start | bytes 1835008 | tf_op jit(solution)/shard_map/all_to_all | solution.py:443
  100.1 9.5 %collective-permute-start.1 = (bf16[1024,128]{1,0:T(8,128)(2,1)S(1)}, bf16[1024,128]{1,0:T(8,128)(2,1)S(1)}, u32[]{:S(2)}, u32[]{:S(2)}) collective-permute-start(bf16[1024,128]{1,0:T(8,128)(2,1)S(1)} %get-tuple-element.67), channel_id=1, source_target_pairs={{0,2},{1,3},{2,4},{3,5},{4,6},{5,7},{6,0},{7,1},{8,10},{9,11},{10,... | collective-permute-start | bytes 786440 | tf_op jit(solution)/shard_map/ppermute | solution.py:439
  101.6 14.5 %collective-permute-start.2 = (bf16[1024,128]{1,0:T(8,128)(2,1)S(1)}, bf16[1024,128]{1,0:T(8,128)(2,1)S(1)}, u32[]{:S(2)}, u32[]{:S(2)}) collective-permute-start(bf16[1024,128]{1,0:T(8,128)(2,1)S(1)} %get-tuple-element.69), channel_id=1, source_target_pairs={{0,4},{1,5},{2,6},{3,7},{4,0},{5,1},{6,2},{7,3},{8,12},{9,13},{10,... | collective-permute-start | bytes 786440 | tf_op jit(solution)/shard_map/ppermute | solution.py:439
  104.4 11.8 %collective-permute-start.3 = (bf16[1024,128]{1,0:T(8,128)(2,1)S(1)}, bf16[1024,128]{1,0:T(8,128)(2,1)S(1)}, u32[]{:S(2)}, u32[]{:S(2)}) collective-permute-start(bf16[1024,128]{1,0:T(8,128)(2,1)S(1)} %get-tuple-element.68), channel_id=1, source_target_pairs={{0,6},{1,7},{2,0},{3,1},{4,2},{5,3},{6,4},{7,5},{8,14},{9,15},{10,... | collective-permute-start | bytes 786440 | tf_op jit(solution)/shard_map/ppermute | solution.py:439
  122.5 29.0 %all-to-all-start.3 = ((bf16[32,32,128]{2,1,0:T(8,128)(2,1)}), bf16[32,32,128]{2,1,0:T(8,128)(2,1)S(1)}, u32[]{:S(2)}, u32[]{:S(2)}) async-start(bf16[32,32,128]{2,1,0:T(8,128)(2,1)} %bitcast.17), calls=%async_computation.3 | async-start | bytes 524288 | tf_op jit(solution)/shard_map/all_to_all | solution.py:443
  149.4 1.2 copy-start.9
  150.5 1.0 copy-start.13
  151.5 0.8 copy-start.4
  152.3 13.5 %collective-permute-start.4 = (bf16[3,2,1024,128]{3,2,1,0:T(8,128)(2,1)S(1)}, bf16[3,2,1024,128]{3,2,1,0:T(8,128)(2,1)S(1)}, u32[]{:S(2)}, u32[]{:S(2)}) collective-permute-start(bf16[3,2,1024,128]{3,2,1,0:T(8,128)(2,1)S(1)} %get-tuple-element.53), channel_id=1, source_target_pairs={{0,1},{1,0},{2,3},{3,2},{4,5},{5,4},{6,7},{7,6},{8,9},{9,8},{10,11... | collective-permute-start | bytes 4718600 | tf_op jit(solution)/shard_map/ppermute | solution.py:435
  152.4 3.4 %collective-permute-start.10 = (f32[32,128]{1,0:T(8,128)S(1)}, f32[32,128]{1,0:T(8,128)S(1)}, u32[]{:S(2)}, u32[]{:S(2)}) collective-permute-start(f32[32,128]{1,0:T(8,128)S(1)} %convert_reduce_fusion), channel_id=1, source_target_pairs={{0,1},{1,0},{2,3},{3,2},{4,5},{5,4},{6,7},{7,6},{8,9},{9,8},{10,11... | collective-permute-start | bytes 49160 | tf_op jit(solution)/shard_map/ppermute | solution.py:435
  153.0 29.7 %collective-permute-start.5 = (bf16[2048,128]{1,0:T(8,128)(2,1)}, bf16[2048,128]{1,0:T(8,128)(2,1)S(1)}, u32[]{:S(2)}, u32[]{:S(2)}) collective-permute-start(bf16[2048,128]{1,0:T(8,128)(2,1)} %copy-done.4), channel_id=1, source_target_pairs={{0,1},{1,0},{2,3},{3,2},{4,5},{5,4},{6,7},{7,6},{8,9},{9,8},{10,11... | collective-permute-start | bytes 1572872 | tf_op jit(solution)/shard_map/ppermute | solution.py:435
  155.8 4.6 %collective-permute-start.11 = (f32[2,32,128]{2,1,0:T(8,128)S(1)}, f32[2,32,128]{2,1,0:T(8,128)S(1)}, u32[]{:S(2)}, u32[]{:S(2)}) collective-permute-start(f32[2,32,128]{2,1,0:T(8,128)S(1)} %maximum_select_fusion.1), channel_id=1, source_target_pairs={{0,6},{1,7},{2,0},{3,1},{4,2},{5,3},{6,4},{7,5},{8,14},{9,15},{10,... | collective-permute-start | bytes 98312 | tf_op jit(solution)/shard_map/ppermute | solution.py:439
  158.6 5.4 %collective-permute-start.12 = (f32[2,32,128]{2,1,0:T(8,128)S(1)}, f32[2,32,128]{2,1,0:T(8,128)S(1)}, u32[]{:S(2)}, u32[]{:S(2)}) collective-permute-start(f32[2,32,128]{2,1,0:T(8,128)S(1)} %maximum_select_fusion.1), channel_id=1, source_target_pairs={{0,4},{1,5},{2,6},{3,7},{4,0},{5,1},{6,2},{7,3},{8,12},{9,13},{10,... | collective-permute-start | bytes 98312 | tf_op jit(solution)/shard_map/ppermute | solution.py:439
  159.4 5.1 %collective-permute-start.13 = (f32[2,32,128]{2,1,0:T(8,128)S(1)}, f32[2,32,128]{2,1,0:T(8,128)S(1)}, u32[]{:S(2)}, u32[]{:S(2)}) collective-permute-start(f32[2,32,128]{2,1,0:T(8,128)S(1)} %maximum_select_fusion.1), channel_id=1, source_target_pairs={{0,2},{1,3},{2,4},{3,5},{4,6},{5,7},{6,0},{7,1},{8,10},{9,11},{10,... | collective-permute-start | bytes 98312 | tf_op jit(solution)/shard_map/ppermute | solution.py:439
  165.8 1.4 copy-start.10
  167.2 3.1 %copy-start.17 = (bf16[8,128,512]{2,1,0:T(8,128)(2,1)S(1)}, bf16[8,128,512]{2,1,0:T(8,128)(2,1)}, u32[]{:S(2)}) copy-start(bf16[8,128,512]{2,1,0:T(8,128)(2,1)} %copy-done.15) | copy-start | bytes 3145732
  167.2 3.1 %copy-start.25 = (bf16[7,128,512]{2,1,0:T(8,128)(2,1)S(1)}, bf16[7,128,512]{2,1,0:T(8,128)(2,1)}, u32[]{:S(2)}) copy-start(bf16[7,128,512]{2,1,0:T(8,128)(2,1)} %copy-done.24) | copy-start | bytes 2752516
  167.2 3.1 %copy-start.28 = (bf16[128,512]{1,0:T(8,128)(2,1)S(1)}, bf16[128,512]{1,0:T(8,128)(2,1)}, u32[]{:S(2)}) copy-start(bf16[128,512]{1,0:T(8,128)(2,1)} %copy-done.26) | copy-start | bytes 393220
  167.6 12.5 %collective-permute-start.6 = (bf16[2,1024,128]{2,1,0:T(8,128)(2,1)S(1)}, bf16[2,1024,128]{2,1,0:T(8,128)(2,1)S(1)}, u32[]{:S(2)}, u32[]{:S(2)}) collective-permute-start(bf16[2,1024,128]{2,1,0:T(8,128)(2,1)S(1)} %get-tuple-element.60), channel_id=1, source_target_pairs={{0,6},{1,7},{2,0},{3,1},{4,2},{5,3},{6,4},{7,5},{8,14},{9,15},{10,... | collective-permute-start | bytes 1572872 | tf_op jit(solution)/shard_map/ppermute | solution.py:439
  168.7 13.8 %collective-permute-start.7 = (bf16[2,1024,128]{2,1,0:T(8,128)(2,1)S(1)}, bf16[2,1024,128]{2,1,0:T(8,128)(2,1)S(1)}, u32[]{:S(2)}, u32[]{:S(2)}) collective-permute-start(bf16[2,1024,128]{2,1,0:T(8,128)(2,1)S(1)} %get-tuple-element.61), channel_id=1, source_target_pairs={{0,2},{1,3},{2,4},{3,5},{4,6},{5,7},{6,0},{7,1},{8,10},{9,11},{10,... | collective-permute-start | bytes 1572872 | tf_op jit(solution)/shard_map/ppermute | solution.py:439
  173.3 16.8 %copy-start.14 = (f32[2048,128]{1,0:T(8,128)S(1)}, f32[2048,128]{1,0:T(8,128)}, u32[]{:S(2)}) copy-start(f32[2048,128]{1,0:T(8,128)} %copy-done.13) | copy-start | bytes 3145732
  180.1 6.4 %collective-permute-start.9 = (bf16[1024,128]{1,0:T(8,128)(2,1)S(1)}, bf16[1024,128]{1,0:T(8,128)(2,1)S(1)}, u32[]{:S(2)}, u32[]{:S(2)}) collective-permute-start(bf16[1024,128]{1,0:T(8,128)(2,1)S(1)} %fusion.4), channel_id=1, source_target_pairs={{0,6},{1,7},{2,0},{3,1},{4,2},{5,3},{6,4},{7,5},{8,14},{9,15},{10,... | collective-permute-start | bytes 786440 | tf_op jit(solution)/shard_map/ppermute | solution.py:439
  182.5 7.7 %collective-permute-start.8 = (bf16[1024,128]{1,0:T(8,128)(2,1)S(1)}, bf16[1024,128]{1,0:T(8,128)(2,1)S(1)}, u32[]{:S(2)}, u32[]{:S(2)}) collective-permute-start(bf16[1024,128]{1,0:T(8,128)(2,1)S(1)} %fusion.5), channel_id=1, source_target_pairs={{0,2},{1,3},{2,4},{3,5},{4,6},{5,7},{6,0},{7,1},{8,10},{9,11},{10,... | collective-permute-start | bytes 786440 | tf_op jit(solution)/shard_map/ppermute | solution.py:439

commit v3 on v2

v3 whole, which is shorter than its diff:
```python
import functools

import jax
import jax.numpy as jnp
from jax import lax
from jax.experimental import pallas as pl
from jax.experimental.pallas import tpu as pltpu
from jax.sharding import PartitionSpec as P

F32 = jnp.float32
BF16 = jnp.bfloat16
LANES = 128
NT = (((1,), (1,)), ((), ()))
TN = (((0,), (0,)), ((), ()))
MIB = 1 << 20


def dot(a, b, dims=(((1,), (0,)), ((), ()))):
    return lax.dot_general(a, b, dims, preferred_element_type=F32)


def split_two(v):
    high = v.astype(BF16)
    return high, (v - high.astype(F32)).astype(BF16)


def iota(shape, dim):
    return lax.broadcasted_iota(jnp.int32, shape, dim)


def call(kernel, outs, scratch=(), specs=None, vmem=16, us=1, grid=None, out_specs=None):
    args = {} if specs is None else {"in_specs": specs}
    if grid is not None:
        args["grid"] = grid
    if out_specs is not None:
        args["out_specs"] = out_specs
    return pl.pallas_call(
        kernel,
        out_shape=outs,
        scratch_shapes=list(scratch),
        compiler_params=pltpu.CompilerParams(vmem_limit_bytes=vmem * MIB),
        cost_estimate=pl.CostEstimate(
            flops=us * 1_100_000_000, bytes_accessed=MIB, transcendentals=0
        ),
        **args,
    )


SMEM = pl.BlockSpec(memory_space=pltpu.SMEM)
VMEM = pl.BlockSpec(memory_space=pltpu.VMEM)
HBM = pl.BlockSpec(memory_space=pltpu.HBM)


def prep_kernel(tables, pairs, owner_ref, local_ref, ids_ref, pos_ref):
    bag = owner_ref.shape[1]
    steps = owner_ref.shape[0] * bag
    owners = [owner_ref[j // bag, j % bag : j % bag + 1, :] for j in range(steps)]
    row, col = iota((LANES, 2 * LANES), 0), iota((LANES, 2 * LANES), 1)
    tri = jnp.where((row < col) | (col >= LANES), 1.0, 0.0).astype(BF16)
    table_row = iota((tables, LANES), 0)
    slot_row = iota((2 * LANES, LANES), 0)
    hits = [
        jnp.where(owner == table_row, 1.0, 0.0) for owner in owners
    ]
    sums = dot(jnp.concatenate(hits, axis=0).astype(BF16), tri)
    carry = jnp.zeros((tables, LANES), F32)
    left, right = [], []
    for j in range(steps):
        part = sums[j * tables : (j + 1) * tables]
        slot = jnp.sum(hits[j] * (part[:, :LANES] + carry), axis=0, keepdims=True)
        slot = slot.astype(jnp.int32)
        carry = carry + part[:, LANES:]
        upper = jnp.where(slot >= pairs, 1, 0)
        pos_ref[j : j + 1, :] = (
            upper * (tables * pairs - pairs) + owners[j] * pairs + slot
        )
        local = local_ref[j // bag, j % bag : j % bag + 1, :]
        code = (((local >> 11) & 1) << 14) | ((local >> 12) << 11) | (local & 2047)
        high, low = (code >> 8).astype(F32), (code & 255).astype(F32)
        left.append(jnp.concatenate([hits[j] * high, hits[j] * low], axis=0).astype(BF16))
        right.append(jnp.where(slot + upper * (LANES - pairs) == slot_row, 1.0, 0.0).astype(BF16))
    placed = dot(jnp.concatenate(left, axis=1), jnp.concatenate(right, axis=1), NT)
    ids = (placed[:tables] * 256.0 + placed[tables:]).astype(jnp.int32)
    for k in range(tables):
        ids_ref[k] = ids[k : k + 1]


def lane_is_low(shape):
    return iota(shape, len(shape) - 1) < 64


def gather_kernel(ids_ref, vec_ref, table_ref, out_ref, packed, got_a, got_b):
    tables, pairs, _ = out_ref.shape
    size = 2048
    for c in range(packed.shape[0] // size):
        first = table_ref[:, 2 * c * size : (2 * c + 1) * size]
        second = table_ref[:, (2 * c + 1) * size : (2 * c + 2) * size]
        both = jnp.concatenate([first, second], axis=0)
        packed[c * size : (c + 1) * size, :] = both.astype(F32).T
    step = pairs // 2

    def one(part, source):
        first = source * (2 * LANES) + part * step
        base = pl.multiple_of(source * pairs + part * step, 8)
        read_a = [packed[pl.ds(ids_ref[first + u], 1), :] for u in range(step)]
        read_b = [packed[pl.ds(ids_ref[first + LANES + u], 1), :] for u in range(step)]
        for u in range(step):
            got_a[pl.ds(base + u, 1), :] = read_a[u]
            got_b[pl.ds(base + u, 1), :] = read_b[u]
        return source

    def per_source(source, carry):
        lax.fori_loop(0, 2, one, source)
        return carry

    lax.fori_loop(0, tables, per_source, 0)
    upper = (vec_ref[...] >> 14).astype(F32).T
    low = lane_is_low((pairs, LANES))
    for k in range(tables):
        a = got_a[k * pairs : (k + 1) * pairs, :]
        b = got_b[k * pairs : (k + 1) * pairs, :]
        up_a = upper[:pairs, k : k + 1] > 0.5
        up_b = upper[LANES : LANES + pairs, k : k + 1] > 0.5
        a = jnp.where(up_a, pltpu.roll(a, 64, 1), a)
        b = jnp.where(up_b, b, pltpu.roll(b, 64, 1))
        out_ref[k] = jnp.where(low, a, b).astype(BF16)


def front_kernel(
    dense_ref,
    weight_ref,
    hot_ref,
    unique_ref,
    map_ref,
    grad_ref,
    pre_ref,
    bottom_ref,
    emb_ref,
    counts_ref,
    high_ref,
    low_ref,
):
    batch = dense_ref.shape[0]
    hot_feats, bag = map_ref.shape[0], map_ref.shape[1]
    unique = unique_ref.shape[0]
    feats = high_ref.shape[0]
    pre = dot(dense_ref[...], weight_ref[...])
    pre_ref[...] = pre
    bottom_ref[...] = jax.nn.silu(pre).astype(BF16)
    picks = jnp.where(unique_ref[...] == iota((unique, hot_ref.shape[0]), 1), 1.0, 0.0)
    rows = dot(picks.astype(BF16), hot_ref[...]).astype(BF16)
    place = iota((unique, batch), 0)
    for h in range(hot_feats):
        count = jnp.zeros((unique, batch), F32)
        for l in range(bag):
            count += jnp.where(map_ref[h, l : l + 1, :] == place, 1.0, 0.0)
        counts_ref[:, h * batch : (h + 1) * batch] = count.astype(BF16)
        emb_ref[h] = dot(count.T.astype(BF16), rows).astype(BF16)
    grad = grad_ref[...]
    grad_high, grad_low = split_two(grad)
    square = feats * feats
    at = iota((square, square), 0)
    other = iota((square, square), 1) // feats
    same = iota((batch, square), 0) % feats == iota((batch, square), 1) % feats
    for f in range(feats):
        pick = jnp.where(at == f * feats + other, 1.0, 0.0) + jnp.where(
            at == other * feats + f, 1.0, 0.0
        )
        pick = pick.astype(BF16)
        spread = jnp.where(same, dot(grad_high, pick) + dot(grad_low, pick), 0.0)
        high_ref[f], low_ref[f] = split_two(spread)


def silu_slope(pre):
    sigma = jax.nn.sigmoid(pre)
    return sigma * (1.0 + pre * (1.0 - sigma))


def main_kernel(
    place_ref,
    pos_ref,
    rows_ref,
    band_ref,
    proj_ref,
    pre_ref,
    dense_ref,
    counts_ref,
    unique_ref,
    bottom_ref,
    hot_ref,
    high_ref,
    low_ref,
    slots_ref,
    cold_ref,
    kept_ref,
    given_ref,
    wide,
    lookups,
    stack,
    high,
    low_part,
    d_stack,
    bags,
    parts,
    kept,
    given,
    sems,
):
    tables, pairs, _ = rows_ref.shape
    feats, batch, hidden = stack.shape
    cold_feats = cold_ref.shape[0]
    bag = band_ref.shape[0] // cold_feats
    half = tables * pairs
    fixed = pl.ds(1 + cold_feats, feats - 1 - cold_feats)
    incoming = [
        pltpu.make_async_copy(bottom_ref, stack.at[0], sems.at[0]),
        pltpu.make_async_copy(hot_ref, stack.at[fixed], sems.at[1]),
        pltpu.make_async_copy(high_ref, high, sems.at[2]),
        pltpu.make_async_copy(low_ref, low_part, sems.at[3]),
    ]
    for copy in incoming:
        copy.start()
    low = lane_is_low((pairs, LANES))
    for k in range(tables):
        x = rows_ref[k].astype(F32)
        r = pltpu.roll(x, 64, 1)
        wide[k * pairs : (k + 1) * pairs, :] = jnp.where(low, x, r)
        wide[half + k * pairs : half + (k + 1) * pairs, :] = jnp.where(low, r, x)

    def fetch(i, carry):
        base = pl.multiple_of(i * 56, 8)
        got = [wide[pl.ds(pos_ref[base + u], 1), :] for u in range(56)]
        for u in range(56):
            lookups[pl.ds(base + u, 1), :] = got[u]
        return carry

    lax.fori_loop(0, lookups.shape[0] // 56, fetch, 0)
    band = band_ref[...].astype(F32).T
    side = jnp.where(lane_is_low((batch, LANES)), 0.0, 1.0)
    for f in range(cold_feats):
        first = jnp.zeros((batch, LANES), F32)
        second = jnp.zeros((batch, LANES), F32)
        for l in range(bag):
            j = f * bag + l
            x = lookups[j * batch : (j + 1) * batch, :]
            b = band[:, j : j + 1] - side
            first += jnp.where(b == 0.0, x, 0.0)
            second += jnp.where(b == 2.0, x, 0.0)
        pooled = jnp.concatenate([first, second], axis=1).astype(BF16)
        bags[f] = pooled
        stack[1 + f] = dot(pooled, proj_ref[...]).astype(BF16)
    outgoing = pltpu.make_async_copy(stack.at[pl.ds(1, cold_feats)], cold_ref, sems.at[4])
    outgoing.start()
    for copy in incoming:
        copy.wait()
    for g in range(batch // 16):
        at = slice(g * 16, (g + 1) * 16)
        x = stack[:, at, :].reshape(feats * 16, hidden)
        first = high[:, at, :].reshape(feats * 16, feats * 16)
        rest = low_part[:, at, :].reshape(feats * 16, feats * 16)
        d = (dot(first, x) + dot(rest, x)).astype(BF16)
        d_stack[:, at, :] = d.reshape(feats, 16, hidden)
    hot_feats = feats - 1 - cold_feats
    cuts = hidden // LANES
    d_pre = (d_stack[0].astype(F32) * silu_slope(pre_ref[...])).astype(BF16)
    bottom = dot(dense_ref[...], d_pre, TN)
    d_cold = d_stack[1 : 1 + cold_feats].reshape(cold_feats * batch, hidden)
    pooled = bags[...].reshape(cold_feats * batch, bags.shape[2])
    proj = dot(pooled, d_cold, TN)
    d_hot = d_stack[1 + cold_feats :].reshape(hot_feats * batch, hidden)
    first, rest = split_two(dot(counts_ref[...], d_hot))
    hot_rows = tables * 32
    picks = jnp.where(
        iota((hot_rows, unique_ref.shape[1]), 0) == unique_ref[...], 1.0, 0.0
    ).astype(BF16)
    hot = dot(picks, first) + dot(picks, rest)
    for c in range(cuts):
        at = slice(c * LANES, (c + 1) * LANES)
        parts[0, c] = hot[:, at]
        parts[1, c] = jnp.concatenate(
            [
                bottom[:, at].reshape(tables, 16, LANES),
                proj[:, at].reshape(tables, 8, LANES),
                jnp.zeros((tables, 8, LANES), F32),
            ],
            axis=1,
        ).reshape(hot_rows, LANES)
    core = place_ref[1]
    for k in range(cuts):
        chunk = (place_ref[0] + k) % cuts
        kept[k] = parts[core, chunk]
        given[k] = parts[1 - core, chunk].astype(BF16)
    dense_copies = [
        pltpu.make_async_copy(given, given_ref, sems.at[5]),
        pltpu.make_async_copy(kept, kept_ref, sems.at[6]),
    ]
    for copy in dense_copies:
        copy.start()
    low = lane_is_low((batch, LANES))
    for f in range(cold_feats):
        d_pool = dot(d_stack[1 + f], proj_ref[...], NT).astype(BF16).astype(F32)
        first, second = d_pool[:, :LANES], d_pool[:, LANES:]
        first_r, second_r = pltpu.roll(first, 64, 1), pltpu.roll(second, 64, 1)
        each = [
            jnp.where(low, first, first_r),
            jnp.where(low, first_r, first),
            jnp.where(low, second, second_r),
            jnp.where(low, second_r, second),
        ]
        for l in range(bag):
            j = f * bag + l
            b = jnp.broadcast_to(band[:, j : j + 1], (batch, LANES))
            x = jnp.where(b < 0.5, each[0], each[1])
            y = jnp.where(b < 2.5, each[2], each[3])
            lookups[j * batch : (j + 1) * batch, :] = jnp.where(b < 1.5, x, y)
            share = wide.shape[0] // (cold_feats * bag)
            wide[j * share : (j + 1) * share, :] = jnp.zeros((share, LANES), F32)

    def place(i, carry):
        base = pl.multiple_of(i * 56, 8)
        got = [lookups[pl.ds(base + u, 1), :] for u in range(56)]
        for u in range(56):
            wide[pl.ds(pos_ref[base + u], 1), :] = got[u]
        return carry

    lax.fori_loop(0, lookups.shape[0] // 56, place, 0)
    low = lane_is_low((pairs, LANES))
    for k in range(tables):
        a = wide[k * pairs : (k + 1) * pairs, :]
        b = wide[half + k * pairs : half + (k + 1) * pairs, :]
        slots_ref[k] = jnp.where(low, a, b).astype(BF16)
    outgoing.wait()
    for copy in dense_copies:
        copy.wait()


def inter_kernel(bottom_ref, cold_ref, hot_ref, inter_ref, stack, grams):
    feats, batch, hidden = stack.shape
    cold_feats = cold_ref.shape[0]
    stack[0] = bottom_ref[...]
    for f in range(cold_feats):
        stack[1 + f] = cold_ref[f]
    for h in range(hot_ref.shape[0]):
        stack[1 + cold_feats + h] = hot_ref[h]
    square = feats * feats
    same = iota((square, square), 0) % feats == iota((square, square), 1) % feats
    for g in range(batch // 16):
        at = slice(g * 16, (g + 1) * 16)
        x = stack[:, at, :].reshape(feats * 16, hidden)
        grams[:, at, :] = jnp.where(same, dot(x, x, NT), 0.0).reshape(feats, 16, square)
    total = jnp.zeros((batch, square), F32)
    other = iota((square, square), 0) // feats
    to = iota((square, square), 1)
    for f in range(feats):
        pick = jnp.where(to == f * feats + other, 1.0, 0.0).astype(BF16)
        high, rest = split_two(grams[f])
        total += dot(high, pick) + dot(rest, pick)
    inter_ref[...] = total


def add_kernel(
    place_ref,
    ids_ref,
    vec_ref,
    rows_ref,
    given_far_ref,
    given_near_ref,
    given_own_ref,
    kept_far_ref,
    kept_near_ref,
    kept_own_ref,
    val_a,
    val_b,
    given,
    kept,
    kept_own,
    sems,
    *sums,
):
    tables, pairs, _ = rows_ref.shape
    upper = (vec_ref[...] >> 14).astype(F32).T
    low = lane_is_low((pairs, LANES))
    side = jnp.where(low, 0.0, 1.0)
    for k in range(tables):
        x = rows_ref[k].astype(F32)
        r = pltpu.roll(x, 64, 1)
        share = sums[0].shape[0] // tables
        for part in sums:
            part[k * share : (k + 1) * share, :] = jnp.zeros((share, LANES), F32)
        at = slice(k * pairs, (k + 1) * pairs)
        up_a, up_b = upper[:pairs, k : k + 1], upper[LANES : LANES + pairs, k : k + 1]
        val_a[at, :] = jnp.where(up_a == side, jnp.where(low, x, r), 0.0)
        val_b[at, :] = jnp.where(up_b == side, jnp.where(low, r, x), 0.0)
    half = tables // 2
    step = pairs // 2

    def one(group, source):
        first = source * (2 * LANES) + group * step
        base = pl.multiple_of(source * pairs + group * step, 8)
        for u in range(step):
            spots = [
                ids_ref[first + half * which * 2 * LANES + side * LANES + u]
                for which in range(2)
                for side in range(2)
            ]
            new = [
                sums[2 * which + side][pl.ds(spots[2 * which + side], 1), :]
                + val[pl.ds(base + half * which * pairs + u, 1), :]
                for which in range(2)
                for side, val in enumerate((val_a, val_b))
            ]
            for part, spot, value in zip(sums, spots, new):
                part[pl.ds(spot, 1), :] = value
        return source

    def per_source(source, carry):
        lax.fori_loop(0, 2, one, source)
        return carry

    lax.fori_loop(0, half, per_source, 0)
    core = place_ref[1]
    half = kept_own.shape[1]
    size = 2 * half

    def total(k, h, of):
        chunk = 2 * ((place_ref[0] + k) % 4) + of
        at = pl.ds(pl.multiple_of(chunk * size + h * half, half), half)
        return functools.reduce(jnp.add, [part[at, :] for part in sums])

    copies = []

    def send(source, target):
        copies.append(pltpu.make_async_copy(source, target, sems.at[len(copies)]))
        copies[-1].start()

    for k, target in enumerate((given_far_ref, given_near_ref, given_near_ref, given_own_ref)):
        for h in range(2):
            given[k, h] = total((2, 1, 3, 0)[k], h, 1 - core).astype(BF16)
        send(given.at[k], target.at[k - 1] if k in (1, 2) else target)
    for k, target in enumerate((kept_far_ref, kept_near_ref, kept_near_ref)):
        for h in range(2):
            kept[k, h] = total((2, 1, 3)[k], h, core).astype(BF16)
        send(kept.at[k], target.at[k - 1] if k else target)
    for h in range(2):
        kept_own[h] = total(0, h, core)
    send(kept_own, kept_own_ref)
    for copy in copies:
        copy.wait()


def sum_rows(rows_ref):
    total = rows_ref[0].astype(F32)
    for k in range(1, rows_ref.shape[0]):
        total += rows_ref[k].astype(F32)
    return total


def dense_kernel(rows_ref, out_ref):
    rows = rows_ref.shape[1]
    out_ref[:rows], out_ref[rows:] = split_two(sum_rows(rows_ref))


def add_pair(kept, taken):
    return (kept.astype(F32) + taken.astype(F32)).astype(BF16)


def far_kernel(place_ref, kept_ref, taken_ref, mine_ref, theirs_ref, up_ref, down_ref):
    half = kept_ref.shape[1]
    rows = mine_ref.shape[0]
    first = place_ref[1] == 0
    mine, theirs = mine_ref[...].astype(F32), theirs_ref[...].astype(F32)
    low = jnp.where(first, mine, theirs).astype(BF16)
    high = jnp.where(first, theirs, mine).astype(BF16)
    for h, out_ref in enumerate((up_ref, down_ref)):
        out_ref[:half] = add_pair(kept_ref[h], taken_ref[h])
        out_ref[half : half + rows] = low
        out_ref[half + rows :] = high


def second_kernel(kept_ref, taken_ref, below_ref, above_ref, up_ref, down_ref):
    half = kept_ref.shape[2]

    def total(k, h, far):
        return (
            kept_ref[k, h].astype(F32) + taken_ref[k, h].astype(F32) + far.astype(F32)
        ).astype(BF16)

    up_ref[:half] = total(0, 0, below_ref[:half])
    up_ref[half : 2 * half] = add_pair(kept_ref[0, 1], taken_ref[0, 1])
    up_ref[2 * half :] = below_ref[half:]
    down_ref[:half] = add_pair(kept_ref[1, 0], taken_ref[1, 0])
    down_ref[half:] = total(1, 1, above_ref[:half])


def own_kernel(kept_ref, taken_ref, out_ref):
    out_ref[...] = kept_ref[...] + taken_ref[...].astype(F32)


def last_kernel(
    place_ref,
    pair_ref,
    below_ref,
    above_ref,
    own_ref,
    next_ref,
    before_ref,
    out_ref,
    hot_ref,
    proj_ref,
    bottom_ref,
):
    half = pair_ref.shape[1]

    def total(h):
        at = slice(h * half, (h + 1) * half)
        return pair_ref[h] + below_ref[at].astype(F32) + above_ref[at].astype(F32)

    wide = jnp.concatenate([total(0), total(1)], axis=0).T
    out_ref[...] = jnp.concatenate([wide[:64], wide[64:]], axis=1)
    tails = (own_ref[half:], next_ref[half:], below_ref[2 * half :], before_ref[half:])
    for k, tail in enumerate(tails):
        chunk = (place_ref[0] + k) % len(tails)
        at = pl.ds(pl.multiple_of(chunk * LANES, LANES), LANES)
        rows = tail.astype(F32)
        hot_ref[:, at] = rows[:32] + rows[32:64]
        rest = rows[64:96] + rows[96:]
        bottom_ref[:, at] = rest[:16]
        proj_ref[:, at] = rest[16:24]


def to_other_core(x):
    return lax.ppermute(x, "dp", [(i, i ^ 1) for i in range(8)])


def along_x(x, steps):
    return lax.ppermute(x, "dp", [(i, (i + 2 * steps) % 8) for i in range(8)])


def exchange(x, axis):
    return lax.all_to_all(x, axis, split_axis=0, concat_axis=0, tiled=True)


def shards(
    dense_input,
    bottom_weight,
    cold_table,
    projection,
    hot_table,
    cold_owner,
    cold_local,
    cold_band,
    hot_unique,
    hot_map,
    grad_inter,
):
    batch, hidden = dense_input.shape
    cold_feats, bag = cold_local.shape[1], cold_local.shape[2]
    hot_feats = hot_map.shape[1]
    feats = 1 + cold_feats + hot_feats
    tables = lax.axis_size("table")
    rows_dev, width = cold_table.shape
    unique = hot_unique.shape[0]
    lookups = batch * cold_feats * bag
    slots = 2 * lookups // tables
    pairs = slots // 2
    bands = projection.shape[0]
    at_dp = lax.axis_index("dp").astype(jnp.int32)
    place = jnp.stack([at_dp // 2, at_dp % 2])

    def by_sample(v):
        return jnp.transpose(v.reshape(batch, cold_feats, bag), (1, 2, 0))

    shape = jax.ShapeDtypeStruct
    ids, pos = call(
        functools.partial(prep_kernel, tables, pairs),
        (shape((tables, 1, 2 * LANES), jnp.int32), shape((cold_feats * bag, batch), jnp.int32)),
    )(by_sample(cold_owner), by_sample(cold_local))
    pos = pos.reshape(lookups)
    asked = exchange(ids, "table").reshape(tables, 2 * LANES)
    row_ids = (asked & (rows_dev // 2 - 1)).reshape(tables * 2 * LANES)
    fetched = call(
        gather_kernel,
        shape((tables, pairs, LANES), BF16),
        scratch=[pltpu.VMEM((rows_dev // 2, LANES), F32)]
        + [pltpu.VMEM((tables * pairs, LANES), F32)] * 2,
        specs=[SMEM, VMEM, VMEM],
        us=12,
        vmem=24,
    )(row_ids, asked, cold_table.T)
    received = exchange(fetched, "table")
    pre, bottom, hot_emb, counts, high, low = call(
        front_kernel,
        (
            shape((batch, hidden), F32),
            shape((batch, hidden), BF16),
            shape((hot_feats, batch, hidden), BF16),
            shape((unique, hot_feats * batch), BF16),
            shape((feats, batch, feats * feats), BF16),
            shape((feats, batch, feats * feats), BF16),
        ),
        us=3,
    )(
        dense_input,
        bottom_weight,
        hot_table,
        hot_unique.reshape(unique, 1),
        jnp.transpose(hot_map, (1, 2, 0)),
        grad_inter,
    )
    cuts = hidden // LANES
    slot_grads, cold_emb, dense_kept, dense_given = call(
        main_kernel,
        (
            shape((tables, pairs, LANES), BF16),
            shape((cold_feats, batch, hidden), BF16),
            shape((cuts, tables * 32, LANES), F32),
            shape((cuts, tables * 32, LANES), BF16),
        ),
        scratch=[
            pltpu.VMEM((2 * tables * pairs, LANES), F32),
            pltpu.VMEM((lookups, LANES), F32),
            pltpu.VMEM((feats, batch, hidden), BF16),
            pltpu.VMEM((feats, batch, feats * feats), BF16),
            pltpu.VMEM((feats, batch, feats * feats), BF16),
            pltpu.VMEM((feats, batch, hidden), BF16),
            pltpu.VMEM((cold_feats, batch, bands), BF16),
            pltpu.VMEM((2, cuts, tables * 32, LANES), F32),
            pltpu.VMEM((cuts, tables * 32, LANES), F32),
            pltpu.VMEM((cuts, tables * 32, LANES), BF16),
            pltpu.SemaphoreType.DMA((7,)),
        ],
        specs=[SMEM] * 2 + [VMEM] * 7 + [HBM] * 4,
        out_specs=[VMEM, HBM, HBM, HBM],
        us=14,
        vmem=62,
    )(
        place,
        pos,
        received,
        by_sample(cold_band).reshape(cold_feats * bag, batch),
        projection,
        pre,
        dense_input,
        counts,
        hot_unique.reshape(1, unique),
        bottom,
        hot_emb,
        high,
        low,
    )
    returned = exchange(slot_grads, "table")
    dense_pair = dense_kept + to_other_core(dense_given).astype(F32)
    dense_out = dense_pair[1:].astype(BF16)
    dense_row = dense_pair[0]
    for k, steps in enumerate((1, 2, -1)):
        dense_row += along_x(dense_out[k], steps).astype(F32)
    dense_row = dense_row.astype(BF16).reshape(tables, 32, LANES)
    returned, dense_row = lax.optimization_barrier((returned, dense_row))
    dense_all = exchange(dense_row, "table")

    half = rows_dev // 32
    given_far, given_near, given_own, kept_far, kept_near, kept_own = call(
        add_kernel,
        (
            shape((2, half, LANES), BF16),
            shape((2, 2, half, LANES), BF16),
            shape((2, half, LANES), BF16),
            shape((2, half, LANES), BF16),
            shape((2, 2, half, LANES), BF16),
            shape((2, half, LANES), F32),
        ),
        scratch=[pltpu.VMEM((tables * pairs, LANES), F32)] * 2
        + [
            pltpu.VMEM((4, 2, half, LANES), BF16),
            pltpu.VMEM((3, 2, half, LANES), BF16),
            pltpu.VMEM((2, half, LANES), F32),
            pltpu.SemaphoreType.DMA((8,)),
        ]
        + [pltpu.VMEM((rows_dev // 2, LANES), F32)] * 4,
        specs=[SMEM, SMEM, VMEM, VMEM],
        out_specs=[HBM] * 6,
        us=20,
        vmem=62,
    )(place, row_ids, asked, returned)
    given_far, given_near, given_own, dense_all = lax.optimization_barrier(
        (given_far, given_near, given_own, dense_all)
    )
    mine = call(dense_kernel, shape((64, LANES), BF16))(dense_all)
    taken_far = to_other_core(given_far)
    theirs = to_other_core(mine)
    taken_near = to_other_core(given_near)
    taken_own = to_other_core(given_own)
    up, down = call(far_kernel, (shape((half + 128, LANES), BF16),) * 2, specs=[SMEM] + [VMEM] * 4)(
        place, kept_far, taken_far, mine, theirs
    )
    from_below = along_x(up, 1)
    from_above = along_x(down, -1)
    up, down, cold_emb = lax.optimization_barrier((up, down, cold_emb))
    inter = call(
        inter_kernel,
        shape((batch, feats * feats), F32),
        scratch=[
            pltpu.VMEM((feats, batch, hidden), BF16),
            pltpu.VMEM((feats, batch, feats * feats), F32),
        ],
        us=4,
    )(bottom, cold_emb, hot_emb)
    from_below, from_above, taken_near, taken_own, inter = lax.optimization_barrier(
        (from_below, from_above, taken_near, taken_own, inter)
    )
    next_up, next_down = call(
        second_kernel,
        (shape((2 * half + 128, LANES), BF16), shape((2 * half, LANES), BF16)),
    )(kept_near, taken_near, from_below, from_above)
    next_up, next_down, kept_own, taken_own = lax.optimization_barrier(
        (next_up, next_down, kept_own, taken_own)
    )
    pair_own = call(own_kernel, shape((2, half, LANES), F32), us=2)(kept_own, taken_own)
    next_below = along_x(next_up, 1)
    next_above = along_x(next_down, -1)
    cold_grad, hot_grad, projection_grad, bottom_grad = call(
        last_kernel,
        (
            shape((width, rows_dev // 8), F32),
            shape((32, hidden), F32),
            shape((8, hidden), F32),
            shape((16, hidden), F32),
        ),
        specs=[SMEM] + [VMEM] * 6,
        us=2,
    )(place, pair_own, next_below, next_above, up, from_above, from_below)
    return inter, cold_grad.T, hot_grad, projection_grad, bottom_grad


def solution(mesh):
    placed = (
        P(("table", "dp"), None),
        P(),
        P("table", None),
        P(),
        P(),
        P(("table", "dp"), None, None, None),
        P(("table", "dp"), None, None),
        P(("table", "dp"), None, None),
        P(("table", "dp")),
        P(("table", "dp"), None, None),
        P(("table", "dp"), None),
    )
    return jax.shard_map(
        shards,
        mesh=mesh,
        in_specs=placed,
        out_specs=(
            P(("table", "dp"), None),
            P(("table", "dp"), None),
            P("table", None),
            P("table", None),
            P("table", None),
        ),
        check_vma=False,
    )
```

time: 192 us -> 171 us (0.89)
  blocking collectives: 0 us -> 20.3 us
  local copies, waits for them, and re-layouts: 27.4 us -> 8.63 us
  starting transfers between devices: 50.4 us -> 33.7 us
  waiting for transfers between devices: 52.7 us -> 47.8 us
    all_to_all x0 -> x1, blocking collectives: none -> 20.3 us  [exchange(): return lax.all_to_all(x, axis, split_axis=0, concat_axis=0, tiled=True)]
    unnamed x61 -> x59, local copies, waits for them, and re-layouts: 24.4 us -> 7.83 us
    all_to_all x4 -> x3, starting transfers between devices: 35.1 us -> 20.4 us  [exchange(): return lax.all_to_all(x, axis, split_axis=0, concat_axis=0, tiled=True)]
    all_to_all x4 -> x3, waiting for transfers between devices: 21.2 us -> 18 us  [exchange(): return lax.all_to_all(x, axis, split_axis=0, concat_axis=0, tiled=True)]
    ppermute x10 -> x7, starting transfers between devices: 14.5 us -> 12 us  [along_x(): return lax.ppermute(x, 'dp', [(i, (i + 2 * steps) % 8) for i in range(8)])]
    ppermute x10 -> x7, waiting for transfers between devices: 28.9 us -> 26.6 us  [along_x(): return lax.ppermute(x, 'dp', [(i, (i + 2 * steps) % 8) for i in range(8)])]
    pallas_call x7 -> x8, Pallas kernels: 40.5 us -> 38.6 us  [the longest x1 20.5 us: shards(): call(add_kernel, (shape((2, half, LANES), BF16), shape((2, 2, half, LANES...]
  transfers between devices with their start and end apart: 18 -> 15, of which waited for: 13 -> 10; matrix products, arithmetic and copies ran while one was open for 2% -> 2% of each run, Pallas kernels for 14% -> 16%
where the time goes in v3:
time: 171 us; the launch traced here: 170 us
  Pallas kernels  55.2 us (32%)
  waiting for transfers between devices  47.8 us (28%)
  starting transfers between devices  33.7 us (20%)
  blocking collectives  20.3 us (12%)
  local copies, waits for them, and re-layouts  8.63 us (5%)
  other arithmetic  3.38 us (2%)
    ppermute x7, waiting for transfers between devices, along_x(): return lax.ppermute(x, 'dp', [(i, (i + 2 * steps) % 8) for i in range(8)])  26.6 us
    pallas_call x1, Pallas kernels, shards(): call(add_kernel, (shape((2, half, LANES), BF16), shape((2, 2, half, LANES...  20.5 us
    all_to_all x3, starting transfers between devices, exchange(): return lax.all_to_all(x, axis, split_axis=0, concat_axis=0, tiled=True)  20.4 us
    all_to_all x1, blocking collectives, exchange(): return lax.all_to_all(x, axis, split_axis=0, concat_axis=0, tiled=True)  20.3 us
    all_to_all x3, waiting for transfers between devices, exchange(): return lax.all_to_all(x, axis, split_axis=0, concat_axis=0, tiled=True)  18 us
    pallas_call x1, Pallas kernels, shards(): call(main_kernel, (shape((tables, pairs, LANES), BF16), shape((cold_feats...  14.1 us
    ppermute x7, starting transfers between devices, along_x(): return lax.ppermute(x, 'dp', [(i, (i + 2 * steps) % 8) for i in range(8)])  12 us
    pallas_call x1, Pallas kernels, shards(): call(gather_kernel, shape((tables, pairs, LANES), BF16), scratch=[pltpu.V...  11 us
  transfers between devices with their start and end apart: 15, of which 10 were waited for; matrix products, arithmetic and copies ran while one was open for 2% of the time, Pallas kernels for 16%

profile of v3, /device:TPU:8, one launch (start us, length us, event | category | flops | bytes accessed | tf_op | source)
XLA Modules:
  0.0 170.1 jit_solution(8097900049522036781)
XLA Ops:
  0.6 0.7 copy-done.8
  1.3 0.7 copy-done.9
  2.1 1.0 shard_map.146
  3.1 0.0 copy-start.10
  3.1 20.3 %all_to_all.20 = s32[32,1,256]{2,1,0:T(1,128)S(1)} all-to-all(s32[32,1,256]{2,1,0:T(1,128)S(1)} %get-tuple-element.48), channel_id=1, replica_groups=mesh['table'=32,'dp'=8] {'table'}, dimensions={0} | all-to-all | bytes 65536 | tf_op jit(solution)/shard_map/all_to_all | solution.py:540
  23.5 0.0 copy-start.1
  23.5 0.0 copy-start.26
  23.5 0.0 copy-start.27
  23.5 0.0 copy-start.3
  23.5 0.0 copy-start.4
  23.5 0.0 copy-start.5
  23.6 0.0 copy-start.6
  23.6 0.0 copy-start.7
  23.6 11.0 %shard_map.147 = bf16[32,112,128]{2,1,0:T(8,128)(2,1)} custom-call(s32[8192]{0:T(1024)S(1)} %bitcast.36, s32[32,256]{1,0:T(8,128)S(1)} %bitcast.34, bf16[64,32768]{1,0:T(8,128)(2,1)S(1)} %bitcast.38), custom_call_target="tpu_custom_call" | custom-call | flops 13200000000 | bytes 1048576 | tf_op jit(solution)/shard_map/pallas_call | solution.py:581
  34.6 5.1 %all-to-all-start.1 = ((bf16[32,112,128]{2,1,0:T(8,128)(2,1)}), bf16[32,112,128]{2,1,0:T(8,128)(2,1)S(1)}, u32[]{:S(2)}, u32[]{:S(2)}) async-start(bf16[32,112,128]{2,1,0:T(8,128)(2,1)} %shard_map.147), calls=%async_computation.1 | async-start | bytes 1835008 | tf_op jit(solution)/shard_map/all_to_all | solution.py:540
  39.7 0.6 reshape.38.band_ref
  40.3 0.1 copy.19.unique_ref
  40.5 0.6 pad_add_fusion.place_ref
  41.2 2.6 %shard_map.148 = (f32[128,512]{1,0:T(8,128)S(1)}, bf16[128,512]{1,0:T(8,128)(2,1)S(1)}, bf16[8,128,512]{2,1,0:T(8,128)(2,1)S(1)}, bf16[256,1024]{1,0:T(8,128)(2,...) custom-call(bf16[128,512]{1,0:T(8,128)(2,1)S(1)} %copy-done.6, ...), custom_call_target="tpu_custom_call" | custom-call | flops 3300000000 | bytes 1048576 | tf_op jit(solution)/shard_map/pallas_call | solution.py:591
  43.8 0.0 copy-start.15
  43.8 1.0 copy-done.15
  44.7 1.0 copy-done.17
  45.7 1.0 copy-done.18
  46.7 0.9 copy-done.19
  47.6 0.7 copy-done.21
  48.3 0.7 copy-done.22
  48.9 12.8 %all-to-all-done.1.rows_ref = bf16[32,112,128]{2,1,0:T(8,128)(2,1)S(1)} async-done(((bf16[32,112,128]{2,1,0:T(8,128)(2,1)}), bf16[32,112,128]{2,1,0:T(8,128)(2,1)S(1)}, u32[]{:S(2)}, u32[]{:S(2)}) %all-to-all-start.1) | async-done | bytes 917536 | tf_op jit(solution)/shard_map/all_to_all | solution.py:540
  61.8 1.0 copy-done.24
  62.8 14.1 %shard_map.149 = (bf16[32,112,128]{2,1,0:T(8,128)(2,1)}, bf16[7,128,512]{2,1,0:T(8,128)(2,1)}, f32[4,1024,128]{2,1,0:T(8,128)}, bf16[4,1024,128]{2,1,0:T(8,128)(2,1)}) custom-call(s32[2]{0:T(128)} %pad_add_fusion.place_ref, s32[3584]{0:T(1024)} %bitcast.42, bf16[32,112,128]{2,1,0:T(8,128)(2,1)} %copy-done.24, s32[28,128]{1,0:T(8,128)} %reshape.38.band_ref, ...), custom_call_target="tpu_custom_call" | custom-call | flops 15399999488 | bytes 1048576 | tf_op jit(solution)/shard_map/pallas_call | solution.py:611
  76.9 0.3 collective-permute-start
  77.2 7.8 %all-to-all-start.2 = ((bf16[32,112,128]{2,1,0:T(8,128)(2,1)}), bf16[32,112,128]{2,1,0:T(8,128)(2,1)S(1)}, u32[]{:S(2)}, u32[]{:S(2)}) async-start(bf16[32,112,128]{2,1,0:T(8,128)(2,1)} %get-tuple-element.56), calls=%async_computation.2 | async-start | bytes 1835008 | tf_op jit(solution)/shard_map/all_to_all | solution.py:540
  85.0 1.9 %fusion.4 = (bf16[4,1024,128]{2,1,0:T(8,128)(2,1)S(1)}, f32[4,1024,128]{2,1,0:T(8,128)S(1)}) fusion(f32[4,1024,128]{2,1,0:T(8,128)} %get-tuple-element.57, bf16[4,1024,128]{2,1,0:T(8,128)(2,1)S(1)} %collective-permute-done), kind=kLoop, calls=%fused_computation.12 | loop fusion | flops 1572864 | bytes 6291456 | tf_op jit(solution)/shard_map/convert
  86.8 0.1 slice_bitcast_fusion.3
  86.9 1.6 collective-permute-start.1
  88.5 1.7 %collective-permute-start.3 = (bf16[1024,128]{1,0:T(8,128)(2,1)S(1)}, bf16[1024,128]{1,0:T(8,128)(2,1)S(1)}, u32[]{:S(2)}, u32[]{:S(2)}) collective-permute-start(bf16[1024,128]{1,0:T(8,128)(2,1)S(1)} %get-tuple-element.94), channel_id=1, source_target_pairs={{0,6},{1,7},{2,0},{3,1},{4,2},{5,3},{6,4},{7,5},{8,14},{9,15},{10,... | collective-permute-start | bytes 786440 | tf_op jit(solution)/shard_map/ppermute | solution.py:536
  90.2 1.8 %collective-permute-start.2 = (bf16[1024,128]{1,0:T(8,128)(2,1)S(1)}, bf16[1024,128]{1,0:T(8,128)(2,1)S(1)}, u32[]{:S(2)}, u32[]{:S(2)}) collective-permute-start(bf16[1024,128]{1,0:T(8,128)(2,1)S(1)} %get-tuple-element.95), channel_id=1, source_target_pairs={{0,4},{1,5},{2,6},{3,7},{4,0},{5,1},{6,2},{7,3},{8,12},{9,13},{10,... | collective-permute-start | bytes 786440 | tf_op jit(solution)/shard_map/ppermute | solution.py:536
  92.0 4.4 %collective-permute-done.1 = bf16[1024,128]{1,0:T(8,128)(2,1)S(1)} collective-permute-done((bf16[1024,128]{1,0:T(8,128)(2,1)S(1)}, bf16[1024,128]{1,0:T(8,128)(2,1)S(1)}, u32[]{:S(2)}, u32[]{:S(2)}) %collective-permute-start.1) | collective-permute-done | bytes 262176 | tf_op jit(solution)/shard_map/ppermute | solution.py:536
  96.4 4.8 %collective-permute-done.3 = bf16[1024,128]{1,0:T(8,128)(2,1)S(1)} collective-permute-done((bf16[1024,128]{1,0:T(8,128)(2,1)S(1)}, bf16[1024,128]{1,0:T(8,128)(2,1)S(1)}, u32[]{:S(2)}, u32[]{:S(2)}) %collective-permute-start.3) | collective-permute-done | bytes 262176 | tf_op jit(solution)/shard_map/ppermute | solution.py:536
  101.2 1.7 collective-permute-done.2
  102.9 0.8 fusion.3
  103.8 5.2 %all-to-all-done.2.rows_ref = bf16[32,112,128]{2,1,0:T(8,128)(2,1)S(1)} async-done(((bf16[32,112,128]{2,1,0:T(8,128)(2,1)}), bf16[32,112,128]{2,1,0:T(8,128)(2,1)S(1)}, u32[]{:S(2)}, u32[]{:S(2)}) %all-to-all-start.2) | async-done | bytes 917536 | tf_op jit(solution)/shard_map/all_to_all | solution.py:540
  109.0 7.5 %all-to-all-start.3 = ((bf16[32,32,128]{2,1,0:T(8,128)(2,1)}), bf16[32,32,128]{2,1,0:T(8,128)(2,1)S(1)}, u32[]{:S(2)}, u32[]{:S(2)}) async-start(bf16[32,32,128]{2,1,0:T(8,128)(2,1)} %bitcast.16), calls=%async_computation.3 | async-start | bytes 524288 | tf_op jit(solution)/shard_map/all_to_all | solution.py:540
  116.5 20.5 %shard_map.150 = (bf16[2,1024,128]{2,1,0:T(8,128)(2,1)}, bf16[2,2,1024,128]{3,2,1,0:T(8,128)(2,1)}, bf16[2,1024,128]{2,1,0:T(8,128)(2,1)}, bf16[2,1024,128]{2,1,...) custom-call(s32[2]{0:T(128)} %pad_add_fusion.place_ref, s32[8192]{0:T(1024)} %bitcast.37, ...), custom_call_target="tpu_custom_call" | custom-call | flops 22000001024 | bytes 1048576 | tf_op jit(solution)/shard_map/pallas_call | solution.py:662
  137.1 0.0 all-to-all-done.3.rows_ref
  137.1 0.1 collective-permute-start.8
  137.2 0.5 collective-permute-start.4
  137.7 0.0 copy-start.23
  137.8 0.2 collective-permute-start.5
  137.9 0.1 copy-done.28
  138.1 0.3 collective-permute-start.9
  138.4 1.5 collective-permute-done.5.theirs_ref
  139.9 1.7 collective-permute-done.4.taken_ref
  141.5 0.7 shard_map.152
  142.2 1.8 %collective-permute-start.6 = (bf16[1152,128]{1,0:T(8,128)(2,1)S(1)}, bf16[1152,128]{1,0:T(8,128)(2,1)S(1)}, u32[]{:S(2)}, u32[]{:S(2)}) collective-permute-start(bf16[1152,128]{1,0:T(8,128)(2,1)S(1)} %get-tuple-element.86.own_ref), channel_id=1, source_target_pairs={{0,2},{1,3},{2,4},{3,5},{4,6},{5,7},{6,0},{7,1},{8,10},{9,11},{10,... | collective-permute-start | bytes 884744 | tf_op jit(solution)/shard_map/ppermute | solution.py:536
  144.0 1.8 %collective-permute-start.7 = (bf16[1152,128]{1,0:T(8,128)(2,1)S(1)}, bf16[1152,128]{1,0:T(8,128)(2,1)S(1)}, u32[]{:S(2)}, u32[]{:S(2)}) collective-permute-start(bf16[1152,128]{1,0:T(8,128)(2,1)S(1)} %get-tuple-element.68), channel_id=1, source_target_pairs={{0,6},{1,7},{2,0},{3,1},{4,2},{5,3},{6,4},{7,5},{8,14},{9,15},{10,... | collective-permute-start | bytes 884744 | tf_op jit(solution)/shard_map/ppermute | solution.py:536
  145.8 3.0 %shard_map.153 = f32[128,256]{1,0:T(8,128)} custom-call(bf16[128,512]{1,0:T(8,128)(2,1)S(1)} %copy-done.23, bf16[7,128,512]{2,1,0:T(8,128)(2,1)S(1)} %copy-done.20, bf16[8,128,512]{2,1,0:T(8,128)(2,1)S(1)} %copy-done.16), custom_call_target="tpu_custom_call" | custom-call | flops 4400000000 | bytes 1048576 | tf_op jit(solution)/shard_map/pallas_call | solution.py:699
  148.8 4.0 %collective-permute-done.6.below_ref.before_ref = bf16[1152,128]{1,0:T(8,128)(2,1)S(1)} collective-permute-done((bf16[1152,128]{1,0:T(8,128)(2,1)S(1)}, bf16[1152,128]{1,0:T(8,128)(2,1)S(1)}, u32[]{:S(2)}, u32[]{:S(2)}) %collective-permute-start.6) | collective-permute-done | bytes 294944 | tf_op jit(solution)/shard_map/ppermute | solution.py:536
  152.8 0.3 shard_map.154
  153.1 1.5 collective-permute-start.10
  154.6 1.8 %collective-permute-start.11 = (bf16[2048,128]{1,0:T(8,128)(2,1)S(1)}, bf16[2048,128]{1,0:T(8,128)(2,1)S(1)}, u32[]{:S(2)}, u32[]{:S(2)}) collective-permute-start(bf16[2048,128]{1,0:T(8,128)(2,1)S(1)} %get-tuple-element.85), channel_id=1, source_target_pairs={{0,6},{1,7},{2,0},{3,1},{4,2},{5,3},{6,4},{7,5},{8,14},{9,15},{10,... | collective-permute-start | bytes 1572872 | tf_op jit(solution)/shard_map/ppermute | solution.py:536
  156.4 0.1 shard_map.155.pair_ref
  156.5 10.7 %collective-permute-done.11.above_ref = bf16[2048,128]{1,0:T(8,128)(2,1)S(1)} collective-permute-done((bf16[2048,128]{1,0:T(8,128)(2,1)S(1)}, bf16[2048,128]{1,0:T(8,128)(2,1)S(1)}, u32[]{:S(2)}, u32[]{:S(2)}) %collective-permute-start.11) | collective-permute-done | bytes 524320 | tf_op jit(solution)/shard_map/ppermute | solution.py:536
  167.2 1.1 collective-permute-done.10.below_ref
  168.2 1.9 %shard_map.156 = (f32[64,4096]{1,0:T(8,128)}, f32[32,512]{1,0:T(8,128)}, f32[8,512]{1,0:T(8,128)}, f32[16,512]{1,0:T(8,128)}) custom-call(s32[2]{0:T(128)S(1)} %copy-done.11, f32[2,1024,128]{2,1,0:T(8,128)S(1)} %shard_map.155.pair_ref, bf16[2176,128]{1,0:T(8,128)(2,1)S(1)} %collective-permute-done.10.below_ref, ...), custom_call_target="tpu_custom_call" | custom-call | flops 2200000000 | bytes 1048576 | tf_op jit(solution)/shard_map/pallas_call | solution.py:721
  (44 shorter events, 0.2 us)
Async XLA Ops:
  0.6 0.7 copy-start.8
  1.3 0.7 copy-start.9
  2.1 21.4 %copy-start.2 = (bf16[32768,64]{0,1:T(8,128)(2,1)S(1)}, bf16[32768,64]{0,1:T(8,128)(2,1)}, u32[]{:S(2)}) copy-start(bf16[32768,64]{0,1:T(8,128)(2,1)} %param.13) | copy-start | bytes 12582916
  3.1 20.4 %copy-start.10 = (s32[28,128]{1,0:T(8,128)}, s32[28,128]{1,0:T(8,128)S(1)}, u32[]{:S(2)}) copy-start(s32[28,128]{1,0:T(8,128)S(1)} %get-tuple-element.49) | copy-start | bytes 43012
  23.4 11.2 %copy-start = (s32[32,1,256]{2,0,1:T(8,128)}, s32[32,1,256]{2,0,1:T(8,128)S(1)}, u32[]{:S(2)}) copy-start(s32[32,1,256]{2,0,1:T(8,128)S(1)} %copy.22) | copy-start | bytes 98308
  23.5 11.1 %copy-start.1 = (s32[32,1,256]{2,1,0:T(1,128)}, s32[32,1,256]{2,1,0:T(1,128)S(1)}, u32[]{:S(2)}) copy-start(s32[32,1,256]{2,1,0:T(1,128)S(1)} %broadcast_and_fusion) | copy-start | bytes 98308
  23.5 16.2 %copy-start.26 = (s32[128,7,4]{0,2,1:T(4,128)S(1)}, s32[128,7,4]{0,2,1:T(4,128)}, u32[]{:S(2)}) copy-start(s32[128,7,4]{0,2,1:T(4,128)} %param.18) | copy-start | bytes 43012
  23.5 16.8 %copy-start.27 = (s32[256]{0:T(256)S(1)}, s32[256]{0:T(256)}, u32[]{:S(2)}) copy-start(s32[256]{0:T(256)} %param.19) | copy-start | bytes 3076
  23.5 17.6 %copy-start.3 = (bf16[1024,512]{1,0:T(8,128)(2,1)S(1)}, bf16[1024,512]{1,0:T(8,128)(2,1)}, u32[]{:S(2)}) copy-start(bf16[1024,512]{1,0:T(8,128)(2,1)} %hot_ref.1) | copy-start | bytes 3145732
  23.5 17.6 %copy-start.4 = (bf16[512,512]{1,0:T(8,128)(2,1)S(1)}, bf16[512,512]{1,0:T(8,128)(2,1)}, u32[]{:S(2)}) copy-start(bf16[512,512]{1,0:T(8,128)(2,1)} %weight_ref.1) | copy-start | bytes 1572868
  23.5 17.6 %copy-start.5 = (f32[128,256]{1,0:T(8,128)S(1)}, f32[128,256]{1,0:T(8,128)}, u32[]{:S(2)}) copy-start(f32[128,256]{1,0:T(8,128)} %grad_ref.1) | copy-start | bytes 393220
  23.6 17.6 %copy-start.6 = (bf16[128,512]{1,0:T(8,128)(2,1)S(1)}, bf16[128,512]{1,0:T(8,128)(2,1)}, u32[]{:S(2)}) copy-start(bf16[128,512]{1,0:T(8,128)(2,1)} %dense_ref.3) | copy-start | bytes 393220
  23.6 17.6 %copy-start.7 = (s32[128,8,4]{0,2,1:T(4,128)S(1)}, s32[128,8,4]{0,2,1:T(4,128)}, u32[]{:S(2)}) copy-start(s32[128,8,4]{0,2,1:T(4,128)} %param.20) | copy-start | bytes 49156
  34.6 27.2 %all-to-all-start.1 = ((bf16[32,112,128]{2,1,0:T(8,128)(2,1)}), bf16[32,112,128]{2,1,0:T(8,128)(2,1)S(1)}, u32[]{:S(2)}, u32[]{:S(2)}) async-start(bf16[32,112,128]{2,1,0:T(8,128)(2,1)} %shard_map.147), calls=%async_computation.1 | async-start | bytes 1835008 | tf_op jit(solution)/shard_map/all_to_all | solution.py:540
  43.8 1.0 copy-start.15
  44.7 1.0 copy-start.17
  45.7 1.0 copy-start.18
  46.7 0.9 copy-start.19
  47.6 0.7 copy-start.21
  48.3 0.7 copy-start.22
  61.8 1.0 copy-start.24
  76.9 8.1 %collective-permute-start = (bf16[4,1024,128]{2,1,0:T(8,128)(2,1)}, bf16[4,1024,128]{2,1,0:T(8,128)(2,1)S(1)}, u32[]{:S(2)}, u32[]{:S(2)}) collective-permute-start(bf16[4,1024,128]{2,1,0:T(8,128)(2,1)} %get-tuple-element.58), channel_id=1, source_target_pairs={{0,1},{1,0},{2,3},{3,2},{4,5},{5,4},{6,7},{7,6},{8,9},{9,8},{10,11... | collective-permute-start | bytes 3145736 | tf_op jit(solution)/shard_map/ppermute | solution.py:532
  77.2 31.8 %all-to-all-start.2 = ((bf16[32,112,128]{2,1,0:T(8,128)(2,1)}), bf16[32,112,128]{2,1,0:T(8,128)(2,1)S(1)}, u32[]{:S(2)}, u32[]{:S(2)}) async-start(bf16[32,112,128]{2,1,0:T(8,128)(2,1)} %get-tuple-element.56), calls=%async_computation.2 | async-start | bytes 1835008 | tf_op jit(solution)/shard_map/all_to_all | solution.py:540
  86.9 9.5 %collective-permute-start.1 = (bf16[1024,128]{1,0:T(8,128)(2,1)S(1)}, bf16[1024,128]{1,0:T(8,128)(2,1)S(1)}, u32[]{:S(2)}, u32[]{:S(2)}) collective-permute-start(bf16[1024,128]{1,0:T(8,128)(2,1)S(1)} %get-tuple-element.93), channel_id=1, source_target_pairs={{0,2},{1,3},{2,4},{3,5},{4,6},{5,7},{6,0},{7,1},{8,10},{9,11},{10,... | collective-permute-start | bytes 786440 | tf_op jit(solution)/shard_map/ppermute | solution.py:536
  88.5 12.8 %collective-permute-start.3 = (bf16[1024,128]{1,0:T(8,128)(2,1)S(1)}, bf16[1024,128]{1,0:T(8,128)(2,1)S(1)}, u32[]{:S(2)}, u32[]{:S(2)}) collective-permute-start(bf16[1024,128]{1,0:T(8,128)(2,1)S(1)} %get-tuple-element.94), channel_id=1, source_target_pairs={{0,6},{1,7},{2,0},{3,1},{4,2},{5,3},{6,4},{7,5},{8,14},{9,15},{10,... | collective-permute-start | bytes 786440 | tf_op jit(solution)/shard_map/ppermute | solution.py:536
  90.2 12.7 %collective-permute-start.2 = (bf16[1024,128]{1,0:T(8,128)(2,1)S(1)}, bf16[1024,128]{1,0:T(8,128)(2,1)S(1)}, u32[]{:S(2)}, u32[]{:S(2)}) collective-permute-start(bf16[1024,128]{1,0:T(8,128)(2,1)S(1)} %get-tuple-element.95), channel_id=1, source_target_pairs={{0,4},{1,5},{2,6},{3,7},{4,0},{5,1},{6,2},{7,3},{8,12},{9,13},{10,... | collective-permute-start | bytes 786440 | tf_op jit(solution)/shard_map/ppermute | solution.py:536
  109.0 7.5 %copy-start.25 = (bf16[32,112,128]{2,1,0:T(8,128)(2,1)}, bf16[32,112,128]{2,1,0:T(8,128)(2,1)S(1)}, u32[]{:S(2)}) copy-start(bf16[32,112,128]{2,1,0:T(8,128)(2,1)S(1)} %all-to-all-done.2.rows_ref) | copy-start | bytes 2752516
  109.0 28.1 %all-to-all-start.3 = ((bf16[32,32,128]{2,1,0:T(8,128)(2,1)}), bf16[32,32,128]{2,1,0:T(8,128)(2,1)S(1)}, u32[]{:S(2)}, u32[]{:S(2)}) async-start(bf16[32,32,128]{2,1,0:T(8,128)(2,1)} %bitcast.16), calls=%async_computation.3 | async-start | bytes 524288 | tf_op jit(solution)/shard_map/all_to_all | solution.py:540
  137.0 1.0 copy-start.28
  137.0 4.5 %copy-start.11 = (s32[2]{0:T(128)S(1)}, s32[2]{0:T(128)}, u32[]{:S(2)}) copy-start(s32[2]{0:T(128)} %pad_add_fusion.place_ref) | copy-start | bytes 28
  137.1 4.5 %copy-start.13 = (bf16[2,1024,128]{2,1,0:T(8,128)(2,1)S(1)}, bf16[2,1024,128]{2,1,0:T(8,128)(2,1)}, u32[]{:S(2)}) copy-start(bf16[2,1024,128]{2,1,0:T(8,128)(2,1)} %get-tuple-element.60.kept_ref) | copy-start | bytes 1572868
  137.1 15.7 %collective-permute-start.8 = (bf16[2,2,1024,128]{3,2,1,0:T(8,128)(2,1)}, bf16[2,2,1024,128]{3,2,1,0:T(8,128)(2,1)S(1)}, u32[]{:S(2)}, u32[]{:S(2)}) collective-permute-start(bf16[2,2,1024,128]{3,2,1,0:T(8,128)(2,1)} %get-tuple-element.69), channel_id=1, source_target_pairs={{0,1},{1,0},{2,3},{3,2},{4,5},{5,4},{6,7},{7,6},{8,9},{9,8},{10,11... | collective-permute-start | bytes 3145736 | tf_op jit(solution)/shard_map/ppermute | solution.py:532
  137.2 4.4 %collective-permute-start.4 = (bf16[2,1024,128]{2,1,0:T(8,128)(2,1)}, bf16[2,1024,128]{2,1,0:T(8,128)(2,1)S(1)}, u32[]{:S(2)}, u32[]{:S(2)}) collective-permute-start(bf16[2,1024,128]{2,1,0:T(8,128)(2,1)} %get-tuple-element.65), channel_id=1, source_target_pairs={{0,1},{1,0},{2,3},{3,2},{4,5},{5,4},{6,7},{7,6},{8,9},{9,8},{10,11... | collective-permute-start | bytes 1572872 | tf_op jit(solution)/shard_map/ppermute | solution.py:532
  137.7 8.0 %copy-start.16 = (bf16[8,128,512]{2,1,0:T(8,128)(2,1)S(1)}, bf16[8,128,512]{2,1,0:T(8,128)(2,1)}, u32[]{:S(2)}) copy-start(bf16[8,128,512]{2,1,0:T(8,128)(2,1)} %copy-done.15) | copy-start | bytes 3145732
  137.7 8.0 %copy-start.20 = (bf16[7,128,512]{2,1,0:T(8,128)(2,1)S(1)}, bf16[7,128,512]{2,1,0:T(8,128)(2,1)}, u32[]{:S(2)}) copy-start(bf16[7,128,512]{2,1,0:T(8,128)(2,1)} %get-tuple-element.72.cold_ref) | copy-start | bytes 2752516
  137.7 8.0 %copy-start.23 = (bf16[128,512]{1,0:T(8,128)(2,1)S(1)}, bf16[128,512]{1,0:T(8,128)(2,1)}, u32[]{:S(2)}) copy-start(bf16[128,512]{1,0:T(8,128)(2,1)} %copy-done.22) | copy-start | bytes 393220
  137.8 2.1 %collective-permute-start.5 = (bf16[64,128]{1,0:T(8,128)(2,1)S(1)}, bf16[64,128]{1,0:T(8,128)(2,1)S(1)}, u32[]{:S(2)}, u32[]{:S(2)}) collective-permute-start(bf16[64,128]{1,0:T(8,128)(2,1)S(1)} %shard_map.151.mine_ref), channel_id=1, source_target_pairs={{0,1},{1,0},{2,3},{3,2},{4,5},{5,4},{6,7},{7,6},{8,9},{9,8},{10,11... | collective-permute-start | bytes 49160 | tf_op jit(solution)/shard_map/ppermute | solution.py:532
  138.1 10.7 %collective-permute-start.9 = (bf16[2,1024,128]{2,1,0:T(8,128)(2,1)S(1)}, bf16[2,1024,128]{2,1,0:T(8,128)(2,1)S(1)}, u32[]{:S(2)}, u32[]{:S(2)}) collective-permute-start(bf16[2,1024,128]{2,1,0:T(8,128)(2,1)S(1)} %copy-done.28), channel_id=1, source_target_pairs={{0,1},{1,0},{2,3},{3,2},{4,5},{5,4},{6,7},{7,6},{8,9},{9,8},{10,11... | collective-permute-start | bytes 1572872 | tf_op jit(solution)/shard_map/ppermute | solution.py:532
  142.2 10.6 %collective-permute-start.6 = (bf16[1152,128]{1,0:T(8,128)(2,1)S(1)}, bf16[1152,128]{1,0:T(8,128)(2,1)S(1)}, u32[]{:S(2)}, u32[]{:S(2)}) collective-permute-start(bf16[1152,128]{1,0:T(8,128)(2,1)S(1)} %get-tuple-element.86.own_ref), channel_id=1, source_target_pairs={{0,2},{1,3},{2,4},{3,5},{4,6},{5,7},{6,0},{7,1},{8,10},{9,11},{10,... | collective-permute-start | bytes 884744 | tf_op jit(solution)/shard_map/ppermute | solution.py:536
  144.0 8.8 %collective-permute-start.7 = (bf16[1152,128]{1,0:T(8,128)(2,1)S(1)}, bf16[1152,128]{1,0:T(8,128)(2,1)S(1)}, u32[]{:S(2)}, u32[]{:S(2)}) collective-permute-start(bf16[1152,128]{1,0:T(8,128)(2,1)S(1)} %get-tuple-element.68), channel_id=1, source_target_pairs={{0,6},{1,7},{2,0},{3,1},{4,2},{5,3},{6,4},{7,5},{8,14},{9,15},{10,... | collective-permute-start | bytes 884744 | tf_op jit(solution)/shard_map/ppermute | solution.py:536
  145.8 7.0 %copy-start.12 = (bf16[2,2,1024,128]{3,2,1,0:T(8,128)(2,1)S(1)}, bf16[2,2,1024,128]{3,2,1,0:T(8,128)(2,1)}, u32[]{:S(2)}) copy-start(bf16[2,2,1024,128]{3,2,1,0:T(8,128)(2,1)} %get-tuple-element.74.kept_ref) | copy-start | bytes 3145732
  148.8 7.6 %copy-start.14 = (f32[2,1024,128]{2,1,0:T(8,128)S(1)}, f32[2,1024,128]{2,1,0:T(8,128)}, u32[]{:S(2)}) copy-start(f32[2,1024,128]{2,1,0:T(8,128)} %get-tuple-element.82.kept_ref) | copy-start | bytes 3145732
  153.1 15.1 %collective-permute-start.10 = (bf16[2176,128]{1,0:T(8,128)(2,1)S(1)}, bf16[2176,128]{1,0:T(8,128)(2,1)S(1)}, u32[]{:S(2)}, u32[]{:S(2)}) collective-permute-start(bf16[2176,128]{1,0:T(8,128)(2,1)S(1)} %get-tuple-element.84), channel_id=1, source_target_pairs={{0,2},{1,3},{2,4},{3,5},{4,6},{5,7},{6,0},{7,1},{8,10},{9,11},{10,... | collective-permute-start | bytes 1671176 | tf_op jit(solution)/shard_map/ppermute | solution.py:536
  154.6 12.5 %collective-permute-start.11 = (bf16[2048,128]{1,0:T(8,128)(2,1)S(1)}, bf16[2048,128]{1,0:T(8,128)(2,1)S(1)}, u32[]{:S(2)}, u32[]{:S(2)}) collective-permute-start(bf16[2048,128]{1,0:T(8,128)(2,1)S(1)} %get-tuple-element.85), channel_id=1, source_target_pairs={{0,6},{1,7},{2,0},{3,1},{4,2},{5,3},{6,4},{7,5},{8,14},{9,15},{10,... | collective-permute-start | bytes 1572872 | tf_op jit(solution)/shard_map/ppermute | solution.py:536

commit v4 on v3

--- a/solution.py
+++ b/solution.py
@@ -77,10 +77,21 @@
         local = local_ref[j // bag, j % bag : j % bag + 1, :]
         code = (((local >> 11) & 1) << 14) | ((local >> 12) << 11) | (local & 2047)
         high, low = (code >> 8).astype(F32), (code & 255).astype(F32)
-        left.append(jnp.concatenate([hits[j] * high, hits[j] * low], axis=0).astype(BF16))
+        left.append(
+            jnp.concatenate([hits[j] * high, hits[j] * low, hits[j]], axis=0).astype(BF16)
+        )
         right.append(jnp.where(slot + upper * (LANES - pairs) == slot_row, 1.0, 0.0).astype(BF16))
     placed = dot(jnp.concatenate(left, axis=1), jnp.concatenate(right, axis=1), NT)
-    ids = (placed[:tables] * 256.0 + placed[tables:]).astype(jnp.int32)
+    ids = (placed[:tables] * 256.0 + placed[tables : 2 * tables]).astype(jnp.int32)
+    ids = jnp.where(placed[2 * tables :] > 0.5, ids, iota(ids.shape, 0) * 256 + iota(ids.shape, 1))
+    lane = iota(ids.shape, 1)
+    rows = ids & 16383
+    twice = jnp.zeros(ids.shape, F32)
+    for d in range(1, 4):
+        met = (rows == pltpu.roll(rows, d, 1)) & (lane % 4 >= d) & (lane % LANES < pairs)
+        twice = jnp.where(met, 1.0, twice)
+    twice = jnp.max(twice, axis=1, keepdims=True).astype(jnp.int32)
+    ids = jnp.where(lane == pairs, twice, ids)
     for k in range(tables):
         ids_ref[k] = ids[k : k + 1]
 
@@ -228,13 +239,13 @@
         wide[half + k * pairs : half + (k + 1) * pairs, :] = jnp.where(low, r, x)
 
     def fetch(i, carry):
-        base = pl.multiple_of(i * 56, 8)
-        got = [wide[pl.ds(pos_ref[base + u], 1), :] for u in range(56)]
-        for u in range(56):
+        base = pl.multiple_of(i * 128, 8)
+        got = [wide[pl.ds(pos_ref[base + u], 1), :] for u in range(128)]
+        for u in range(128):
             lookups[pl.ds(base + u, 1), :] = got[u]
         return carry
 
-    lax.fori_loop(0, lookups.shape[0] // 56, fetch, 0)
+    lax.fori_loop(0, lookups.shape[0] // 128, fetch, 0)
     band = band_ref[...].astype(F32).T
     side = jnp.where(lane_is_low((batch, LANES)), 0.0, 1.0)
     for f in range(cold_feats):
@@ -317,13 +328,13 @@
             wide[j * share : (j + 1) * share, :] = jnp.zeros((share, LANES), F32)
 
     def place(i, carry):
-        base = pl.multiple_of(i * 56, 8)
-        got = [lookups[pl.ds(base + u, 1), :] for u in range(56)]
-        for u in range(56):
+        base = pl.multiple_of(i * 128, 8)
+        got = [lookups[pl.ds(base + u, 1), :] for u in range(128)]
+        for u in range(128):
             wide[pl.ds(pos_ref[base + u], 1), :] = got[u]
         return carry
 
-    lax.fori_loop(0, lookups.shape[0] // 56, place, 0)
+    lax.fori_loop(0, lookups.shape[0] // 128, place, 0)
     low = lane_is_low((pairs, LANES))
     for k in range(tables):
         a = wide[k * pairs : (k + 1) * pairs, :]
@@ -391,33 +402,46 @@
         up_a, up_b = upper[:pairs, k : k + 1], upper[LANES : LANES + pairs, k : k + 1]
         val_a[at, :] = jnp.where(up_a == side, jnp.where(low, x, r), 0.0)
         val_b[at, :] = jnp.where(up_b == side, jnp.where(low, r, x), 0.0)
-    half = tables // 2
+    sides = ((0, val_a, sums[0]), (LANES, val_b, sums[1]))
     step = pairs // 2
 
-    def one(group, source):
-        first = source * (2 * LANES) + group * step
-        base = pl.multiple_of(source * pairs + group * step, 8)
-        for u in range(step):
-            spots = [
-                ids_ref[first + half * which * 2 * LANES + side * LANES + u]
-                for which in range(2)
-                for side in range(2)
+    def spread(part, source):
+        first = source * (2 * LANES) + part * step
+        base = pl.multiple_of(source * pairs + part * step, 8)
+        for q in range(0, step, 4):
+            work = [
+                (to, ids_ref[first + lane + q + t], val[pl.ds(base + q + t, 1), :])
+                for lane, val, to in sides
+                for t in range(4)
             ]
-            new = [
-                sums[2 * which + side][pl.ds(spots[2 * which + side], 1), :]
-                + val[pl.ds(base + half * which * pairs + u, 1), :]
-                for which in range(2)
-                for side, val in enumerate((val_a, val_b))
-            ]
-            for part, spot, value in zip(sums, spots, new):
-                part[pl.ds(spot, 1), :] = value
+            new = [to[pl.ds(row, 1), :] + value for to, row, value in work]
+            for (to, row, _), value in zip(work, new):
+                to[pl.ds(row, 1), :] = value
         return source
 
+    def one_by_one(group, source):
+        first = source * (2 * LANES) + group * 8
+        base = pl.multiple_of(source * pairs + group * 8, 8)
+        for u in range(8):
+            for lane, val, to in sides:
+                row = ids_ref[first + lane + u]
+                to[pl.ds(row, 1), :] = to[pl.ds(row, 1), :] + val[pl.ds(base + u, 1), :]
+        return source
+
     def per_source(source, carry):
-        lax.fori_loop(0, 2, one, source)
+        twice = ids_ref[source * (2 * LANES) + pairs]
+
+        @pl.when(twice == 0)
+        def _():
+            lax.fori_loop(0, 2, spread, source)
+
+        @pl.when(twice != 0)
+        def _():
+            lax.fori_loop(0, pairs // 8, one_by_one, source)
+
         return carry
 
-    lax.fori_loop(0, half, per_source, 0)
+    lax.fori_loop(0, tables, per_source, 0)
     core = place_ref[1]
     half = kept_own.shape[1]
     size = 2 * half
@@ -676,26 +700,26 @@
             pltpu.VMEM((2, half, LANES), F32),
             pltpu.SemaphoreType.DMA((8,)),
         ]
-        + [pltpu.VMEM((rows_dev // 2, LANES), F32)] * 4,
+        + [pltpu.VMEM((rows_dev // 2, LANES), F32)] * 2,
         specs=[SMEM, SMEM, VMEM, VMEM],
         out_specs=[HBM] * 6,
         us=20,
         vmem=62,
     )(place, row_ids, asked, returned)
-    given_far, given_near, given_own, dense_all = lax.optimization_barrier(
-        (given_far, given_near, given_own, dense_all)
-    )
+    given_far, dense_all = lax.optimization_barrier((given_far, dense_all))
     mine = call(dense_kernel, shape((64, LANES), BF16))(dense_all)
     taken_far = to_other_core(given_far)
     theirs = to_other_core(mine)
+    up, down = call(far_kernel, (shape((half + 128, LANES), BF16),) * 2, specs=[SMEM] + [VMEM] * 4)(
+        place, kept_far, taken_far, mine, theirs
+    )
+    from_below = along_x(up, 1)
+    from_above = along_x(down, -1)
+    up, down, cold_emb, given_near, given_own = lax.optimization_barrier(
+        (up, down, cold_emb, given_near, given_own)
+    )
     taken_near = to_other_core(given_near)
     taken_own = to_other_core(given_own)
-    up, down = call(far_kernel, (shape((half + 128, LANES), BF16),) * 2, specs=[SMEM] + [VMEM] * 4)(
-        place, kept_far, taken_far, mine, theirs
-    )
-    from_below = along_x(up, 1)
-    from_above = along_x(down, -1)
-    up, down, cold_emb = lax.optimization_barrier((up, down, cold_emb))
     inter = call(
         inter_kernel,
         shape((batch, feats * feats), F32),

time: 171 us -> 162 us (0.947)
  Pallas kernels: 55.2 us -> 48.2 us
    pallas_call x1, Pallas kernels: 20.5 us -> 13.6 us  [shards(): call(add_kernel, (shape((2, half, LANES), BF16), shape((2, 2, half, LANES...]
    ppermute x5, waiting for transfers between devices: 3.19 us -> 1.43 us  [to_other_core(): return lax.ppermute(x, 'dp', [(i, i ^ 1) for i in range(8)])]
    unnamed x59 -> x61, local copies, waits for them, and re-layouts: 7.83 us -> 7.72 us
  transfers between devices with their start and end apart: 15 -> 15, of which waited for: 10 -> 10; matrix products, arithmetic and copies ran while one was open for 2% -> 3% of each run, Pallas kernels for 16% -> 12%
where the time goes in v4:
time: 162 us; the launch traced here: 161 us
  Pallas kernels  48.2 us (30%)
  waiting for transfers between devices  46.2 us (29%)
  starting transfers between devices  33.4 us (21%)
  blocking collectives  20.3 us (13%)
  local copies, waits for them, and re-layouts  8.51 us (5%)
  other arithmetic  3.29 us (2%)
    ppermute x7, waiting for transfers between devices, along_x(): return lax.ppermute(x, 'dp', [(i, (i + 2 * steps) % 8) for i in range(8)])  26.6 us
    all_to_all x3, starting transfers between devices, exchange(): return lax.all_to_all(x, axis, split_axis=0, concat_axis=0, tiled=True)  20.4 us
    all_to_all x1, blocking collectives, exchange(): return lax.all_to_all(x, axis, split_axis=0, concat_axis=0, tiled=True)  20.3 us
    all_to_all x3, waiting for transfers between devices, exchange(): return lax.all_to_all(x, axis, split_axis=0, concat_axis=0, tiled=True)  18.2 us
    pallas_call x1, Pallas kernels, shards(): call(main_kernel, (shape((tables, pairs, LANES), BF16), shape((cold_feats...  13.9 us
    pallas_call x1, Pallas kernels, shards(): call(add_kernel, (shape((2, half, LANES), BF16), shape((2, 2, half, LANES...  13.6 us
    ppermute x7, starting transfers between devices, along_x(): return lax.ppermute(x, 'dp', [(i, (i + 2 * steps) % 8) for i in range(8)])  11.7 us
    pallas_call x1, Pallas kernels, shards(): call(gather_kernel, shape((tables, pairs, LANES), BF16), scratch=[pltpu.V...  11 us
  transfers between devices with their start and end apart: 15, of which 10 were waited for; matrix products, arithmetic and copies ran while one was open for 3% of the time, Pallas kernels for 12%

profile of v4, /device:TPU:8, one launch (start us, length us, event | category | flops | bytes accessed | tf_op | source)
XLA Modules:
  0.0 161.0 jit_solution(9890383901613136661)
XLA Ops:
  0.6 0.7 copy-done.8
  1.3 0.7 copy-done.9
  2.1 1.2 shard_map.146
  3.3 0.0 copy-start.10
  3.3 20.3 %all_to_all.20 = s32[32,1,256]{2,1,0:T(1,128)S(1)} all-to-all(s32[32,1,256]{2,1,0:T(1,128)S(1)} %get-tuple-element.48), channel_id=1, replica_groups=mesh['table'=32,'dp'=8] {'table'}, dimensions={0} | all-to-all | bytes 65536 | tf_op jit(solution)/shard_map/all_to_all | solution.py:564
  23.6 0.0 copy-start.1
  23.7 0.0 copy-start.26
  23.7 0.0 copy-start.27
  23.7 0.0 copy-start.3
  23.7 0.0 copy-start.4
  23.7 0.0 copy-start.5
  23.7 0.0 copy-start.6
  23.8 0.0 copy-start.7
  23.8 11.0 %shard_map.147 = bf16[32,112,128]{2,1,0:T(8,128)(2,1)} custom-call(s32[8192]{0:T(1024)S(1)} %bitcast.36, s32[32,256]{1,0:T(8,128)S(1)} %bitcast.34, bf16[64,32768]{1,0:T(8,128)(2,1)S(1)} %bitcast.38), custom_call_target="tpu_custom_call" | custom-call | flops 13200000000 | bytes 1048576 | tf_op jit(solution)/shard_map/pallas_call | solution.py:605
  34.8 5.1 %all-to-all-start.1 = ((bf16[32,112,128]{2,1,0:T(8,128)(2,1)}), bf16[32,112,128]{2,1,0:T(8,128)(2,1)S(1)}, u32[]{:S(2)}, u32[]{:S(2)}) async-start(bf16[32,112,128]{2,1,0:T(8,128)(2,1)} %shard_map.147), calls=%async_computation.1 | async-start | bytes 1835008 | tf_op jit(solution)/shard_map/all_to_all | solution.py:564
  39.9 0.6 reshape.38.band_ref
  40.5 0.1 copy.19.unique_ref
  40.7 0.6 pad_add_fusion.place_ref
  41.3 2.6 %shard_map.148 = (f32[128,512]{1,0:T(8,128)S(1)}, bf16[128,512]{1,0:T(8,128)(2,1)S(1)}, bf16[8,128,512]{2,1,0:T(8,128)(2,1)S(1)}, bf16[256,1024]{1,0:T(8,128)(2,...) custom-call(bf16[128,512]{1,0:T(8,128)(2,1)S(1)} %copy-done.6, ...), custom_call_target="tpu_custom_call" | custom-call | flops 3300000000 | bytes 1048576 | tf_op jit(solution)/shard_map/pallas_call | solution.py:615
  43.9 0.0 copy-start.15
  43.9 1.0 copy-done.15
  44.8 1.0 copy-done.17
  45.8 1.0 copy-done.18
  46.8 0.9 copy-done.19
  47.7 0.7 copy-done.21
  48.4 0.7 copy-done.22
  49.0 13.0 %all-to-all-done.1.rows_ref = bf16[32,112,128]{2,1,0:T(8,128)(2,1)S(1)} async-done(((bf16[32,112,128]{2,1,0:T(8,128)(2,1)}), bf16[32,112,128]{2,1,0:T(8,128)(2,1)S(1)}, u32[]{:S(2)}, u32[]{:S(2)}) %all-to-all-start.1) | async-done | bytes 917536 | tf_op jit(solution)/shard_map/all_to_all | solution.py:564
  62.0 1.0 copy-done.24
  63.0 13.9 %shard_map.149 = (bf16[32,112,128]{2,1,0:T(8,128)(2,1)}, bf16[7,128,512]{2,1,0:T(8,128)(2,1)}, f32[4,1024,128]{2,1,0:T(8,128)}, bf16[4,1024,128]{2,1,0:T(8,128)(2,1)}) custom-call(s32[2]{0:T(128)} %pad_add_fusion.place_ref, s32[3584]{0:T(1024)} %bitcast.42, bf16[32,112,128]{2,1,0:T(8,128)(2,1)} %copy-done.24, s32[28,128]{1,0:T(8,128)} %reshape.38.band_ref, ...), custom_call_target="tpu_custom_call" | custom-call | flops 15399999488 | bytes 1048576 | tf_op jit(solution)/shard_map/pallas_call | solution.py:635
  76.9 0.1 collective-permute-start
  77.0 7.7 %all-to-all-start.2 = ((bf16[32,112,128]{2,1,0:T(8,128)(2,1)}), bf16[32,112,128]{2,1,0:T(8,128)(2,1)S(1)}, u32[]{:S(2)}, u32[]{:S(2)}) async-start(bf16[32,112,128]{2,1,0:T(8,128)(2,1)} %get-tuple-element.56), calls=%async_computation.2 | async-start | bytes 1835008 | tf_op jit(solution)/shard_map/all_to_all | solution.py:564
  84.7 1.9 %fusion.4 = (bf16[4,1024,128]{2,1,0:T(8,128)(2,1)S(1)}, f32[4,1024,128]{2,1,0:T(8,128)S(1)}) fusion(f32[4,1024,128]{2,1,0:T(8,128)} %get-tuple-element.57, bf16[4,1024,128]{2,1,0:T(8,128)(2,1)S(1)} %collective-permute-done), kind=kLoop, calls=%fused_computation.12 | loop fusion | flops 1572864 | bytes 6291456 | tf_op jit(solution)/shard_map/convert
  86.6 0.1 slice_bitcast_fusion.3
  86.7 1.6 collective-permute-start.1
  88.2 1.7 %collective-permute-start.3 = (bf16[1024,128]{1,0:T(8,128)(2,1)S(1)}, bf16[1024,128]{1,0:T(8,128)(2,1)S(1)}, u32[]{:S(2)}, u32[]{:S(2)}) collective-permute-start(bf16[1024,128]{1,0:T(8,128)(2,1)S(1)} %get-tuple-element.94), channel_id=1, source_target_pairs={{0,6},{1,7},{2,0},{3,1},{4,2},{5,3},{6,4},{7,5},{8,14},{9,15},{10,... | collective-permute-start | bytes 786440 | tf_op jit(solution)/shard_map/ppermute | solution.py:560
  90.0 1.8 %collective-permute-start.2 = (bf16[1024,128]{1,0:T(8,128)(2,1)S(1)}, bf16[1024,128]{1,0:T(8,128)(2,1)S(1)}, u32[]{:S(2)}, u32[]{:S(2)}) collective-permute-start(bf16[1024,128]{1,0:T(8,128)(2,1)S(1)} %get-tuple-element.95), channel_id=1, source_target_pairs={{0,4},{1,5},{2,6},{3,7},{4,0},{5,1},{6,2},{7,3},{8,12},{9,13},{10,... | collective-permute-start | bytes 786440 | tf_op jit(solution)/shard_map/ppermute | solution.py:560
  91.8 4.4 %collective-permute-done.1 = bf16[1024,128]{1,0:T(8,128)(2,1)S(1)} collective-permute-done((bf16[1024,128]{1,0:T(8,128)(2,1)S(1)}, bf16[1024,128]{1,0:T(8,128)(2,1)S(1)}, u32[]{:S(2)}, u32[]{:S(2)}) %collective-permute-start.1) | collective-permute-done | bytes 262176 | tf_op jit(solution)/shard_map/ppermute | solution.py:560
  96.2 4.8 %collective-permute-done.3 = bf16[1024,128]{1,0:T(8,128)(2,1)S(1)} collective-permute-done((bf16[1024,128]{1,0:T(8,128)(2,1)S(1)}, bf16[1024,128]{1,0:T(8,128)(2,1)S(1)}, u32[]{:S(2)}, u32[]{:S(2)}) %collective-permute-start.3) | collective-permute-done | bytes 262176 | tf_op jit(solution)/shard_map/ppermute | solution.py:560
  101.0 1.7 %collective-permute-done.2 = bf16[1024,128]{1,0:T(8,128)(2,1)S(1)} collective-permute-done((bf16[1024,128]{1,0:T(8,128)(2,1)S(1)}, bf16[1024,128]{1,0:T(8,128)(2,1)S(1)}, u32[]{:S(2)}, u32[]{:S(2)}) %collective-permute-start.2) | collective-permute-done | bytes 262176 | tf_op jit(solution)/shard_map/ppermute | solution.py:560
  102.7 0.8 fusion.3
  103.5 5.2 %all-to-all-done.2.rows_ref = bf16[32,112,128]{2,1,0:T(8,128)(2,1)S(1)} async-done(((bf16[32,112,128]{2,1,0:T(8,128)(2,1)}), bf16[32,112,128]{2,1,0:T(8,128)(2,1)S(1)}, u32[]{:S(2)}, u32[]{:S(2)}) %all-to-all-start.2) | async-done | bytes 917536 | tf_op jit(solution)/shard_map/all_to_all | solution.py:564
  108.7 7.5 %all-to-all-start.3 = ((bf16[32,32,128]{2,1,0:T(8,128)(2,1)}), bf16[32,32,128]{2,1,0:T(8,128)(2,1)S(1)}, u32[]{:S(2)}, u32[]{:S(2)}) async-start(bf16[32,32,128]{2,1,0:T(8,128)(2,1)} %bitcast.16), calls=%async_computation.3 | async-start | bytes 524288 | tf_op jit(solution)/shard_map/all_to_all | solution.py:564
  116.3 13.6 %shard_map.150 = (bf16[2,1024,128]{2,1,0:T(8,128)(2,1)}, bf16[2,2,1024,128]{3,2,1,0:T(8,128)(2,1)}, bf16[2,1024,128]{2,1,0:T(8,128)(2,1)}, bf16[2,1024,128]{2,1,...) custom-call(s32[2]{0:T(128)} %pad_add_fusion.place_ref, s32[8192]{0:T(1024)} %bitcast.37, ...), custom_call_target="tpu_custom_call" | custom-call | flops 22000001024 | bytes 1048576 | tf_op jit(solution)/shard_map/pallas_call | solution.py:686
  129.9 0.1 collective-permute-start.4
  130.1 0.0 copy-start.16
  130.1 0.0 copy-start.23
  130.1 0.6 collective-permute-start.5
  130.7 1.2 collective-permute-done.5.theirs_ref
  131.9 0.2 collective-permute-done.4.taken_ref
  132.1 0.7 shard_map.152
  132.8 0.2 collective-permute-start.8
  133.0 0.4 collective-permute-start.9
  133.4 1.5 collective-permute-start.6
  134.9 1.7 %collective-permute-start.7 = (bf16[1152,128]{1,0:T(8,128)(2,1)S(1)}, bf16[1152,128]{1,0:T(8,128)(2,1)S(1)}, u32[]{:S(2)}, u32[]{:S(2)}) collective-permute-start(bf16[1152,128]{1,0:T(8,128)(2,1)S(1)} %get-tuple-element.66), channel_id=1, source_target_pairs={{0,6},{1,7},{2,0},{3,1},{4,2},{5,3},{6,4},{7,5},{8,14},{9,15},{10,... | collective-permute-start | bytes 884744 | tf_op jit(solution)/shard_map/ppermute | solution.py:560
  136.7 3.0 %shard_map.153 = f32[128,256]{1,0:T(8,128)} custom-call(bf16[128,512]{1,0:T(8,128)(2,1)S(1)} %copy-done.23, bf16[7,128,512]{2,1,0:T(8,128)(2,1)S(1)} %copy-done.20, bf16[8,128,512]{2,1,0:T(8,128)(2,1)S(1)} %copy-done.16), custom_call_target="tpu_custom_call" | custom-call | flops 4400000000 | bytes 1048576 | tf_op jit(solution)/shard_map/pallas_call | solution.py:723
  139.7 4.0 %collective-permute-done.6.below_ref.before_ref = bf16[1152,128]{1,0:T(8,128)(2,1)S(1)} collective-permute-done((bf16[1152,128]{1,0:T(8,128)(2,1)S(1)}, bf16[1152,128]{1,0:T(8,128)(2,1)S(1)}, u32[]{:S(2)}, u32[]{:S(2)}) %collective-permute-start.6) | collective-permute-done | bytes 294944 | tf_op jit(solution)/shard_map/ppermute | solution.py:560
  143.7 0.0 collective-permute-done.7.above_ref.next_ref
  143.7 0.3 shard_map.154
  144.0 1.8 %collective-permute-start.10 = (bf16[2176,128]{1,0:T(8,128)(2,1)S(1)}, bf16[2176,128]{1,0:T(8,128)(2,1)S(1)}, u32[]{:S(2)}, u32[]{:S(2)}) collective-permute-start(bf16[2176,128]{1,0:T(8,128)(2,1)S(1)} %get-tuple-element.84), channel_id=1, source_target_pairs={{0,2},{1,3},{2,4},{3,5},{4,6},{5,7},{6,0},{7,1},{8,10},{9,11},{10,... | collective-permute-start | bytes 1671176 | tf_op jit(solution)/shard_map/ppermute | solution.py:560
  145.9 1.5 collective-permute-start.11
  147.4 0.1 shard_map.155.pair_ref
  147.5 10.9 %collective-permute-done.11.above_ref = bf16[2048,128]{1,0:T(8,128)(2,1)S(1)} collective-permute-done((bf16[2048,128]{1,0:T(8,128)(2,1)S(1)}, bf16[2048,128]{1,0:T(8,128)(2,1)S(1)}, u32[]{:S(2)}, u32[]{:S(2)}) %collective-permute-start.11) | collective-permute-done | bytes 524320 | tf_op jit(solution)/shard_map/ppermute | solution.py:560
  158.4 0.7 collective-permute-done.10.below_ref
  159.1 1.9 %shard_map.156 = (f32[64,4096]{1,0:T(8,128)}, f32[32,512]{1,0:T(8,128)}, f32[8,512]{1,0:T(8,128)}, f32[16,512]{1,0:T(8,128)}) custom-call(s32[2]{0:T(128)S(1)} %copy-done.11, f32[2,1024,128]{2,1,0:T(8,128)S(1)} %shard_map.155.pair_ref, bf16[2176,128]{1,0:T(8,128)(2,1)S(1)} %collective-permute-done.10.below_ref, ...), custom_call_target="tpu_custom_call" | custom-call | flops 2200000000 | bytes 1048576 | tf_op jit(solution)/shard_map/pallas_call | solution.py:745
  (46 shorter events, 0.2 us)
Async XLA Ops:
  0.6 0.7 copy-start.8
  1.3 0.7 copy-start.9
  2.1 21.6 %copy-start.2 = (bf16[32768,64]{0,1:T(8,128)(2,1)S(1)}, bf16[32768,64]{0,1:T(8,128)(2,1)}, u32[]{:S(2)}) copy-start(bf16[32768,64]{0,1:T(8,128)(2,1)} %param.13) | copy-start | bytes 12582916
  3.3 20.4 %copy-start.10 = (s32[28,128]{1,0:T(8,128)}, s32[28,128]{1,0:T(8,128)S(1)}, u32[]{:S(2)}) copy-start(s32[28,128]{1,0:T(8,128)S(1)} %get-tuple-element.49) | copy-start | bytes 43012
  23.6 11.2 %copy-start = (s32[32,1,256]{2,0,1:T(8,128)}, s32[32,1,256]{2,0,1:T(8,128)S(1)}, u32[]{:S(2)}) copy-start(s32[32,1,256]{2,0,1:T(8,128)S(1)} %copy.22) | copy-start | bytes 98308
  23.6 11.1 %copy-start.1 = (s32[32,1,256]{2,1,0:T(1,128)}, s32[32,1,256]{2,1,0:T(1,128)S(1)}, u32[]{:S(2)}) copy-start(s32[32,1,256]{2,1,0:T(1,128)S(1)} %broadcast_and_fusion) | copy-start | bytes 98308
  23.7 16.2 %copy-start.26 = (s32[128,7,4]{0,2,1:T(4,128)S(1)}, s32[128,7,4]{0,2,1:T(4,128)}, u32[]{:S(2)}) copy-start(s32[128,7,4]{0,2,1:T(4,128)} %param.18) | copy-start | bytes 43012
  23.7 16.8 %copy-start.27 = (s32[256]{0:T(256)S(1)}, s32[256]{0:T(256)}, u32[]{:S(2)}) copy-start(s32[256]{0:T(256)} %param.19) | copy-start | bytes 3076
  23.7 17.5 %copy-start.3 = (bf16[1024,512]{1,0:T(8,128)(2,1)S(1)}, bf16[1024,512]{1,0:T(8,128)(2,1)}, u32[]{:S(2)}) copy-start(bf16[1024,512]{1,0:T(8,128)(2,1)} %hot_ref.1) | copy-start | bytes 3145732
  23.7 17.5 %copy-start.4 = (bf16[512,512]{1,0:T(8,128)(2,1)S(1)}, bf16[512,512]{1,0:T(8,128)(2,1)}, u32[]{:S(2)}) copy-start(bf16[512,512]{1,0:T(8,128)(2,1)} %weight_ref.1) | copy-start | bytes 1572868
  23.7 17.5 %copy-start.5 = (f32[128,256]{1,0:T(8,128)S(1)}, f32[128,256]{1,0:T(8,128)}, u32[]{:S(2)}) copy-start(f32[128,256]{1,0:T(8,128)} %grad_ref.1) | copy-start | bytes 393220
  23.7 17.5 %copy-start.6 = (bf16[128,512]{1,0:T(8,128)(2,1)S(1)}, bf16[128,512]{1,0:T(8,128)(2,1)}, u32[]{:S(2)}) copy-start(bf16[128,512]{1,0:T(8,128)(2,1)} %dense_ref.3) | copy-start | bytes 393220
  23.8 17.5 %copy-start.7 = (s32[128,8,4]{0,2,1:T(4,128)S(1)}, s32[128,8,4]{0,2,1:T(4,128)}, u32[]{:S(2)}) copy-start(s32[128,8,4]{0,2,1:T(4,128)} %param.20) | copy-start | bytes 49156
  34.8 27.2 %all-to-all-start.1 = ((bf16[32,112,128]{2,1,0:T(8,128)(2,1)}), bf16[32,112,128]{2,1,0:T(8,128)(2,1)S(1)}, u32[]{:S(2)}, u32[]{:S(2)}) async-start(bf16[32,112,128]{2,1,0:T(8,128)(2,1)} %shard_map.147), calls=%async_computation.1 | async-start | bytes 1835008 | tf_op jit(solution)/shard_map/all_to_all | solution.py:564
  43.9 1.0 copy-start.15
  44.8 1.0 copy-start.17
  45.8 1.0 copy-start.18
  46.8 0.9 copy-start.19
  47.7 0.7 copy-start.21
  48.4 0.7 copy-start.22
  62.0 1.0 copy-start.24
  76.9 7.8 %collective-permute-start = (bf16[4,1024,128]{2,1,0:T(8,128)(2,1)}, bf16[4,1024,128]{2,1,0:T(8,128)(2,1)S(1)}, u32[]{:S(2)}, u32[]{:S(2)}) collective-permute-start(bf16[4,1024,128]{2,1,0:T(8,128)(2,1)} %get-tuple-element.58), channel_id=1, source_target_pairs={{0,1},{1,0},{2,3},{3,2},{4,5},{5,4},{6,7},{7,6},{8,9},{9,8},{10,11... | collective-permute-start | bytes 3145736 | tf_op jit(solution)/shard_map/ppermute | solution.py:556
  77.0 31.7 %all-to-all-start.2 = ((bf16[32,112,128]{2,1,0:T(8,128)(2,1)}), bf16[32,112,128]{2,1,0:T(8,128)(2,1)S(1)}, u32[]{:S(2)}, u32[]{:S(2)}) async-start(bf16[32,112,128]{2,1,0:T(8,128)(2,1)} %get-tuple-element.56), calls=%async_computation.2 | async-start | bytes 1835008 | tf_op jit(solution)/shard_map/all_to_all | solution.py:564
  86.7 9.5 %collective-permute-start.1 = (bf16[1024,128]{1,0:T(8,128)(2,1)S(1)}, bf16[1024,128]{1,0:T(8,128)(2,1)S(1)}, u32[]{:S(2)}, u32[]{:S(2)}) collective-permute-start(bf16[1024,128]{1,0:T(8,128)(2,1)S(1)} %get-tuple-element.93), channel_id=1, source_target_pairs={{0,2},{1,3},{2,4},{3,5},{4,6},{5,7},{6,0},{7,1},{8,10},{9,11},{10,... | collective-permute-start | bytes 786440 | tf_op jit(solution)/shard_map/ppermute | solution.py:560
  88.2 12.8 %collective-permute-start.3 = (bf16[1024,128]{1,0:T(8,128)(2,1)S(1)}, bf16[1024,128]{1,0:T(8,128)(2,1)S(1)}, u32[]{:S(2)}, u32[]{:S(2)}) collective-permute-start(bf16[1024,128]{1,0:T(8,128)(2,1)S(1)} %get-tuple-element.94), channel_id=1, source_target_pairs={{0,6},{1,7},{2,0},{3,1},{4,2},{5,3},{6,4},{7,5},{8,14},{9,15},{10,... | collective-permute-start | bytes 786440 | tf_op jit(solution)/shard_map/ppermute | solution.py:560
  90.0 12.7 %collective-permute-start.2 = (bf16[1024,128]{1,0:T(8,128)(2,1)S(1)}, bf16[1024,128]{1,0:T(8,128)(2,1)S(1)}, u32[]{:S(2)}, u32[]{:S(2)}) collective-permute-start(bf16[1024,128]{1,0:T(8,128)(2,1)S(1)} %get-tuple-element.95), channel_id=1, source_target_pairs={{0,4},{1,5},{2,6},{3,7},{4,0},{5,1},{6,2},{7,3},{8,12},{9,13},{10,... | collective-permute-start | bytes 786440 | tf_op jit(solution)/shard_map/ppermute | solution.py:560
  108.7 7.6 %copy-start.25 = (bf16[32,112,128]{2,1,0:T(8,128)(2,1)}, bf16[32,112,128]{2,1,0:T(8,128)(2,1)S(1)}, u32[]{:S(2)}) copy-start(bf16[32,112,128]{2,1,0:T(8,128)(2,1)S(1)} %all-to-all-done.2.rows_ref) | copy-start | bytes 2752516
  108.7 21.1 %all-to-all-start.3 = ((bf16[32,32,128]{2,1,0:T(8,128)(2,1)}), bf16[32,32,128]{2,1,0:T(8,128)(2,1)S(1)}, u32[]{:S(2)}, u32[]{:S(2)}) async-start(bf16[32,32,128]{2,1,0:T(8,128)(2,1)} %bitcast.16), calls=%async_computation.3 | async-start | bytes 524288 | tf_op jit(solution)/shard_map/all_to_all | solution.py:564
  129.9 2.2 %copy-start.11 = (s32[2]{0:T(128)S(1)}, s32[2]{0:T(128)}, u32[]{:S(2)}) copy-start(s32[2]{0:T(128)} %pad_add_fusion.place_ref) | copy-start | bytes 28
  129.9 2.2 %copy-start.13 = (bf16[2,1024,128]{2,1,0:T(8,128)(2,1)S(1)}, bf16[2,1024,128]{2,1,0:T(8,128)(2,1)}, u32[]{:S(2)}) copy-start(bf16[2,1024,128]{2,1,0:T(8,128)(2,1)} %get-tuple-element.60.kept_ref) | copy-start | bytes 1572868
  129.9 2.2 %collective-permute-start.4 = (bf16[2,1024,128]{2,1,0:T(8,128)(2,1)}, bf16[2,1024,128]{2,1,0:T(8,128)(2,1)S(1)}, u32[]{:S(2)}, u32[]{:S(2)}) collective-permute-start(bf16[2,1024,128]{2,1,0:T(8,128)(2,1)} %get-tuple-element.63), channel_id=1, source_target_pairs={{0,1},{1,0},{2,3},{3,2},{4,5},{5,4},{6,7},{7,6},{8,9},{9,8},{10,11... | collective-permute-start | bytes 1572872 | tf_op jit(solution)/shard_map/ppermute | solution.py:556
  130.1 2.7 %copy-start.28 = (bf16[2,2,1024,128]{3,2,1,0:T(8,128)(2,1)S(1)}, bf16[2,2,1024,128]{3,2,1,0:T(8,128)(2,1)}, u32[]{:S(2)}) copy-start(bf16[2,2,1024,128]{3,2,1,0:T(8,128)(2,1)} %get-tuple-element.70) | copy-start | bytes 3145732
  130.1 3.0 %copy-start.29 = (bf16[2,1024,128]{2,1,0:T(8,128)(2,1)S(1)}, bf16[2,1024,128]{2,1,0:T(8,128)(2,1)}, u32[]{:S(2)}) copy-start(bf16[2,1024,128]{2,1,0:T(8,128)(2,1)} %get-tuple-element.71) | copy-start | bytes 1572868
  130.1 6.6 %copy-start.16 = (bf16[8,128,512]{2,1,0:T(8,128)(2,1)S(1)}, bf16[8,128,512]{2,1,0:T(8,128)(2,1)}, u32[]{:S(2)}) copy-start(bf16[8,128,512]{2,1,0:T(8,128)(2,1)} %copy-done.15) | copy-start | bytes 3145732
  130.1 6.6 %copy-start.20 = (bf16[7,128,512]{2,1,0:T(8,128)(2,1)S(1)}, bf16[7,128,512]{2,1,0:T(8,128)(2,1)}, u32[]{:S(2)}) copy-start(bf16[7,128,512]{2,1,0:T(8,128)(2,1)} %get-tuple-element.72.cold_ref) | copy-start | bytes 2752516
  130.1 6.6 %copy-start.23 = (bf16[128,512]{1,0:T(8,128)(2,1)S(1)}, bf16[128,512]{1,0:T(8,128)(2,1)}, u32[]{:S(2)}) copy-start(bf16[128,512]{1,0:T(8,128)(2,1)} %copy-done.22) | copy-start | bytes 393220
  130.1 1.8 %collective-permute-start.5 = (bf16[64,128]{1,0:T(8,128)(2,1)S(1)}, bf16[64,128]{1,0:T(8,128)(2,1)S(1)}, u32[]{:S(2)}, u32[]{:S(2)}) collective-permute-start(bf16[64,128]{1,0:T(8,128)(2,1)S(1)} %shard_map.151.mine_ref), channel_id=1, source_target_pairs={{0,1},{1,0},{2,3},{3,2},{4,5},{5,4},{6,7},{7,6},{8,9},{9,8},{10,11... | collective-permute-start | bytes 49160 | tf_op jit(solution)/shard_map/ppermute | solution.py:556
  132.8 10.9 %copy-start.12 = (bf16[2,2,1024,128]{3,2,1,0:T(8,128)(2,1)S(1)}, bf16[2,2,1024,128]{3,2,1,0:T(8,128)(2,1)}, u32[]{:S(2)}) copy-start(bf16[2,2,1024,128]{3,2,1,0:T(8,128)(2,1)} %get-tuple-element.74.kept_ref) | copy-start | bytes 3145732
  132.8 10.9 %collective-permute-start.8 = (bf16[2,2,1024,128]{3,2,1,0:T(8,128)(2,1)S(1)}, bf16[2,2,1024,128]{3,2,1,0:T(8,128)(2,1)S(1)}, u32[]{:S(2)}, u32[]{:S(2)}) collective-permute-start(bf16[2,2,1024,128]{3,2,1,0:T(8,128)(2,1)S(1)} %copy-done.28), channel_id=1, source_target_pairs={{0,1},{1,0},{2,3},{3,2},{4,5},{5,4},{6,7},{7,6},{8,9},{9,8},{10,11... | collective-permute-start | bytes 3145736 | tf_op jit(solution)/shard_map/ppermute | solution.py:556
  133.0 10.7 %collective-permute-start.9 = (bf16[2,1024,128]{2,1,0:T(8,128)(2,1)S(1)}, bf16[2,1024,128]{2,1,0:T(8,128)(2,1)S(1)}, u32[]{:S(2)}, u32[]{:S(2)}) collective-permute-start(bf16[2,1024,128]{2,1,0:T(8,128)(2,1)S(1)} %copy-done.29), channel_id=1, source_target_pairs={{0,1},{1,0},{2,3},{3,2},{4,5},{5,4},{6,7},{7,6},{8,9},{9,8},{10,11... | collective-permute-start | bytes 1572872 | tf_op jit(solution)/shard_map/ppermute | solution.py:556
  133.4 10.3 %collective-permute-start.6 = (bf16[1152,128]{1,0:T(8,128)(2,1)S(1)}, bf16[1152,128]{1,0:T(8,128)(2,1)S(1)}, u32[]{:S(2)}, u32[]{:S(2)}) collective-permute-start(bf16[1152,128]{1,0:T(8,128)(2,1)S(1)} %get-tuple-element.86.own_ref), channel_id=1, source_target_pairs={{0,2},{1,3},{2,4},{3,5},{4,6},{5,7},{6,0},{7,1},{8,10},{9,11},{10,... | collective-permute-start | bytes 884744 | tf_op jit(solution)/shard_map/ppermute | solution.py:560
  134.9 8.8 %collective-permute-start.7 = (bf16[1152,128]{1,0:T(8,128)(2,1)S(1)}, bf16[1152,128]{1,0:T(8,128)(2,1)S(1)}, u32[]{:S(2)}, u32[]{:S(2)}) collective-permute-start(bf16[1152,128]{1,0:T(8,128)(2,1)S(1)} %get-tuple-element.66), channel_id=1, source_target_pairs={{0,6},{1,7},{2,0},{3,1},{4,2},{5,3},{6,4},{7,5},{8,14},{9,15},{10,... | collective-permute-start | bytes 884744 | tf_op jit(solution)/shard_map/ppermute | solution.py:560
  139.7 7.7 %copy-start.14 = (f32[2,1024,128]{2,1,0:T(8,128)S(1)}, f32[2,1024,128]{2,1,0:T(8,128)}, u32[]{:S(2)}) copy-start(f32[2,1024,128]{2,1,0:T(8,128)} %get-tuple-element.82.kept_ref) | copy-start | bytes 3145732
  144.0 15.1 %collective-permute-start.10 = (bf16[2176,128]{1,0:T(8,128)(2,1)S(1)}, bf16[2176,128]{1,0:T(8,128)(2,1)S(1)}, u32[]{:S(2)}, u32[]{:S(2)}) collective-permute-start(bf16[2176,128]{1,0:T(8,128)(2,1)S(1)} %get-tuple-element.84), channel_id=1, source_target_pairs={{0,2},{1,3},{2,4},{3,5},{4,6},{5,7},{6,0},{7,1},{8,10},{9,11},{10,... | collective-permute-start | bytes 1671176 | tf_op jit(solution)/shard_map/ppermute | solution.py:560
  145.9 12.5 %collective-permute-start.11 = (bf16[2048,128]{1,0:T(8,128)(2,1)S(1)}, bf16[2048,128]{1,0:T(8,128)(2,1)S(1)}, u32[]{:S(2)}, u32[]{:S(2)}) collective-permute-start(bf16[2048,128]{1,0:T(8,128)(2,1)S(1)} %get-tuple-element.85), channel_id=1, source_target_pairs={{0,6},{1,7},{2,0},{3,1},{4,2},{5,3},{6,4},{7,5},{8,14},{9,15},{10,... | collective-permute-start | bytes 1572872 | tf_op jit(solution)/shard_map/ppermute | solution.py:560

commit v5 on v4

--- a/solution.py
+++ b/solution.py
@@ -142,12 +142,13 @@
     weight_ref,
     hot_ref,
     unique_ref,
+    line_ref,
     map_ref,
     grad_ref,
     pre_ref,
     bottom_ref,
     emb_ref,
-    counts_ref,
+    extra_ref,
     high_ref,
     low_ref,
 ):
@@ -165,8 +166,13 @@
         count = jnp.zeros((unique, batch), F32)
         for l in range(bag):
             count += jnp.where(map_ref[h, l : l + 1, :] == place, 1.0, 0.0)
-        counts_ref[:, h * batch : (h + 1) * batch] = count.astype(BF16)
+        at = slice(h % 4 * batch, (h % 4 + 1) * batch)
+        extra_ref[h // 4 * 2, :, at] = count[:batch].astype(BF16)
+        extra_ref[h // 4 * 2 + 1, :, at] = count[batch:].astype(BF16)
         emb_ref[h] = dot(count.T.astype(BF16), rows).astype(BF16)
+    line = line_ref[...]
+    line = jnp.concatenate([line >> 5, line & 31], axis=1).astype(F32)
+    extra_ref[4] = jnp.broadcast_to(line, extra_ref.shape[1:]).astype(BF16)
     grad = grad_ref[...]
     grad_high, grad_low = split_two(grad)
     square = feats * feats
@@ -195,16 +201,15 @@
     proj_ref,
     pre_ref,
     dense_ref,
-    counts_ref,
-    unique_ref,
+    extra_ref,
     bottom_ref,
     hot_ref,
     high_ref,
     low_ref,
     slots_ref,
     cold_ref,
-    kept_ref,
-    given_ref,
+    keep_ref,
+    give_ref,
     wide,
     lookups,
     stack,
@@ -212,9 +217,10 @@
     low_part,
     d_stack,
     bags,
-    parts,
-    kept,
-    given,
+    pre,
+    d_pre,
+    dense,
+    extra,
     sems,
 ):
     tables, pairs, _ = rows_ref.shape
@@ -228,6 +234,9 @@
         pltpu.make_async_copy(hot_ref, stack.at[fixed], sems.at[1]),
         pltpu.make_async_copy(high_ref, high, sems.at[2]),
         pltpu.make_async_copy(low_ref, low_part, sems.at[3]),
+        pltpu.make_async_copy(pre_ref, pre, sems.at[11]),
+        pltpu.make_async_copy(dense_ref, dense, sems.at[12]),
+        pltpu.make_async_copy(extra_ref, extra, sems.at[13]),
     ]
     for copy in incoming:
         copy.start()
@@ -248,6 +257,8 @@
     lax.fori_loop(0, lookups.shape[0] // 128, fetch, 0)
     band = band_ref[...].astype(F32).T
     side = jnp.where(lane_is_low((batch, LANES)), 0.0, 1.0)
+    bands = proj_ref.shape[0]
+    bags[3, :, bands:] = jnp.zeros((batch, hidden - bands), BF16)
     for f in range(cold_feats):
         first = jnp.zeros((batch, LANES), F32)
         second = jnp.zeros((batch, LANES), F32)
@@ -258,7 +269,7 @@
             first += jnp.where(b == 0.0, x, 0.0)
             second += jnp.where(b == 2.0, x, 0.0)
         pooled = jnp.concatenate([first, second], axis=1).astype(BF16)
-        bags[f] = pooled
+        bags[f // 2, :, f % 2 * bands : (f % 2 + 1) * bands] = pooled
         stack[1 + f] = dot(pooled, proj_ref[...]).astype(BF16)
     outgoing = pltpu.make_async_copy(stack.at[pl.ds(1, cold_feats)], cold_ref, sems.at[4])
     outgoing.start()
@@ -271,42 +282,31 @@
         rest = low_part[:, at, :].reshape(feats * 16, feats * 16)
         d = (dot(first, x) + dot(rest, x)).astype(BF16)
         d_stack[:, at, :] = d.reshape(feats, 16, hidden)
-    hot_feats = feats - 1 - cold_feats
-    cuts = hidden // LANES
-    d_pre = (d_stack[0].astype(F32) * silu_slope(pre_ref[...])).astype(BF16)
-    bottom = dot(dense_ref[...], d_pre, TN)
-    d_cold = d_stack[1 : 1 + cold_feats].reshape(cold_feats * batch, hidden)
-    pooled = bags[...].reshape(cold_feats * batch, bags.shape[2])
-    proj = dot(pooled, d_cold, TN)
-    d_hot = d_stack[1 + cold_feats :].reshape(hot_feats * batch, hidden)
-    first, rest = split_two(dot(counts_ref[...], d_hot))
-    hot_rows = tables * 32
-    picks = jnp.where(
-        iota((hot_rows, unique_ref.shape[1]), 0) == unique_ref[...], 1.0, 0.0
-    ).astype(BF16)
-    hot = dot(picks, first) + dot(picks, rest)
-    for c in range(cuts):
-        at = slice(c * LANES, (c + 1) * LANES)
-        parts[0, c] = hot[:, at]
-        parts[1, c] = jnp.concatenate(
-            [
-                bottom[:, at].reshape(tables, 16, LANES),
-                proj[:, at].reshape(tables, 8, LANES),
-                jnp.zeros((tables, 8, LANES), F32),
-            ],
-            axis=1,
-        ).reshape(hot_rows, LANES)
-    core = place_ref[1]
-    for k in range(cuts):
-        chunk = (place_ref[0] + k) % cuts
-        kept[k] = parts[core, chunk]
-        given[k] = parts[1 - core, chunk].astype(BF16)
-    dense_copies = [
-        pltpu.make_async_copy(given, given_ref, sems.at[5]),
-        pltpu.make_async_copy(kept, kept_ref, sems.at[6]),
-    ]
-    for copy in dense_copies:
-        copy.start()
+    d_pre[...] = (d_stack[0].astype(F32) * silu_slope(pre[...])).astype(BF16)
+
+    def factors(hot_to, rest_to):
+        pieces = [
+            (d_stack.at[fixed], hot_to.at[pl.ds(0, 8)]),
+            (extra, hot_to.at[pl.ds(8, 5)]),
+            (d_stack.at[pl.ds(1, cold_feats)], rest_to.at[pl.ds(0, 7)]),
+            (bags, rest_to.at[pl.ds(7, 4)]),
+            (dense, rest_to.at[11]),
+            (d_pre, rest_to.at[12]),
+        ]
+        return [pltpu.make_async_copy(*p, sems.at[5 + i]) for i, p in enumerate(pieces)]
+
+    first_core = place_ref[1] == 0
+
+    @pl.when(first_core)
+    def _():
+        for copy in factors(keep_ref, give_ref):
+            copy.start()
+
+    @pl.when(jnp.logical_not(first_core))
+    def _():
+        for copy in factors(give_ref, keep_ref):
+            copy.start()
+
     low = lane_is_low((batch, LANES))
     for f in range(cold_feats):
         d_pool = dot(d_stack[1 + f], proj_ref[...], NT).astype(BF16).astype(F32)
@@ -341,8 +341,69 @@
         b = wide[half + k * pairs : half + (k + 1) * pairs, :]
         slots_ref[k] = jnp.where(low, a, b).astype(BF16)
     outgoing.wait()
-    for copy in dense_copies:
-        copy.wait()
+
+    @pl.when(first_core)
+    def _():
+        for copy in factors(keep_ref, give_ref):
+            copy.wait()
+
+    @pl.when(jnp.logical_not(first_core))
+    def _():
+        for copy in factors(give_ref, keep_ref):
+            copy.wait()
+
+
+def dense_part_kernel(place_ref, keep_ref, took_ref, own_ref, up_ref, far_ref, down_ref, sums):
+    cuts, rows, _ = sums.shape
+    batch, hidden = keep_ref.shape[1:]
+
+    def put(make):
+        for c in range(cuts):
+            sums[(c - place_ref[0] + cuts) % cuts] = make(slice(c * LANES, (c + 1) * LANES))
+
+    @pl.when(place_ref[1] == 0)
+    def _():
+        picks, parts = [], []
+        for ref in (keep_ref, took_ref):
+            d_hot = ref[:8].reshape(8 * batch, hidden)
+            counts = [jnp.concatenate([ref[8 + u], ref[10 + u]], axis=1) for u in range(2)]
+            parts.append(dot(jnp.concatenate(counts, axis=0), d_hot))
+            line = ref[12][:16].astype(F32)[:1]
+            line = line[:, : hidden // 2] * 32.0 + line[:, hidden // 2 :]
+            at = iota((rows, hidden // 2), 0).astype(F32)
+            picks.append(jnp.where(at == line, 1.0, 0.0).astype(BF16))
+        picks = jnp.concatenate(picks, axis=1)
+        high, rest = split_two(jnp.concatenate(parts, axis=0))
+        hot = dot(picks, high) + dot(picks, rest)
+        put(lambda at: hot[:, at])
+
+    @pl.when(place_ref[1] != 0)
+    def _():
+        both = (keep_ref, took_ref)
+        dense = jnp.concatenate([ref[11] for ref in both], axis=0)
+        d_pre = jnp.concatenate([ref[12] for ref in both], axis=0)
+        bottom = dot(dense, d_pre, TN)
+        half = hidden // 2
+        proj = jnp.zeros((half, hidden), F32)
+        for ref in both:
+            bags = [ref[7 + f // 2][:, f % 2 * half : (f % 2 + 1) * half] for f in range(7)]
+            d_cold = ref[:7].reshape(7 * batch, hidden)
+            proj += dot(jnp.concatenate(bags, axis=0), d_cold, TN)
+        tables = rows // 32
+        put(
+            lambda at: jnp.concatenate(
+                [
+                    bottom[:, at].reshape(tables, 16, LANES),
+                    proj[:, at].reshape(tables, 8, LANES),
+                    jnp.zeros((tables, 8, LANES), F32),
+                ],
+                axis=1,
+            ).reshape(rows, LANES)
+        )
+
+    own_ref[...] = sums[0]
+    for k, out_ref in enumerate((up_ref, far_ref, down_ref)):
+        out_ref[...] = sums[k + 1].astype(BF16)
 
 
 def inter_kernel(bottom_ref, cold_ref, hot_ref, inter_ref, stack, grams):
@@ -612,13 +673,13 @@
         vmem=24,
     )(row_ids, asked, cold_table.T)
     received = exchange(fetched, "table")
-    pre, bottom, hot_emb, counts, high, low = call(
+    pre, bottom, hot_emb, extra, high, low = call(
         front_kernel,
         (
             shape((batch, hidden), F32),
             shape((batch, hidden), BF16),
             shape((hot_feats, batch, hidden), BF16),
-            shape((unique, hot_feats * batch), BF16),
+            shape((5, batch, hidden), BF16),
             shape((feats, batch, feats * feats), BF16),
             shape((feats, batch, feats * feats), BF16),
         ),
@@ -628,17 +689,18 @@
         bottom_weight,
         hot_table,
         hot_unique.reshape(unique, 1),
+        hot_unique.reshape(1, unique),
         jnp.transpose(hot_map, (1, 2, 0)),
         grad_inter,
     )
     cuts = hidden // LANES
-    slot_grads, cold_emb, dense_kept, dense_given = call(
+    slot_grads, cold_emb, keep, give = call(
         main_kernel,
         (
             shape((tables, pairs, LANES), BF16),
             shape((cold_feats, batch, hidden), BF16),
-            shape((cuts, tables * 32, LANES), F32),
-            shape((cuts, tables * 32, LANES), BF16),
+            shape((13, batch, hidden), BF16),
+            shape((13, batch, hidden), BF16),
         ),
         scratch=[
             pltpu.VMEM((2 * tables * pairs, LANES), F32),
@@ -647,13 +709,14 @@
             pltpu.VMEM((feats, batch, feats * feats), BF16),
             pltpu.VMEM((feats, batch, feats * feats), BF16),
             pltpu.VMEM((feats, batch, hidden), BF16),
-            pltpu.VMEM((cold_feats, batch, bands), BF16),
-            pltpu.VMEM((2, cuts, tables * 32, LANES), F32),
-            pltpu.VMEM((cuts, tables * 32, LANES), F32),
-            pltpu.VMEM((cuts, tables * 32, LANES), BF16),
-            pltpu.SemaphoreType.DMA((7,)),
+            pltpu.VMEM((4, batch, hidden), BF16),
+            pltpu.VMEM((batch, hidden), F32),
+            pltpu.VMEM((batch, hidden), BF16),
+            pltpu.VMEM((batch, hidden), BF16),
+            pltpu.VMEM((5, batch, hidden), BF16),
+            pltpu.SemaphoreType.DMA((14,)),
         ],
-        specs=[SMEM] * 2 + [VMEM] * 7 + [HBM] * 4,
+        specs=[SMEM] * 2 + [VMEM] * 3 + [HBM] * 7,
         out_specs=[VMEM, HBM, HBM, HBM],
         us=14,
         vmem=62,
@@ -665,19 +728,24 @@
         projection,
         pre,
         dense_input,
-        counts,
-        hot_unique.reshape(1, unique),
+        extra,
         bottom,
         hot_emb,
         high,
         low,
     )
     returned = exchange(slot_grads, "table")
-    dense_pair = dense_kept + to_other_core(dense_given).astype(F32)
-    dense_out = dense_pair[1:].astype(BF16)
-    dense_row = dense_pair[0]
-    for k, steps in enumerate((1, 2, -1)):
-        dense_row += along_x(dense_out[k], steps).astype(F32)
+    took = to_other_core(give)
+    dense_row, dense_up, dense_far, dense_down = call(
+        dense_part_kernel,
+        (shape((tables * 32, LANES), F32),) + (shape((tables * 32, LANES), BF16),) * 3,
+        scratch=[pltpu.VMEM((cuts, tables * 32, LANES), F32)],
+        specs=[SMEM, VMEM, VMEM],
+        us=4,
+        vmem=32,
+    )(place, keep, took)
+    for part, steps in ((dense_up, 1), (dense_far, 2), (dense_down, -1)):
+        dense_row += along_x(part, steps).astype(F32)
     dense_row = dense_row.astype(BF16).reshape(tables, 32, LANES)
     returned, dense_row = lax.optimization_barrier((returned, dense_row))
     dense_all = exchange(dense_row, "table")

time: 162 us -> 161 us (level)
  other arithmetic: 3.29 us -> 1.46 us
    pallas_call x0 -> x1, Pallas kernels: none -> 2.74 us  [shards(): call(dense_part_kernel, (shape((tables * 32, LANES), F32),) + (shape((tab...]
    pallas_call x1, Pallas kernels: 13.9 us -> 11.9 us  [shards(): call(main_kernel, (shape((tables, pairs, LANES), BF16), shape((cold_feats...]
    another operation x1 -> x0, other arithmetic: 1.87 us -> none
    ppermute x7, waiting for transfers between devices: 26.6 us -> 24.9 us  [along_x(): return lax.ppermute(x, 'dp', [(i, (i + 2 * steps) % 8) for i in range(8)])]
    unnamed x61 -> x63, local copies, waits for them, and re-layouts: 7.72 us -> 8.18 us
  transfers between devices with their start and end apart: 15 -> 15, of which waited for: 10 -> 9; matrix products, arithmetic and copies ran while one was open for 3% -> 1% of each run, Pallas kernels for 12% -> 14%
where the time goes in v5:
time: 161 us; the launch traced here: 160 us
  Pallas kernels  49.3 us (31%)
  waiting for transfers between devices  44.6 us (28%)
  starting transfers between devices  34.3 us (21%)
  blocking collectives  20.3 us (13%)
  local copies, waits for them, and re-layouts  8.92 us (6%)
    ppermute x7, waiting for transfers between devices, along_x(): return lax.ppermute(x, 'dp', [(i, (i + 2 * steps) % 8) for i in range(8)])  24.9 us
    all_to_all x3, starting transfers between devices, exchange(): return lax.all_to_all(x, axis, split_axis=0, concat_axis=0, tiled=True)  20.7 us
    all_to_all x1, blocking collectives, exchange(): return lax.all_to_all(x, axis, split_axis=0, concat_axis=0, tiled=True)  20.3 us
    all_to_all x3, waiting for transfers between devices, exchange(): return lax.all_to_all(x, axis, split_axis=0, concat_axis=0, tiled=True)  18.2 us
    pallas_call x1, Pallas kernels, shards(): call(add_kernel, (shape((2, half, LANES), BF16), shape((2, 2, half, LANES...  13.9 us
    ppermute x7, starting transfers between devices, along_x(): return lax.ppermute(x, 'dp', [(i, (i + 2 * steps) % 8) for i in range(8)])  12.3 us
    pallas_call x1, Pallas kernels, shards(): call(main_kernel, (shape((tables, pairs, LANES), BF16), shape((cold_feats...  11.9 us
    pallas_call x1, Pallas kernels, shards(): call(gather_kernel, shape((tables, pairs, LANES), BF16), scratch=[pltpu.V...  11 us
  transfers between devices with their start and end apart: 15, of which 9 were waited for; matrix products, arithmetic and copies ran while one was open for 1% of the time, Pallas kernels for 14%

profile of v5, /device:TPU:8, one launch (start us, length us, event | category | flops | bytes accessed | tf_op | source)
XLA Modules:
  0.0 160.0 jit_solution(2161518989507303955)
XLA Ops:
  0.6 0.7 copy-done.9
  1.3 0.7 copy-done.10
  2.1 1.2 shard_map.146
  3.3 0.0 copy-start.11
  3.3 20.3 %all_to_all.20 = s32[32,1,256]{2,1,0:T(1,128)S(1)} all-to-all(s32[32,1,256]{2,1,0:T(1,128)S(1)} %get-tuple-element.52), channel_id=1, replica_groups=mesh['table'=32,'dp'=8] {'table'}, dimensions={0} | all-to-all | bytes 65536 | tf_op jit(solution)/shard_map/all_to_all | solution.py:625
  23.7 0.0 copy-start.1
  23.7 11.0 %shard_map.147 = bf16[32,112,128]{2,1,0:T(8,128)(2,1)} custom-call(s32[8192]{0:T(1024)S(1)} %bitcast.20, s32[32,256]{1,0:T(8,128)S(1)} %bitcast.18, bf16[64,32768]{1,0:T(8,128)(2,1)S(1)} %bitcast.24), custom_call_target="tpu_custom_call" | custom-call | flops 13200000000 | bytes 1048576 | tf_op jit(solution)/shard_map/pallas_call | solution.py:666
  34.7 0.0 copy-start.4
  34.7 0.0 copy-start.5
  34.7 0.0 copy-start.6
  34.7 0.0 copy-start.7
  34.8 0.0 copy-start.8
  34.8 5.2 %all-to-all-start.1 = ((bf16[32,112,128]{2,1,0:T(8,128)(2,1)}), bf16[32,112,128]{2,1,0:T(8,128)(2,1)S(1)}, u32[]{:S(2)}, u32[]{:S(2)}) async-start(bf16[32,112,128]{2,1,0:T(8,128)(2,1)} %shard_map.147), calls=%async_computation.1 | async-start | bytes 1835008 | tf_op jit(solution)/shard_map/all_to_all | solution.py:625
  40.0 0.6 reshape.38.band_ref
  40.7 0.1 copy.19.unique_ref
  40.8 0.6 pad_add_fusion.place_ref
  41.5 2.6 %shard_map.148 = (f32[128,512]{1,0:T(8,128)S(1)}, bf16[128,512]{1,0:T(8,128)(2,1)S(1)}, bf16[8,128,512]{2,1,0:T(8,128)(2,1)S(1)}, bf16[5,128,512]{2,1,0:T(8,128)...) custom-call(bf16[128,512]{1,0:T(8,128)(2,1)S(1)} %copy-done.7, ...), custom_call_target="tpu_custom_call" | custom-call | flops 3300000000 | bytes 1048576 | tf_op jit(solution)/shard_map/pallas_call | solution.py:676
  44.0 0.0 copy-start.18
  44.1 1.0 copy-done.18
  45.0 1.0 copy-done.20
  46.0 1.0 copy-done.21
  47.0 0.9 copy-done.22
  47.9 0.7 copy-done.24
  48.6 0.7 copy-done.25
  49.2 12.8 %all-to-all-done.1.rows_ref = bf16[32,112,128]{2,1,0:T(8,128)(2,1)S(1)} async-done(((bf16[32,112,128]{2,1,0:T(8,128)(2,1)}), bf16[32,112,128]{2,1,0:T(8,128)(2,1)S(1)}, u32[]{:S(2)}, u32[]{:S(2)}) %all-to-all-start.1) | async-done | bytes 917536 | tf_op jit(solution)/shard_map/all_to_all | solution.py:625
  62.1 1.0 copy-done.27
  63.0 11.9 %shard_map.149 = (bf16[32,112,128]{2,1,0:T(8,128)(2,1)}, bf16[7,128,512]{2,1,0:T(8,128)(2,1)}, bf16[13,128,512]{2,1,0:T(8,128)(2,1)}, bf16[13,128,512]{2,1,0:T(8,128)(2,1)}) custom-call(s32[2]{0:T(128)} %pad_add_fusion.place_ref, s32[3584]{0:T(1024)} %bitcast.28, bf16[32,112,128]{2,1,0:T(8,128)(2,1)} %copy-done.27, s32[28,128]{1,0:T(8,128)} %reshape.38.band_ref, ...), custom_call_target="tpu_custom_call" | custom-call | flops 15399999488 | bytes 1048576 | tf_op jit(solution)/shard_map/pallas_call | solution.py:697
  75.0 0.1 collective-permute-start
  75.1 8.0 %all-to-all-start.2 = ((bf16[32,112,128]{2,1,0:T(8,128)(2,1)}), bf16[32,112,128]{2,1,0:T(8,128)(2,1)}, u32[]{:S(2)}, u32[]{:S(2)}) async-start(bf16[32,112,128]{2,1,0:T(8,128)(2,1)} %get-tuple-element.60), calls=%async_computation.2 | async-start | bytes 1835008 | tf_op jit(solution)/shard_map/all_to_all | solution.py:625
  83.1 0.0 collective-permute-done.took_ref
  83.1 2.7 %shard_map.150 = (f32[1024,128]{1,0:T(8,128)S(1)}, bf16[1024,128]{1,0:T(8,128)(2,1)S(1)}, bf16[1024,128]{1,0:T(8,128)(2,1)S(1)}, bf16[1024,128]{1,0:T(8,128)(2,1)S(1)}) custom-call(s32[2]{0:T(128)S(1)} %copy-done.12, bf16[13,128,512]{2,1,0:T(8,128)(2,1)S(1)} %copy-done.17, bf16[13,128,512]{2,1,0:T(8,128)(2,1)S(1)} %collective-permute-done.took_ref), custom_call_target="tpu_custom_call" | custom-call | flops 4400000000 | bytes 1048576 | tf_op jit(solution)/shard_map/pallas_call | solution.py:739
  85.8 1.6 collective-permute-start.1
  87.4 2.7 %collective-permute-start.2 = (bf16[1024,128]{1,0:T(8,128)(2,1)S(1)}, bf16[1024,128]{1,0:T(8,128)(2,1)S(1)}, u32[]{:S(2)}, u32[]{:S(2)}) collective-permute-start(bf16[1024,128]{1,0:T(8,128)(2,1)S(1)} %get-tuple-element.65), channel_id=1, source_target_pairs={{0,4},{1,5},{2,6},{3,7},{4,0},{5,1},{6,2},{7,3},{8,12},{9,13},{10,... | collective-permute-start | bytes 786440 | tf_op jit(solution)/shard_map/ppermute | solution.py:621
  90.1 1.4 collective-permute-start.3
  91.6 3.8 %collective-permute-done.1 = bf16[1024,128]{1,0:T(8,128)(2,1)S(1)} collective-permute-done((bf16[1024,128]{1,0:T(8,128)(2,1)S(1)}, bf16[1024,128]{1,0:T(8,128)(2,1)S(1)}, u32[]{:S(2)}, u32[]{:S(2)}) %collective-permute-start.1) | collective-permute-done | bytes 262176 | tf_op jit(solution)/shard_map/ppermute | solution.py:621
  95.4 5.4 %collective-permute-done.2 = bf16[1024,128]{1,0:T(8,128)(2,1)S(1)} collective-permute-done((bf16[1024,128]{1,0:T(8,128)(2,1)S(1)}, bf16[1024,128]{1,0:T(8,128)(2,1)S(1)}, u32[]{:S(2)}, u32[]{:S(2)}) %collective-permute-start.2) | collective-permute-done | bytes 262176 | tf_op jit(solution)/shard_map/ppermute | solution.py:621
  100.8 0.0 collective-permute-done.3
  100.8 0.8 add_convert_fusion
  101.6 5.4 %all-to-all-done.2.rows_ref = bf16[32,112,128]{2,1,0:T(8,128)(2,1)} async-done(((bf16[32,112,128]{2,1,0:T(8,128)(2,1)}), bf16[32,112,128]{2,1,0:T(8,128)(2,1)}, u32[]{:S(2)}, u32[]{:S(2)}) %all-to-all-start.2) | async-done | bytes 917536 | tf_op jit(solution)/shard_map/all_to_all | solution.py:625
  107.0 7.5 %all-to-all-start.3 = ((bf16[32,32,128]{2,1,0:T(8,128)(2,1)}), bf16[32,32,128]{2,1,0:T(8,128)(2,1)S(1)}, u32[]{:S(2)}, u32[]{:S(2)}) async-start(bf16[32,32,128]{2,1,0:T(8,128)(2,1)} %bitcast.12), calls=%async_computation.3 | async-start | bytes 524288 | tf_op jit(solution)/shard_map/all_to_all | solution.py:625
  114.5 13.9 %shard_map.151 = (bf16[2,1024,128]{2,1,0:T(8,128)(2,1)}, bf16[2,2,1024,128]{3,2,1,0:T(8,128)(2,1)}, bf16[2,1024,128]{2,1,0:T(8,128)(2,1)}, bf16[2,1024,128]{2,1,...) custom-call(s32[2]{0:T(128)} %pad_add_fusion.place_ref, s32[8192]{0:T(1024)} %bitcast.21, ...), custom_call_target="tpu_custom_call" | custom-call | flops 22000001024 | bytes 1048576 | tf_op jit(solution)/shard_map/pallas_call | solution.py:754
  128.4 0.0 all-to-all-done.3.rows_ref
  128.4 0.1 collective-permute-start.4
  128.6 0.6 collective-permute-start.5
  129.2 1.3 collective-permute-done.5.theirs_ref
  130.5 0.2 collective-permute-done.4.taken_ref
  130.7 0.0 copy-start.19
  130.7 0.0 copy-start.26
  130.7 0.7 shard_map.153
  131.4 0.5 copy-done.29
  131.9 0.1 collective-permute-start.8
  132.0 0.4 collective-permute-start.9
  132.4 1.5 collective-permute-start.6
  133.9 1.7 %collective-permute-start.7 = (bf16[1152,128]{1,0:T(8,128)(2,1)S(1)}, bf16[1152,128]{1,0:T(8,128)(2,1)S(1)}, u32[]{:S(2)}, u32[]{:S(2)}) collective-permute-start(bf16[1152,128]{1,0:T(8,128)(2,1)S(1)} %get-tuple-element.74), channel_id=1, source_target_pairs={{0,6},{1,7},{2,0},{3,1},{4,2},{5,3},{6,4},{7,5},{8,14},{9,15},{10,... | collective-permute-start | bytes 884744 | tf_op jit(solution)/shard_map/ppermute | solution.py:621
  135.6 3.0 %shard_map.154 = f32[128,256]{1,0:T(8,128)} custom-call(bf16[128,512]{1,0:T(8,128)(2,1)S(1)} %copy-done.26, bf16[7,128,512]{2,1,0:T(8,128)(2,1)S(1)} %copy-done.23, bf16[8,128,512]{2,1,0:T(8,128)(2,1)S(1)} %copy-done.19), custom_call_target="tpu_custom_call" | custom-call | flops 4400000000 | bytes 1048576 | tf_op jit(solution)/shard_map/pallas_call | solution.py:791
  138.7 4.0 %collective-permute-done.6.below_ref.before_ref = bf16[1152,128]{1,0:T(8,128)(2,1)S(1)} collective-permute-done((bf16[1152,128]{1,0:T(8,128)(2,1)S(1)}, bf16[1152,128]{1,0:T(8,128)(2,1)S(1)}, u32[]{:S(2)}, u32[]{:S(2)}) %collective-permute-start.6) | collective-permute-done | bytes 294944 | tf_op jit(solution)/shard_map/ppermute | solution.py:621
  142.6 0.0 collective-permute-done.7.above_ref.next_ref
  142.7 0.3 shard_map.155
  143.0 1.3 collective-permute-start.10
  144.3 2.1 %collective-permute-start.11 = (bf16[2048,128]{1,0:T(8,128)(2,1)S(1)}, bf16[2048,128]{1,0:T(8,128)(2,1)S(1)}, u32[]{:S(2)}, u32[]{:S(2)}) collective-permute-start(bf16[2048,128]{1,0:T(8,128)(2,1)S(1)} %get-tuple-element.93), channel_id=1, source_target_pairs={{0,6},{1,7},{2,0},{3,1},{4,2},{5,3},{6,4},{7,5},{8,14},{9,15},{10,... | collective-permute-start | bytes 1572872 | tf_op jit(solution)/shard_map/ppermute | solution.py:621
  146.3 0.1 shard_map.156.pair_ref
  146.4 10.4 %collective-permute-done.11.above_ref = bf16[2048,128]{1,0:T(8,128)(2,1)S(1)} collective-permute-done((bf16[2048,128]{1,0:T(8,128)(2,1)S(1)}, bf16[2048,128]{1,0:T(8,128)(2,1)S(1)}, u32[]{:S(2)}, u32[]{:S(2)}) %collective-permute-start.11) | collective-permute-done | bytes 524320 | tf_op jit(solution)/shard_map/ppermute | solution.py:621
  156.8 1.3 collective-permute-done.10.below_ref
  158.1 1.9 %shard_map.157 = (f32[64,4096]{1,0:T(8,128)}, f32[32,512]{1,0:T(8,128)}, f32[8,512]{1,0:T(8,128)}, f32[16,512]{1,0:T(8,128)}) custom-call(s32[2]{0:T(128)S(1)} %copy-done.13, f32[2,1024,128]{2,1,0:T(8,128)S(1)} %shard_map.156.pair_ref, bf16[2176,128]{1,0:T(8,128)(2,1)S(1)} %collective-permute-done.10.below_ref, ...), custom_call_target="tpu_custom_call" | custom-call | flops 2200000000 | bytes 1048576 | tf_op jit(solution)/shard_map/pallas_call | solution.py:813
  (47 shorter events, 0.2 us)
Async XLA Ops:
  0.6 0.7 copy-start.9
  1.3 0.7 copy-start.10
  2.1 21.6 %copy-start.3 = (bf16[32768,64]{0,1:T(8,128)(2,1)S(1)}, bf16[32768,64]{0,1:T(8,128)(2,1)}, u32[]{:S(2)}) copy-start(bf16[32768,64]{0,1:T(8,128)(2,1)} %param.13) | copy-start | bytes 12582916
  3.3 20.3 %copy-start.11 = (s32[28,128]{1,0:T(8,128)}, s32[28,128]{1,0:T(8,128)S(1)}, u32[]{:S(2)}) copy-start(s32[28,128]{1,0:T(8,128)S(1)} %get-tuple-element.53) | copy-start | bytes 43012
  23.6 11.1 %copy-start = (s32[32,1,256]{2,0,1:T(8,128)}, s32[32,1,256]{2,0,1:T(8,128)S(1)}, u32[]{:S(2)}) copy-start(s32[32,1,256]{2,0,1:T(8,128)S(1)} %copy.22) | copy-start | bytes 98308
  23.7 11.0 %copy-start.1 = (s32[32,1,256]{2,1,0:T(1,128)}, s32[32,1,256]{2,1,0:T(1,128)S(1)}, u32[]{:S(2)}) copy-start(s32[32,1,256]{2,1,0:T(1,128)S(1)} %broadcast_and_fusion) | copy-start | bytes 98308
  34.7 5.3 %copy-start.28 = (s32[128,7,4]{0,2,1:T(4,128)S(1)}, s32[128,7,4]{0,2,1:T(4,128)}, u32[]{:S(2)}) copy-start(s32[128,7,4]{0,2,1:T(4,128)} %param.18) | copy-start | bytes 43012
  34.7 6.0 %copy-start.2 = (s32[256]{0:T(256)S(1)}, s32[256]{0:T(256)}, u32[]{:S(2)}) copy-start(s32[256]{0:T(256)} %param.19) | copy-start | bytes 3076
  34.7 6.7 %copy-start.4 = (bf16[1024,512]{1,0:T(8,128)(2,1)S(1)}, bf16[1024,512]{1,0:T(8,128)(2,1)}, u32[]{:S(2)}) copy-start(bf16[1024,512]{1,0:T(8,128)(2,1)} %hot_ref.1) | copy-start | bytes 3145732
  34.7 6.7 %copy-start.5 = (bf16[512,512]{1,0:T(8,128)(2,1)S(1)}, bf16[512,512]{1,0:T(8,128)(2,1)}, u32[]{:S(2)}) copy-start(bf16[512,512]{1,0:T(8,128)(2,1)} %weight_ref.1) | copy-start | bytes 1572868
  34.7 6.7 %copy-start.6 = (f32[128,256]{1,0:T(8,128)S(1)}, f32[128,256]{1,0:T(8,128)}, u32[]{:S(2)}) copy-start(f32[128,256]{1,0:T(8,128)} %grad_ref.1) | copy-start | bytes 393220
  34.7 6.7 %copy-start.7 = (bf16[128,512]{1,0:T(8,128)(2,1)S(1)}, bf16[128,512]{1,0:T(8,128)(2,1)}, u32[]{:S(2)}) copy-start(bf16[128,512]{1,0:T(8,128)(2,1)} %dense_ref.3) | copy-start | bytes 393220
  34.8 6.7 %copy-start.8 = (s32[128,8,4]{0,2,1:T(4,128)S(1)}, s32[128,8,4]{0,2,1:T(4,128)}, u32[]{:S(2)}) copy-start(s32[128,8,4]{0,2,1:T(4,128)} %param.20) | copy-start | bytes 49156
  34.8 27.3 %all-to-all-start.1 = ((bf16[32,112,128]{2,1,0:T(8,128)(2,1)}), bf16[32,112,128]{2,1,0:T(8,128)(2,1)S(1)}, u32[]{:S(2)}, u32[]{:S(2)}) async-start(bf16[32,112,128]{2,1,0:T(8,128)(2,1)} %shard_map.147), calls=%async_computation.1 | async-start | bytes 1835008 | tf_op jit(solution)/shard_map/all_to_all | solution.py:625
  44.0 1.0 copy-start.18
  45.0 1.0 copy-start.20
  46.0 1.0 copy-start.21
  47.0 0.9 copy-start.22
  47.9 0.7 copy-start.24
  48.6 0.7 copy-start.25
  62.1 1.0 copy-start.27
  75.0 8.1 %copy-start.12 = (s32[2]{0:T(128)S(1)}, s32[2]{0:T(128)}, u32[]{:S(2)}) copy-start(s32[2]{0:T(128)} %pad_add_fusion.place_ref) | copy-start | bytes 28
  75.0 8.1 %copy-start.17 = (bf16[13,128,512]{2,1,0:T(8,128)(2,1)S(1)}, bf16[13,128,512]{2,1,0:T(8,128)(2,1)}, u32[]{:S(2)}) copy-start(bf16[13,128,512]{2,1,0:T(8,128)(2,1)} %get-tuple-element.61.keep_ref) | copy-start | bytes 5111812
  75.0 8.1 %collective-permute-start = (bf16[13,128,512]{2,1,0:T(8,128)(2,1)}, bf16[13,128,512]{2,1,0:T(8,128)(2,1)S(1)}, u32[]{:S(2)}, u32[]{:S(2)}) collective-permute-start(bf16[13,128,512]{2,1,0:T(8,128)(2,1)} %get-tuple-element.62), channel_id=1, source_target_pairs={{0,1},{1,0},{2,3},{3,2},{4,5},{5,4},{6,7},{7,6},{8,9},{9,8},{10,11... | collective-permute-start | bytes 5111816 | tf_op jit(solution)/shard_map/ppermute | solution.py:617
  75.1 31.9 %all-to-all-start.2 = ((bf16[32,112,128]{2,1,0:T(8,128)(2,1)}), bf16[32,112,128]{2,1,0:T(8,128)(2,1)}, u32[]{:S(2)}, u32[]{:S(2)}) async-start(bf16[32,112,128]{2,1,0:T(8,128)(2,1)} %get-tuple-element.60), calls=%async_computation.2 | async-start | bytes 1835008 | tf_op jit(solution)/shard_map/all_to_all | solution.py:625
  85.8 9.5 %collective-permute-start.1 = (bf16[1024,128]{1,0:T(8,128)(2,1)S(1)}, bf16[1024,128]{1,0:T(8,128)(2,1)S(1)}, u32[]{:S(2)}, u32[]{:S(2)}) collective-permute-start(bf16[1024,128]{1,0:T(8,128)(2,1)S(1)} %get-tuple-element.64), channel_id=1, source_target_pairs={{0,2},{1,3},{2,4},{3,5},{4,6},{5,7},{6,0},{7,1},{8,10},{9,11},{10,... | collective-permute-start | bytes 786440 | tf_op jit(solution)/shard_map/ppermute | solution.py:621
  87.4 13.4 %collective-permute-start.2 = (bf16[1024,128]{1,0:T(8,128)(2,1)S(1)}, bf16[1024,128]{1,0:T(8,128)(2,1)S(1)}, u32[]{:S(2)}, u32[]{:S(2)}) collective-permute-start(bf16[1024,128]{1,0:T(8,128)(2,1)S(1)} %get-tuple-element.65), channel_id=1, source_target_pairs={{0,4},{1,5},{2,6},{3,7},{4,0},{5,1},{6,2},{7,3},{8,12},{9,13},{10,... | collective-permute-start | bytes 786440 | tf_op jit(solution)/shard_map/ppermute | solution.py:621
  90.1 10.7 %collective-permute-start.3 = (bf16[1024,128]{1,0:T(8,128)(2,1)S(1)}, bf16[1024,128]{1,0:T(8,128)(2,1)S(1)}, u32[]{:S(2)}, u32[]{:S(2)}) collective-permute-start(bf16[1024,128]{1,0:T(8,128)(2,1)S(1)} %get-tuple-element.66), channel_id=1, source_target_pairs={{0,6},{1,7},{2,0},{3,1},{4,2},{5,3},{6,4},{7,5},{8,14},{9,15},{10,... | collective-permute-start | bytes 786440 | tf_op jit(solution)/shard_map/ppermute | solution.py:621
  107.0 21.4 %all-to-all-start.3 = ((bf16[32,32,128]{2,1,0:T(8,128)(2,1)}), bf16[32,32,128]{2,1,0:T(8,128)(2,1)S(1)}, u32[]{:S(2)}, u32[]{:S(2)}) async-start(bf16[32,32,128]{2,1,0:T(8,128)(2,1)} %bitcast.12), calls=%async_computation.3 | async-start | bytes 524288 | tf_op jit(solution)/shard_map/all_to_all | solution.py:625
  128.4 2.2 %copy-start.13 = (s32[2]{0:T(128)S(1)}, s32[2]{0:T(128)}, u32[]{:S(2)}) copy-start(s32[2]{0:T(128)} %pad_add_fusion.place_ref) | copy-start | bytes 28
  128.4 2.2 %copy-start.15 = (bf16[2,1024,128]{2,1,0:T(8,128)(2,1)S(1)}, bf16[2,1024,128]{2,1,0:T(8,128)(2,1)}, u32[]{:S(2)}) copy-start(bf16[2,1024,128]{2,1,0:T(8,128)(2,1)} %get-tuple-element.68.kept_ref) | copy-start | bytes 1572868
  128.4 2.2 %collective-permute-start.4 = (bf16[2,1024,128]{2,1,0:T(8,128)(2,1)}, bf16[2,1024,128]{2,1,0:T(8,128)(2,1)S(1)}, u32[]{:S(2)}, u32[]{:S(2)}) collective-permute-start(bf16[2,1024,128]{2,1,0:T(8,128)(2,1)} %get-tuple-element.71), channel_id=1, source_target_pairs={{0,1},{1,0},{2,3},{3,2},{4,5},{5,4},{6,7},{7,6},{8,9},{9,8},{10,11... | collective-permute-start | bytes 1572872 | tf_op jit(solution)/shard_map/ppermute | solution.py:617
  128.6 1.9 %collective-permute-start.5 = (bf16[64,128]{1,0:T(8,128)(2,1)S(1)}, bf16[64,128]{1,0:T(8,128)(2,1)S(1)}, u32[]{:S(2)}, u32[]{:S(2)}) collective-permute-start(bf16[64,128]{1,0:T(8,128)(2,1)S(1)} %shard_map.152.mine_ref), channel_id=1, source_target_pairs={{0,1},{1,0},{2,3},{3,2},{4,5},{5,4},{6,7},{7,6},{8,9},{9,8},{10,11... | collective-permute-start | bytes 49160 | tf_op jit(solution)/shard_map/ppermute | solution.py:617
  130.6 1.2 copy-start.29
  130.6 1.4 copy-start.30
  130.7 5.0 %copy-start.19 = (bf16[8,128,512]{2,1,0:T(8,128)(2,1)S(1)}, bf16[8,128,512]{2,1,0:T(8,128)(2,1)}, u32[]{:S(2)}) copy-start(bf16[8,128,512]{2,1,0:T(8,128)(2,1)} %copy-done.18) | copy-start | bytes 3145732
  130.7 5.0 %copy-start.23 = (bf16[7,128,512]{2,1,0:T(8,128)(2,1)S(1)}, bf16[7,128,512]{2,1,0:T(8,128)(2,1)}, u32[]{:S(2)}) copy-start(bf16[7,128,512]{2,1,0:T(8,128)(2,1)} %get-tuple-element.80.cold_ref) | copy-start | bytes 2752516
  130.7 5.0 %copy-start.26 = (bf16[128,512]{1,0:T(8,128)(2,1)S(1)}, bf16[128,512]{1,0:T(8,128)(2,1)}, u32[]{:S(2)}) copy-start(bf16[128,512]{1,0:T(8,128)(2,1)} %copy-done.25) | copy-start | bytes 393220
  131.9 10.8 %copy-start.14 = (bf16[2,2,1024,128]{3,2,1,0:T(8,128)(2,1)S(1)}, bf16[2,2,1024,128]{3,2,1,0:T(8,128)(2,1)}, u32[]{:S(2)}) copy-start(bf16[2,2,1024,128]{3,2,1,0:T(8,128)(2,1)} %get-tuple-element.82.kept_ref) | copy-start | bytes 3145732
  131.9 10.8 %collective-permute-start.8 = (bf16[2,2,1024,128]{3,2,1,0:T(8,128)(2,1)S(1)}, bf16[2,2,1024,128]{3,2,1,0:T(8,128)(2,1)S(1)}, u32[]{:S(2)}, u32[]{:S(2)}) collective-permute-start(bf16[2,2,1024,128]{3,2,1,0:T(8,128)(2,1)S(1)} %copy-done.29), channel_id=1, source_target_pairs={{0,1},{1,0},{2,3},{3,2},{4,5},{5,4},{6,7},{7,6},{8,9},{9,8},{10,11... | collective-permute-start | bytes 3145736 | tf_op jit(solution)/shard_map/ppermute | solution.py:617
  132.0 10.6 %collective-permute-start.9 = (bf16[2,1024,128]{2,1,0:T(8,128)(2,1)S(1)}, bf16[2,1024,128]{2,1,0:T(8,128)(2,1)S(1)}, u32[]{:S(2)}, u32[]{:S(2)}) collective-permute-start(bf16[2,1024,128]{2,1,0:T(8,128)(2,1)S(1)} %copy-done.30), channel_id=1, source_target_pairs={{0,1},{1,0},{2,3},{3,2},{4,5},{5,4},{6,7},{7,6},{8,9},{9,8},{10,11... | collective-permute-start | bytes 1572872 | tf_op jit(solution)/shard_map/ppermute | solution.py:617
  132.4 10.3 %collective-permute-start.6 = (bf16[1152,128]{1,0:T(8,128)(2,1)S(1)}, bf16[1152,128]{1,0:T(8,128)(2,1)S(1)}, u32[]{:S(2)}, u32[]{:S(2)}) collective-permute-start(bf16[1152,128]{1,0:T(8,128)(2,1)S(1)} %get-tuple-element.94.own_ref), channel_id=1, source_target_pairs={{0,2},{1,3},{2,4},{3,5},{4,6},{5,7},{6,0},{7,1},{8,10},{9,11},{10,... | collective-permute-start | bytes 884744 | tf_op jit(solution)/shard_map/ppermute | solution.py:621
  133.9 8.8 %collective-permute-start.7 = (bf16[1152,128]{1,0:T(8,128)(2,1)S(1)}, bf16[1152,128]{1,0:T(8,128)(2,1)S(1)}, u32[]{:S(2)}, u32[]{:S(2)}) collective-permute-start(bf16[1152,128]{1,0:T(8,128)(2,1)S(1)} %get-tuple-element.74), channel_id=1, source_target_pairs={{0,6},{1,7},{2,0},{3,1},{4,2},{5,3},{6,4},{7,5},{8,14},{9,15},{10,... | collective-permute-start | bytes 884744 | tf_op jit(solution)/shard_map/ppermute | solution.py:621
  142.7 3.6 %copy-start.16 = (f32[2,1024,128]{2,1,0:T(8,128)S(1)}, f32[2,1024,128]{2,1,0:T(8,128)}, u32[]{:S(2)}) copy-start(f32[2,1024,128]{2,1,0:T(8,128)} %get-tuple-element.90.kept_ref) | copy-start | bytes 3145732
  143.0 15.1 %collective-permute-start.10 = (bf16[2176,128]{1,0:T(8,128)(2,1)S(1)}, bf16[2176,128]{1,0:T(8,128)(2,1)S(1)}, u32[]{:S(2)}, u32[]{:S(2)}) collective-permute-start(bf16[2176,128]{1,0:T(8,128)(2,1)S(1)} %get-tuple-element.92), channel_id=1, source_target_pairs={{0,2},{1,3},{2,4},{3,5},{4,6},{5,7},{6,0},{7,1},{8,10},{9,11},{10,... | collective-permute-start | bytes 1671176 | tf_op jit(solution)/shard_map/ppermute | solution.py:621
  144.3 12.5 %collective-permute-start.11 = (bf16[2048,128]{1,0:T(8,128)(2,1)S(1)}, bf16[2048,128]{1,0:T(8,128)(2,1)S(1)}, u32[]{:S(2)}, u32[]{:S(2)}) collective-permute-start(bf16[2048,128]{1,0:T(8,128)(2,1)S(1)} %get-tuple-element.93), channel_id=1, source_target_pairs={{0,6},{1,7},{2,0},{3,1},{4,2},{5,3},{6,4},{7,5},{8,14},{9,15},{10,... | collective-permute-start | bytes 1572872 | tf_op jit(solution)/shard_map/ppermute | solution.py:621

commit v6 on v5

--- a/solution.py
+++ b/solution.py
@@ -693,6 +693,7 @@
         jnp.transpose(hot_map, (1, 2, 0)),
         grad_inter,
     )
+    received, high, low = lax.optimization_barrier((received, high, low))
     cuts = hidden // LANES
     slot_grads, cold_emb, keep, give = call(
         main_kernel,
@@ -719,7 +720,7 @@
         specs=[SMEM] * 2 + [VMEM] * 3 + [HBM] * 7,
         out_specs=[VMEM, HBM, HBM, HBM],
         us=14,
-        vmem=62,
+        vmem=63,
     )(
         place,
         pos,

time: 161 us -> 161 us (level)
    unnamed x63 -> x61, local copies, waits for them, and re-layouts: 8.18 us -> 7.18 us
  transfers between devices with their start and end apart: 15 -> 15, of which waited for: 9 -> 10; matrix products, arithmetic and copies ran while one was open for 1% -> 1% of each run, Pallas kernels for 14% -> 14%
where the time goes in v6:
time: 161 us; the launch traced here: 160 us
  Pallas kernels  49.2 us (31%)
  waiting for transfers between devices  45.6 us (28%)
  starting transfers between devices  34.9 us (22%)
  blocking collectives  20.3 us (13%)
  local copies, waits for them, and re-layouts  7.92 us (5%)
    ppermute x7, waiting for transfers between devices, along_x(): return lax.ppermute(x, 'dp', [(i, (i + 2 * steps) % 8) for i in range(8)])  25.8 us
    all_to_all x3, starting transfers between devices, exchange(): return lax.all_to_all(x, axis, split_axis=0, concat_axis=0, tiled=True)  21.4 us
    all_to_all x1, blocking collectives, exchange(): return lax.all_to_all(x, axis, split_axis=0, concat_axis=0, tiled=True)  20.3 us
    all_to_all x3, waiting for transfers between devices, exchange(): return lax.all_to_all(x, axis, split_axis=0, concat_axis=0, tiled=True)  18.3 us
    pallas_call x1, Pallas kernels, shards(): call(add_kernel, (shape((2, half, LANES), BF16), shape((2, 2, half, LANES...  13.6 us
    ppermute x7, starting transfers between devices, along_x(): return lax.ppermute(x, 'dp', [(i, (i + 2 * steps) % 8) for i in range(8)])  12.3 us
    pallas_call x1, Pallas kernels, shards(): call(main_kernel, (shape((tables, pairs, LANES), BF16), shape((cold_feats...  11.9 us
    pallas_call x1, Pallas kernels, shards(): call(gather_kernel, shape((tables, pairs, LANES), BF16), scratch=[pltpu.V...  11 us
  transfers between devices with their start and end apart: 15, of which 10 were waited for; matrix products, arithmetic and copies ran while one was open for 1% of the time, Pallas kernels for 14%

profile of v6, /device:TPU:8, one launch (start us, length us, event | category | flops | bytes accessed | tf_op | source)
XLA Modules:
  0.0 160.4 jit_solution(16859444887600995887)
XLA Ops:
  0.6 0.7 copy-done.9
  1.3 0.7 copy-done.10
  2.1 1.2 shard_map.146
  3.3 0.0 copy-start.11
  3.3 20.3 %all_to_all.20 = s32[32,1,256]{2,1,0:T(1,128)S(1)} all-to-all(s32[32,1,256]{2,1,0:T(1,128)S(1)} %get-tuple-element.55), channel_id=1, replica_groups=mesh['table'=32,'dp'=8] {'table'}, dimensions={0} | all-to-all | bytes 65536 | tf_op jit(solution)/shard_map/all_to_all | solution.py:625
  23.7 0.0 copy-start.1
  23.7 11.0 %shard_map.147 = bf16[32,112,128]{2,1,0:T(8,128)(2,1)} custom-call(s32[8192]{0:T(1024)S(1)} %bitcast.20, s32[32,256]{1,0:T(8,128)S(1)} %bitcast.18, bf16[64,32768]{1,0:T(8,128)(2,1)S(1)} %bitcast.24), custom_call_target="tpu_custom_call" | custom-call | flops 13200000000 | bytes 1048576 | tf_op jit(solution)/shard_map/pallas_call | solution.py:666
  34.7 0.0 copy-start.4
  34.7 0.0 copy-start.5
  34.7 0.0 copy-start.6
  34.7 0.0 copy-start.7
  34.8 0.0 copy-start.8
  34.8 5.9 %all-to-all-start.1 = ((bf16[32,112,128]{2,1,0:T(8,128)(2,1)}), bf16[32,112,128]{2,1,0:T(8,128)(2,1)}, u32[]{:S(2)}, u32[]{:S(2)}) async-start(bf16[32,112,128]{2,1,0:T(8,128)(2,1)} %shard_map.147), calls=%async_computation.1 | async-start | bytes 1835008 | tf_op jit(solution)/shard_map/all_to_all | solution.py:625
  40.7 0.6 reshape.40.band_ref
  41.3 0.1 copy.19.unique_ref
  41.5 0.6 pad_add_fusion.place_ref
  42.1 2.6 %shard_map.148 = (f32[128,512]{1,0:T(8,128)S(1)}, bf16[128,512]{1,0:T(8,128)(2,1)S(1)}, bf16[8,128,512]{2,1,0:T(8,128)(2,1)S(1)}, bf16[5,128,512]{2,1,0:T(8,128)...) custom-call(bf16[128,512]{1,0:T(8,128)(2,1)S(1)} %copy-done.7, ...), custom_call_target="tpu_custom_call" | custom-call | flops 3300000000 | bytes 1048576 | tf_op jit(solution)/shard_map/pallas_call | solution.py:676
  44.7 0.0 copy-start.18
  44.7 1.0 copy-done.18
  45.6 1.0 copy-done.20
  46.6 1.0 copy-done.21
  47.6 0.8 copy-done.22
  48.5 0.7 copy-done.24
  49.2 0.7 copy-done.25
  49.8 12.9 %all-to-all-done.1.rows_ref = bf16[32,112,128]{2,1,0:T(8,128)(2,1)} async-done(((bf16[32,112,128]{2,1,0:T(8,128)(2,1)}), bf16[32,112,128]{2,1,0:T(8,128)(2,1)}, u32[]{:S(2)}, u32[]{:S(2)}) %all-to-all-start.1) | async-done | bytes 917536 | tf_op jit(solution)/shard_map/all_to_all | solution.py:625
  62.8 11.9 %shard_map.149 = (bf16[32,112,128]{2,1,0:T(8,128)(2,1)}, bf16[7,128,512]{2,1,0:T(8,128)(2,1)}, bf16[13,128,512]{2,1,0:T(8,128)(2,1)}, bf16[13,128,512]{2,1,0:T(8,128)(2,1)}) custom-call(s32[2]{0:T(128)} %pad_add_fusion.place_ref, s32[3584]{0:T(1024)} %bitcast.28, bf16[32,112,128]{2,1,0:T(8,128)(2,1)} %all-to-all-done.1.rows_ref, ...), custom_call_target="tpu_custom_call" | custom-call | flops 15399999488 | bytes 1048576 | tf_op jit(solution)/shard_map/pallas_call | solution.py:698
  74.7 0.1 collective-permute-start
  74.8 8.0 %all-to-all-start.2 = ((bf16[32,112,128]{2,1,0:T(8,128)(2,1)}), bf16[32,112,128]{2,1,0:T(8,128)(2,1)}, u32[]{:S(2)}, u32[]{:S(2)}) async-start(bf16[32,112,128]{2,1,0:T(8,128)(2,1)} %get-tuple-element.66), calls=%async_computation.2 | async-start | bytes 1835008 | tf_op jit(solution)/shard_map/all_to_all | solution.py:625
  82.8 0.0 collective-permute-done.took_ref
  82.8 2.7 %shard_map.150 = (f32[1024,128]{1,0:T(8,128)S(1)}, bf16[1024,128]{1,0:T(8,128)(2,1)S(1)}, bf16[1024,128]{1,0:T(8,128)(2,1)S(1)}, bf16[1024,128]{1,0:T(8,128)(2,1)S(1)}) custom-call(s32[2]{0:T(128)S(1)} %copy-done.12, bf16[13,128,512]{2,1,0:T(8,128)(2,1)S(1)} %copy-done.17, bf16[13,128,512]{2,1,0:T(8,128)(2,1)S(1)} %collective-permute-done.took_ref), custom_call_target="tpu_custom_call" | custom-call | flops 4400000000 | bytes 1048576 | tf_op jit(solution)/shard_map/pallas_call | solution.py:740
  85.6 1.6 collective-permute-start.1
  87.2 2.7 %collective-permute-start.2 = (bf16[1024,128]{1,0:T(8,128)(2,1)S(1)}, bf16[1024,128]{1,0:T(8,128)(2,1)S(1)}, u32[]{:S(2)}, u32[]{:S(2)}) collective-permute-start(bf16[1024,128]{1,0:T(8,128)(2,1)S(1)} %get-tuple-element.71), channel_id=1, source_target_pairs={{0,4},{1,5},{2,6},{3,7},{4,0},{5,1},{6,2},{7,3},{8,12},{9,13},{10,... | collective-permute-start | bytes 786440 | tf_op jit(solution)/shard_map/ppermute | solution.py:621
  89.9 1.4 collective-permute-start.3
  91.3 3.8 %collective-permute-done.1 = bf16[1024,128]{1,0:T(8,128)(2,1)S(1)} collective-permute-done((bf16[1024,128]{1,0:T(8,128)(2,1)S(1)}, bf16[1024,128]{1,0:T(8,128)(2,1)S(1)}, u32[]{:S(2)}, u32[]{:S(2)}) %collective-permute-start.1) | collective-permute-done | bytes 262176 | tf_op jit(solution)/shard_map/ppermute | solution.py:621
  95.1 5.4 %collective-permute-done.2 = bf16[1024,128]{1,0:T(8,128)(2,1)S(1)} collective-permute-done((bf16[1024,128]{1,0:T(8,128)(2,1)S(1)}, bf16[1024,128]{1,0:T(8,128)(2,1)S(1)}, u32[]{:S(2)}, u32[]{:S(2)}) %collective-permute-start.2) | collective-permute-done | bytes 262176 | tf_op jit(solution)/shard_map/ppermute | solution.py:621
  100.6 0.0 collective-permute-done.3
  100.6 0.8 add_convert_fusion
  101.4 5.4 %all-to-all-done.2.rows_ref = bf16[32,112,128]{2,1,0:T(8,128)(2,1)} async-done(((bf16[32,112,128]{2,1,0:T(8,128)(2,1)}), bf16[32,112,128]{2,1,0:T(8,128)(2,1)}, u32[]{:S(2)}, u32[]{:S(2)}) %all-to-all-start.2) | async-done | bytes 917536 | tf_op jit(solution)/shard_map/all_to_all | solution.py:625
  106.8 7.5 %all-to-all-start.3 = ((bf16[32,32,128]{2,1,0:T(8,128)(2,1)}), bf16[32,32,128]{2,1,0:T(8,128)(2,1)S(1)}, u32[]{:S(2)}, u32[]{:S(2)}) async-start(bf16[32,32,128]{2,1,0:T(8,128)(2,1)} %bitcast.12), calls=%async_computation.3 | async-start | bytes 524288 | tf_op jit(solution)/shard_map/all_to_all | solution.py:625
  114.3 13.6 %shard_map.151 = (bf16[2,1024,128]{2,1,0:T(8,128)(2,1)}, bf16[2,2,1024,128]{3,2,1,0:T(8,128)(2,1)}, bf16[2,1024,128]{2,1,0:T(8,128)(2,1)}, bf16[2,1024,128]{2,1,...) custom-call(s32[2]{0:T(128)} %pad_add_fusion.place_ref, s32[8192]{0:T(1024)} %bitcast.21, ...), custom_call_target="tpu_custom_call" | custom-call | flops 22000001024 | bytes 1048576 | tf_op jit(solution)/shard_map/pallas_call | solution.py:755
  128.0 0.1 collective-permute-start.4
  128.1 0.6 collective-permute-start.5
  128.7 1.3 collective-permute-done.5.theirs_ref
  130.0 0.2 collective-permute-done.4.taken_ref
  130.2 0.0 copy-start.19
  130.2 0.0 copy-start.26
  130.2 0.7 shard_map.153
  130.9 0.5 copy-done.28
  131.4 0.1 collective-permute-start.8
  131.6 0.4 collective-permute-start.9
  131.9 2.7 %collective-permute-start.6 = (bf16[1152,128]{1,0:T(8,128)(2,1)S(1)}, bf16[1152,128]{1,0:T(8,128)(2,1)S(1)}, u32[]{:S(2)}, u32[]{:S(2)}) collective-permute-start(bf16[1152,128]{1,0:T(8,128)(2,1)S(1)} %get-tuple-element.100.own_ref), channel_id=1, source_target_pairs={{0,2},{1,3},{2,4},{3,5},{4,6},{5,7},{6,0},{7,1},{8,10},{9,11},{10,... | collective-permute-start | bytes 884744 | tf_op jit(solution)/shard_map/ppermute | solution.py:621
  134.6 0.5 collective-permute-start.7
  135.2 3.0 %shard_map.154 = f32[128,256]{1,0:T(8,128)} custom-call(bf16[128,512]{1,0:T(8,128)(2,1)S(1)} %copy-done.26, bf16[7,128,512]{2,1,0:T(8,128)(2,1)S(1)} %copy-done.23, bf16[8,128,512]{2,1,0:T(8,128)(2,1)S(1)} %copy-done.19), custom_call_target="tpu_custom_call" | custom-call | flops 4400000000 | bytes 1048576 | tf_op jit(solution)/shard_map/pallas_call | solution.py:792
  138.2 4.0 %collective-permute-done.6.below_ref.before_ref = bf16[1152,128]{1,0:T(8,128)(2,1)S(1)} collective-permute-done((bf16[1152,128]{1,0:T(8,128)(2,1)S(1)}, bf16[1152,128]{1,0:T(8,128)(2,1)S(1)}, u32[]{:S(2)}, u32[]{:S(2)}) %collective-permute-start.6) | collective-permute-done | bytes 294944 | tf_op jit(solution)/shard_map/ppermute | solution.py:621
  142.2 1.2 collective-permute-done.7.above_ref.next_ref
  143.4 0.0 collective-permute-done.9.taken_ref
  143.4 0.0 collective-permute-done.8.taken_ref
  143.4 0.3 shard_map.155
  143.8 0.5 collective-permute-start.10
  144.3 2.8 %collective-permute-start.11 = (bf16[2048,128]{1,0:T(8,128)(2,1)S(1)}, bf16[2048,128]{1,0:T(8,128)(2,1)S(1)}, u32[]{:S(2)}, u32[]{:S(2)}) collective-permute-start(bf16[2048,128]{1,0:T(8,128)(2,1)S(1)} %get-tuple-element.99), channel_id=1, source_target_pairs={{0,6},{1,7},{2,0},{3,1},{4,2},{5,3},{6,4},{7,5},{8,14},{9,15},{10,... | collective-permute-start | bytes 1572872 | tf_op jit(solution)/shard_map/ppermute | solution.py:621
  147.1 0.1 shard_map.156.pair_ref
  147.2 10.0 %collective-permute-done.11.above_ref = bf16[2048,128]{1,0:T(8,128)(2,1)S(1)} collective-permute-done((bf16[2048,128]{1,0:T(8,128)(2,1)S(1)}, bf16[2048,128]{1,0:T(8,128)(2,1)S(1)}, u32[]{:S(2)}, u32[]{:S(2)}) %collective-permute-start.11) | collective-permute-done | bytes 524320 | tf_op jit(solution)/shard_map/ppermute | solution.py:621
  157.1 1.4 collective-permute-done.10.below_ref
  158.6 1.9 %shard_map.157 = (f32[64,4096]{1,0:T(8,128)}, f32[32,512]{1,0:T(8,128)}, f32[8,512]{1,0:T(8,128)}, f32[16,512]{1,0:T(8,128)}) custom-call(s32[2]{0:T(128)S(1)} %copy-done.13, f32[2,1024,128]{2,1,0:T(8,128)S(1)} %shard_map.156.pair_ref, bf16[2176,128]{1,0:T(8,128)(2,1)S(1)} %collective-permute-done.10.below_ref, ...), custom_call_target="tpu_custom_call" | custom-call | flops 2200000000 | bytes 1048576 | tf_op jit(solution)/shard_map/pallas_call | solution.py:814
  (45 shorter events, 0.2 us)
Async XLA Ops:
  0.6 0.7 copy-start.9
  1.3 0.7 copy-start.10
  2.1 21.6 %copy-start.3 = (bf16[32768,64]{0,1:T(8,128)(2,1)S(1)}, bf16[32768,64]{0,1:T(8,128)(2,1)}, u32[]{:S(2)}) copy-start(bf16[32768,64]{0,1:T(8,128)(2,1)} %param.13) | copy-start | bytes 12582916
  3.3 20.3 %copy-start.11 = (s32[28,128]{1,0:T(8,128)}, s32[28,128]{1,0:T(8,128)S(1)}, u32[]{:S(2)}) copy-start(s32[28,128]{1,0:T(8,128)S(1)} %get-tuple-element.56) | copy-start | bytes 43012
  23.6 11.1 %copy-start = (s32[32,1,256]{2,0,1:T(8,128)}, s32[32,1,256]{2,0,1:T(8,128)S(1)}, u32[]{:S(2)}) copy-start(s32[32,1,256]{2,0,1:T(8,128)S(1)} %copy.22) | copy-start | bytes 98308
  23.7 11.0 %copy-start.1 = (s32[32,1,256]{2,1,0:T(1,128)}, s32[32,1,256]{2,1,0:T(1,128)S(1)}, u32[]{:S(2)}) copy-start(s32[32,1,256]{2,1,0:T(1,128)S(1)} %broadcast_and_fusion) | copy-start | bytes 98308
  34.7 6.0 %copy-start.27 = (s32[128,7,4]{0,2,1:T(4,128)S(1)}, s32[128,7,4]{0,2,1:T(4,128)}, u32[]{:S(2)}) copy-start(s32[128,7,4]{0,2,1:T(4,128)} %param.18) | copy-start | bytes 43012
  34.7 6.6 %copy-start.2 = (s32[256]{0:T(256)S(1)}, s32[256]{0:T(256)}, u32[]{:S(2)}) copy-start(s32[256]{0:T(256)} %param.19) | copy-start | bytes 3076
  34.7 7.3 %copy-start.4 = (bf16[1024,512]{1,0:T(8,128)(2,1)S(1)}, bf16[1024,512]{1,0:T(8,128)(2,1)}, u32[]{:S(2)}) copy-start(bf16[1024,512]{1,0:T(8,128)(2,1)} %hot_ref.1) | copy-start | bytes 3145732
  34.7 7.3 %copy-start.5 = (bf16[512,512]{1,0:T(8,128)(2,1)S(1)}, bf16[512,512]{1,0:T(8,128)(2,1)}, u32[]{:S(2)}) copy-start(bf16[512,512]{1,0:T(8,128)(2,1)} %weight_ref.1) | copy-start | bytes 1572868
  34.7 7.3 %copy-start.6 = (f32[128,256]{1,0:T(8,128)S(1)}, f32[128,256]{1,0:T(8,128)}, u32[]{:S(2)}) copy-start(f32[128,256]{1,0:T(8,128)} %grad_ref.1) | copy-start | bytes 393220
  34.7 7.3 %copy-start.7 = (bf16[128,512]{1,0:T(8,128)(2,1)S(1)}, bf16[128,512]{1,0:T(8,128)(2,1)}, u32[]{:S(2)}) copy-start(bf16[128,512]{1,0:T(8,128)(2,1)} %dense_ref.3) | copy-start | bytes 393220
  34.8 7.3 %copy-start.8 = (s32[128,8,4]{0,2,1:T(4,128)S(1)}, s32[128,8,4]{0,2,1:T(4,128)}, u32[]{:S(2)}) copy-start(s32[128,8,4]{0,2,1:T(4,128)} %param.20) | copy-start | bytes 49156
  34.8 28.0 %all-to-all-start.1 = ((bf16[32,112,128]{2,1,0:T(8,128)(2,1)}), bf16[32,112,128]{2,1,0:T(8,128)(2,1)}, u32[]{:S(2)}, u32[]{:S(2)}) async-start(bf16[32,112,128]{2,1,0:T(8,128)(2,1)} %shard_map.147), calls=%async_computation.1 | async-start | bytes 1835008 | tf_op jit(solution)/shard_map/all_to_all | solution.py:625
  44.7 1.0 copy-start.18
  45.6 1.0 copy-start.20
  46.6 1.0 copy-start.21
  47.6 0.9 copy-start.22
  48.5 0.7 copy-start.24
  49.2 0.7 copy-start.25
  74.7 8.1 %copy-start.12 = (s32[2]{0:T(128)S(1)}, s32[2]{0:T(128)}, u32[]{:S(2)}) copy-start(s32[2]{0:T(128)} %pad_add_fusion.place_ref) | copy-start | bytes 28
  74.7 8.1 %copy-start.17 = (bf16[13,128,512]{2,1,0:T(8,128)(2,1)S(1)}, bf16[13,128,512]{2,1,0:T(8,128)(2,1)}, u32[]{:S(2)}) copy-start(bf16[13,128,512]{2,1,0:T(8,128)(2,1)} %get-tuple-element.67.keep_ref) | copy-start | bytes 5111812
  74.7 8.1 %collective-permute-start = (bf16[13,128,512]{2,1,0:T(8,128)(2,1)}, bf16[13,128,512]{2,1,0:T(8,128)(2,1)S(1)}, u32[]{:S(2)}, u32[]{:S(2)}) collective-permute-start(bf16[13,128,512]{2,1,0:T(8,128)(2,1)} %get-tuple-element.68), channel_id=1, source_target_pairs={{0,1},{1,0},{2,3},{3,2},{4,5},{5,4},{6,7},{7,6},{8,9},{9,8},{10,11... | collective-permute-start | bytes 5111816 | tf_op jit(solution)/shard_map/ppermute | solution.py:617
  74.8 31.9 %all-to-all-start.2 = ((bf16[32,112,128]{2,1,0:T(8,128)(2,1)}), bf16[32,112,128]{2,1,0:T(8,128)(2,1)}, u32[]{:S(2)}, u32[]{:S(2)}) async-start(bf16[32,112,128]{2,1,0:T(8,128)(2,1)} %get-tuple-element.66), calls=%async_computation.2 | async-start | bytes 1835008 | tf_op jit(solution)/shard_map/all_to_all | solution.py:625
  85.6 9.5 %collective-permute-start.1 = (bf16[1024,128]{1,0:T(8,128)(2,1)S(1)}, bf16[1024,128]{1,0:T(8,128)(2,1)S(1)}, u32[]{:S(2)}, u32[]{:S(2)}) collective-permute-start(bf16[1024,128]{1,0:T(8,128)(2,1)S(1)} %get-tuple-element.70), channel_id=1, source_target_pairs={{0,2},{1,3},{2,4},{3,5},{4,6},{5,7},{6,0},{7,1},{8,10},{9,11},{10,... | collective-permute-start | bytes 786440 | tf_op jit(solution)/shard_map/ppermute | solution.py:621
  87.2 13.4 %collective-permute-start.2 = (bf16[1024,128]{1,0:T(8,128)(2,1)S(1)}, bf16[1024,128]{1,0:T(8,128)(2,1)S(1)}, u32[]{:S(2)}, u32[]{:S(2)}) collective-permute-start(bf16[1024,128]{1,0:T(8,128)(2,1)S(1)} %get-tuple-element.71), channel_id=1, source_target_pairs={{0,4},{1,5},{2,6},{3,7},{4,0},{5,1},{6,2},{7,3},{8,12},{9,13},{10,... | collective-permute-start | bytes 786440 | tf_op jit(solution)/shard_map/ppermute | solution.py:621
  89.9 10.7 %collective-permute-start.3 = (bf16[1024,128]{1,0:T(8,128)(2,1)S(1)}, bf16[1024,128]{1,0:T(8,128)(2,1)S(1)}, u32[]{:S(2)}, u32[]{:S(2)}) collective-permute-start(bf16[1024,128]{1,0:T(8,128)(2,1)S(1)} %get-tuple-element.72), channel_id=1, source_target_pairs={{0,6},{1,7},{2,0},{3,1},{4,2},{5,3},{6,4},{7,5},{8,14},{9,15},{10,... | collective-permute-start | bytes 786440 | tf_op jit(solution)/shard_map/ppermute | solution.py:621
  106.8 21.2 %all-to-all-start.3 = ((bf16[32,32,128]{2,1,0:T(8,128)(2,1)}), bf16[32,32,128]{2,1,0:T(8,128)(2,1)S(1)}, u32[]{:S(2)}, u32[]{:S(2)}) async-start(bf16[32,32,128]{2,1,0:T(8,128)(2,1)} %bitcast.12), calls=%async_computation.3 | async-start | bytes 524288 | tf_op jit(solution)/shard_map/all_to_all | solution.py:625
  128.0 2.2 %copy-start.13 = (s32[2]{0:T(128)S(1)}, s32[2]{0:T(128)}, u32[]{:S(2)}) copy-start(s32[2]{0:T(128)} %pad_add_fusion.place_ref) | copy-start | bytes 28
  128.0 2.2 %copy-start.15 = (bf16[2,1024,128]{2,1,0:T(8,128)(2,1)S(1)}, bf16[2,1024,128]{2,1,0:T(8,128)(2,1)}, u32[]{:S(2)}) copy-start(bf16[2,1024,128]{2,1,0:T(8,128)(2,1)} %get-tuple-element.74.kept_ref) | copy-start | bytes 1572868
  128.0 2.2 %collective-permute-start.4 = (bf16[2,1024,128]{2,1,0:T(8,128)(2,1)}, bf16[2,1024,128]{2,1,0:T(8,128)(2,1)S(1)}, u32[]{:S(2)}, u32[]{:S(2)}) collective-permute-start(bf16[2,1024,128]{2,1,0:T(8,128)(2,1)} %get-tuple-element.77), channel_id=1, source_target_pairs={{0,1},{1,0},{2,3},{3,2},{4,5},{5,4},{6,7},{7,6},{8,9},{9,8},{10,11... | collective-permute-start | bytes 1572872 | tf_op jit(solution)/shard_map/ppermute | solution.py:617
  128.1 1.9 %collective-permute-start.5 = (bf16[64,128]{1,0:T(8,128)(2,1)S(1)}, bf16[64,128]{1,0:T(8,128)(2,1)S(1)}, u32[]{:S(2)}, u32[]{:S(2)}) collective-permute-start(bf16[64,128]{1,0:T(8,128)(2,1)S(1)} %shard_map.152.mine_ref), channel_id=1, source_target_pairs={{0,1},{1,0},{2,3},{3,2},{4,5},{5,4},{6,7},{7,6},{8,9},{9,8},{10,11... | collective-permute-start | bytes 49160 | tf_op jit(solution)/shard_map/ppermute | solution.py:617
  130.2 1.2 copy-start.28
  130.2 1.4 copy-start.29
  130.2 5.0 %copy-start.19 = (bf16[8,128,512]{2,1,0:T(8,128)(2,1)S(1)}, bf16[8,128,512]{2,1,0:T(8,128)(2,1)}, u32[]{:S(2)}) copy-start(bf16[8,128,512]{2,1,0:T(8,128)(2,1)} %copy-done.18) | copy-start | bytes 3145732
  130.2 5.0 %copy-start.23 = (bf16[7,128,512]{2,1,0:T(8,128)(2,1)S(1)}, bf16[7,128,512]{2,1,0:T(8,128)(2,1)}, u32[]{:S(2)}) copy-start(bf16[7,128,512]{2,1,0:T(8,128)(2,1)} %get-tuple-element.86.cold_ref) | copy-start | bytes 2752516
  130.2 5.0 %copy-start.26 = (bf16[128,512]{1,0:T(8,128)(2,1)S(1)}, bf16[128,512]{1,0:T(8,128)(2,1)}, u32[]{:S(2)}) copy-start(bf16[128,512]{1,0:T(8,128)(2,1)} %copy-done.25) | copy-start | bytes 393220
  131.4 12.0 %copy-start.14 = (bf16[2,2,1024,128]{3,2,1,0:T(8,128)(2,1)S(1)}, bf16[2,2,1024,128]{3,2,1,0:T(8,128)(2,1)}, u32[]{:S(2)}) copy-start(bf16[2,2,1024,128]{3,2,1,0:T(8,128)(2,1)} %get-tuple-element.88.kept_ref) | copy-start | bytes 3145732
  131.4 12.0 %collective-permute-start.8 = (bf16[2,2,1024,128]{3,2,1,0:T(8,128)(2,1)S(1)}, bf16[2,2,1024,128]{3,2,1,0:T(8,128)(2,1)S(1)}, u32[]{:S(2)}, u32[]{:S(2)}) collective-permute-start(bf16[2,2,1024,128]{3,2,1,0:T(8,128)(2,1)S(1)} %copy-done.28), channel_id=1, source_target_pairs={{0,1},{1,0},{2,3},{3,2},{4,5},{5,4},{6,7},{7,6},{8,9},{9,8},{10,11... | collective-permute-start | bytes 3145736 | tf_op jit(solution)/shard_map/ppermute | solution.py:617
  131.6 11.9 %collective-permute-start.9 = (bf16[2,1024,128]{2,1,0:T(8,128)(2,1)S(1)}, bf16[2,1024,128]{2,1,0:T(8,128)(2,1)S(1)}, u32[]{:S(2)}, u32[]{:S(2)}) collective-permute-start(bf16[2,1024,128]{2,1,0:T(8,128)(2,1)S(1)} %copy-done.29), channel_id=1, source_target_pairs={{0,1},{1,0},{2,3},{3,2},{4,5},{5,4},{6,7},{7,6},{8,9},{9,8},{10,11... | collective-permute-start | bytes 1572872 | tf_op jit(solution)/shard_map/ppermute | solution.py:617
  131.9 10.3 %collective-permute-start.6 = (bf16[1152,128]{1,0:T(8,128)(2,1)S(1)}, bf16[1152,128]{1,0:T(8,128)(2,1)S(1)}, u32[]{:S(2)}, u32[]{:S(2)}) collective-permute-start(bf16[1152,128]{1,0:T(8,128)(2,1)S(1)} %get-tuple-element.100.own_ref), channel_id=1, source_target_pairs={{0,2},{1,3},{2,4},{3,5},{4,6},{5,7},{6,0},{7,1},{8,10},{9,11},{10,... | collective-permute-start | bytes 884744 | tf_op jit(solution)/shard_map/ppermute | solution.py:621
  134.6 8.8 %collective-permute-start.7 = (bf16[1152,128]{1,0:T(8,128)(2,1)S(1)}, bf16[1152,128]{1,0:T(8,128)(2,1)S(1)}, u32[]{:S(2)}, u32[]{:S(2)}) collective-permute-start(bf16[1152,128]{1,0:T(8,128)(2,1)S(1)} %get-tuple-element.80), channel_id=1, source_target_pairs={{0,6},{1,7},{2,0},{3,1},{4,2},{5,3},{6,4},{7,5},{8,14},{9,15},{10,... | collective-permute-start | bytes 884744 | tf_op jit(solution)/shard_map/ppermute | solution.py:621
  143.4 3.6 %copy-start.16 = (f32[2,1024,128]{2,1,0:T(8,128)S(1)}, f32[2,1024,128]{2,1,0:T(8,128)}, u32[]{:S(2)}) copy-start(f32[2,1024,128]{2,1,0:T(8,128)} %get-tuple-element.96.kept_ref) | copy-start | bytes 3145732
  143.8 14.8 %collective-permute-start.10 = (bf16[2176,128]{1,0:T(8,128)(2,1)S(1)}, bf16[2176,128]{1,0:T(8,128)(2,1)S(1)}, u32[]{:S(2)}, u32[]{:S(2)}) collective-permute-start(bf16[2176,128]{1,0:T(8,128)(2,1)S(1)} %get-tuple-element.98), channel_id=1, source_target_pairs={{0,2},{1,3},{2,4},{3,5},{4,6},{5,7},{6,0},{7,1},{8,10},{9,11},{10,... | collective-permute-start | bytes 1671176 | tf_op jit(solution)/shard_map/ppermute | solution.py:621
  144.3 12.8 %collective-permute-start.11 = (bf16[2048,128]{1,0:T(8,128)(2,1)S(1)}, bf16[2048,128]{1,0:T(8,128)(2,1)S(1)}, u32[]{:S(2)}, u32[]{:S(2)}) collective-permute-start(bf16[2048,128]{1,0:T(8,128)(2,1)S(1)} %get-tuple-element.99), channel_id=1, source_target_pairs={{0,6},{1,7},{2,0},{3,1},{4,2},{5,3},{6,4},{7,5},{8,14},{9,15},{10,... | collective-permute-start | bytes 1572872 | tf_op jit(solution)/shard_map/ppermute | solution.py:621

commit v7 on v6

--- a/solution.py
+++ b/solution.py
@@ -541,8 +541,7 @@
 
 
 def dense_kernel(rows_ref, out_ref):
-    rows = rows_ref.shape[1]
-    out_ref[:rows], out_ref[rows:] = split_two(sum_rows(rows_ref))
+    out_ref[...] = sum_rows(rows_ref).astype(BF16)
 
 
 def add_pair(kept, taken):
@@ -607,8 +606,8 @@
         chunk = (place_ref[0] + k) % len(tails)
         at = pl.ds(pl.multiple_of(chunk * LANES, LANES), LANES)
         rows = tail.astype(F32)
-        hot_ref[:, at] = rows[:32] + rows[32:64]
-        rest = rows[64:96] + rows[96:]
+        hot_ref[:, at] = rows[:32]
+        rest = rows[32:]
         bottom_ref[:, at] = rest[:16]
         proj_ref[:, at] = rest[16:24]
 
@@ -776,10 +775,10 @@
         vmem=62,
     )(place, row_ids, asked, returned)
     given_far, dense_all = lax.optimization_barrier((given_far, dense_all))
-    mine = call(dense_kernel, shape((64, LANES), BF16))(dense_all)
+    mine = call(dense_kernel, shape((32, LANES), BF16))(dense_all)
     taken_far = to_other_core(given_far)
     theirs = to_other_core(mine)
-    up, down = call(far_kernel, (shape((half + 128, LANES), BF16),) * 2, specs=[SMEM] + [VMEM] * 4)(
+    up, down = call(far_kernel, (shape((half + 64, LANES), BF16),) * 2, specs=[SMEM] + [VMEM] * 4)(
         place, kept_far, taken_far, mine, theirs
     )
     from_below = along_x(up, 1)
@@ -803,7 +802,7 @@
     )
     next_up, next_down = call(
         second_kernel,
-        (shape((2 * half + 128, LANES), BF16), shape((2 * half, LANES), BF16)),
+        (shape((2 * half + 64, LANES), BF16), shape((2 * half, LANES), BF16)),
     )(kept_near, taken_near, from_below, from_above)
     next_up, next_down, kept_own, taken_own = lax.optimization_barrier(
         (next_up, next_down, kept_own, taken_own)

time: 161 us -> 160 us (level)
  transfers between devices with their start and end apart: 15 -> 15, of which waited for: 10 -> 9; matrix products, arithmetic and copies ran while one was open for 1% -> 1% of each run, Pallas kernels for 14% -> 14%
where the time goes in v7:
time: 160 us; the launch traced here: 159 us
  Pallas kernels  49.2 us (31%)
  waiting for transfers between devices  44 us (28%)
  starting transfers between devices  34.9 us (22%)
  blocking collectives  20.3 us (13%)
  local copies, waits for them, and re-layouts  7.92 us (5%)
    ppermute x7, waiting for transfers between devices, along_x(): return lax.ppermute(x, 'dp', [(i, (i + 2 * steps) % 8) for i in range(8)])  24.2 us
    all_to_all x3, starting transfers between devices, exchange(): return lax.all_to_all(x, axis, split_axis=0, concat_axis=0, tiled=True)  21.4 us
    all_to_all x1, blocking collectives, exchange(): return lax.all_to_all(x, axis, split_axis=0, concat_axis=0, tiled=True)  20.3 us
    all_to_all x3, waiting for transfers between devices, exchange(): return lax.all_to_all(x, axis, split_axis=0, concat_axis=0, tiled=True)  18.3 us
    pallas_call x1, Pallas kernels, shards(): call(add_kernel, (shape((2, half, LANES), BF16), shape((2, 2, half, LANES...  13.6 us
    ppermute x7, starting transfers between devices, along_x(): return lax.ppermute(x, 'dp', [(i, (i + 2 * steps) % 8) for i in range(8)])  12.3 us
    pallas_call x1, Pallas kernels, shards(): call(main_kernel, (shape((tables, pairs, LANES), BF16), shape((cold_feats...  11.9 us
    pallas_call x1, Pallas kernels, shards(): call(gather_kernel, shape((tables, pairs, LANES), BF16), scratch=[pltpu.V...  11 us
  transfers between devices with their start and end apart: 15, of which 9 were waited for; matrix products, arithmetic and copies ran while one was open for 1% of the time, Pallas kernels for 14%

profile of v7, /device:TPU:8, one launch (start us, length us, event | category | flops | bytes accessed | tf_op | source)
XLA Modules:
  0.0 158.8 jit_solution(2853568096804038762)
XLA Ops:
  0.6 0.7 copy-done.9
  1.3 0.7 copy-done.10
  2.1 1.2 shard_map.146
  3.3 0.0 copy-start.11
  3.3 20.3 %all_to_all.20 = s32[32,1,256]{2,1,0:T(1,128)S(1)} all-to-all(s32[32,1,256]{2,1,0:T(1,128)S(1)} %get-tuple-element.55), channel_id=1, replica_groups=mesh['table'=32,'dp'=8] {'table'}, dimensions={0} | all-to-all | bytes 65536 | tf_op jit(solution)/shard_map/all_to_all | solution.py:624
  23.7 0.0 copy-start.1
  23.7 11.0 %shard_map.147 = bf16[32,112,128]{2,1,0:T(8,128)(2,1)} custom-call(s32[8192]{0:T(1024)S(1)} %bitcast.20, s32[32,256]{1,0:T(8,128)S(1)} %bitcast.18, bf16[64,32768]{1,0:T(8,128)(2,1)S(1)} %bitcast.24), custom_call_target="tpu_custom_call" | custom-call | flops 13200000000 | bytes 1048576 | tf_op jit(solution)/shard_map/pallas_call | solution.py:665
  34.7 0.0 copy-start.4
  34.7 0.0 copy-start.5
  34.7 0.0 copy-start.6
  34.7 0.0 copy-start.7
  34.8 0.0 copy-start.8
  34.8 5.9 %all-to-all-start.1 = ((bf16[32,112,128]{2,1,0:T(8,128)(2,1)}), bf16[32,112,128]{2,1,0:T(8,128)(2,1)}, u32[]{:S(2)}, u32[]{:S(2)}) async-start(bf16[32,112,128]{2,1,0:T(8,128)(2,1)} %shard_map.147), calls=%async_computation.1 | async-start | bytes 1835008 | tf_op jit(solution)/shard_map/all_to_all | solution.py:624
  40.7 0.6 reshape.40.band_ref
  41.3 0.1 copy.19.unique_ref
  41.5 0.6 pad_add_fusion.place_ref
  42.1 2.6 %shard_map.148 = (f32[128,512]{1,0:T(8,128)S(1)}, bf16[128,512]{1,0:T(8,128)(2,1)S(1)}, bf16[8,128,512]{2,1,0:T(8,128)(2,1)S(1)}, bf16[5,128,512]{2,1,0:T(8,128)...) custom-call(bf16[128,512]{1,0:T(8,128)(2,1)S(1)} %copy-done.7, ...), custom_call_target="tpu_custom_call" | custom-call | flops 3300000000 | bytes 1048576 | tf_op jit(solution)/shard_map/pallas_call | solution.py:675
  44.7 0.0 copy-start.18
  44.7 1.0 copy-done.18
  45.6 1.0 copy-done.20
  46.6 1.0 copy-done.21
  47.6 0.8 copy-done.22
  48.5 0.7 copy-done.24
  49.2 0.7 copy-done.25
  49.8 12.9 %all-to-all-done.1.rows_ref = bf16[32,112,128]{2,1,0:T(8,128)(2,1)} async-done(((bf16[32,112,128]{2,1,0:T(8,128)(2,1)}), bf16[32,112,128]{2,1,0:T(8,128)(2,1)}, u32[]{:S(2)}, u32[]{:S(2)}) %all-to-all-start.1) | async-done | bytes 917536 | tf_op jit(solution)/shard_map/all_to_all | solution.py:624
  62.8 11.9 %shard_map.149 = (bf16[32,112,128]{2,1,0:T(8,128)(2,1)}, bf16[7,128,512]{2,1,0:T(8,128)(2,1)}, bf16[13,128,512]{2,1,0:T(8,128)(2,1)}, bf16[13,128,512]{2,1,0:T(8,128)(2,1)}) custom-call(s32[2]{0:T(128)} %pad_add_fusion.place_ref, s32[3584]{0:T(1024)} %bitcast.28, bf16[32,112,128]{2,1,0:T(8,128)(2,1)} %all-to-all-done.1.rows_ref, ...), custom_call_target="tpu_custom_call" | custom-call | flops 15399999488 | bytes 1048576 | tf_op jit(solution)/shard_map/pallas_call | solution.py:697
  74.7 0.1 collective-permute-start
  74.8 8.0 %all-to-all-start.2 = ((bf16[32,112,128]{2,1,0:T(8,128)(2,1)}), bf16[32,112,128]{2,1,0:T(8,128)(2,1)}, u32[]{:S(2)}, u32[]{:S(2)}) async-start(bf16[32,112,128]{2,1,0:T(8,128)(2,1)} %get-tuple-element.66), calls=%async_computation.2 | async-start | bytes 1835008 | tf_op jit(solution)/shard_map/all_to_all | solution.py:624
  82.8 0.0 collective-permute-done.took_ref
  82.8 2.7 %shard_map.150 = (f32[1024,128]{1,0:T(8,128)S(1)}, bf16[1024,128]{1,0:T(8,128)(2,1)S(1)}, bf16[1024,128]{1,0:T(8,128)(2,1)S(1)}, bf16[1024,128]{1,0:T(8,128)(2,1)S(1)}) custom-call(s32[2]{0:T(128)S(1)} %copy-done.12, bf16[13,128,512]{2,1,0:T(8,128)(2,1)S(1)} %copy-done.17, bf16[13,128,512]{2,1,0:T(8,128)(2,1)S(1)} %collective-permute-done.took_ref), custom_call_target="tpu_custom_call" | custom-call | flops 4400000000 | bytes 1048576 | tf_op jit(solution)/shard_map/pallas_call | solution.py:739
  85.6 1.6 collective-permute-start.1
  87.2 2.7 %collective-permute-start.2 = (bf16[1024,128]{1,0:T(8,128)(2,1)S(1)}, bf16[1024,128]{1,0:T(8,128)(2,1)S(1)}, u32[]{:S(2)}, u32[]{:S(2)}) collective-permute-start(bf16[1024,128]{1,0:T(8,128)(2,1)S(1)} %get-tuple-element.71), channel_id=1, source_target_pairs={{0,4},{1,5},{2,6},{3,7},{4,0},{5,1},{6,2},{7,3},{8,12},{9,13},{10,... | collective-permute-start | bytes 786440 | tf_op jit(solution)/shard_map/ppermute | solution.py:620
  89.9 1.4 collective-permute-start.3
  91.3 3.8 %collective-permute-done.1 = bf16[1024,128]{1,0:T(8,128)(2,1)S(1)} collective-permute-done((bf16[1024,128]{1,0:T(8,128)(2,1)S(1)}, bf16[1024,128]{1,0:T(8,128)(2,1)S(1)}, u32[]{:S(2)}, u32[]{:S(2)}) %collective-permute-start.1) | collective-permute-done | bytes 262176 | tf_op jit(solution)/shard_map/ppermute | solution.py:620
  95.1 5.4 %collective-permute-done.2 = bf16[1024,128]{1,0:T(8,128)(2,1)S(1)} collective-permute-done((bf16[1024,128]{1,0:T(8,128)(2,1)S(1)}, bf16[1024,128]{1,0:T(8,128)(2,1)S(1)}, u32[]{:S(2)}, u32[]{:S(2)}) %collective-permute-start.2) | collective-permute-done | bytes 262176 | tf_op jit(solution)/shard_map/ppermute | solution.py:620
  100.6 0.0 collective-permute-done.3
  100.6 0.8 add_convert_fusion
  101.4 5.4 %all-to-all-done.2.rows_ref = bf16[32,112,128]{2,1,0:T(8,128)(2,1)} async-done(((bf16[32,112,128]{2,1,0:T(8,128)(2,1)}), bf16[32,112,128]{2,1,0:T(8,128)(2,1)}, u32[]{:S(2)}, u32[]{:S(2)}) %all-to-all-start.2) | async-done | bytes 917536 | tf_op jit(solution)/shard_map/all_to_all | solution.py:624
  106.8 7.5 %all-to-all-start.3 = ((bf16[32,32,128]{2,1,0:T(8,128)(2,1)}), bf16[32,32,128]{2,1,0:T(8,128)(2,1)S(1)}, u32[]{:S(2)}, u32[]{:S(2)}) async-start(bf16[32,32,128]{2,1,0:T(8,128)(2,1)} %bitcast.12), calls=%async_computation.3 | async-start | bytes 524288 | tf_op jit(solution)/shard_map/all_to_all | solution.py:624
  114.3 13.6 %shard_map.151 = (bf16[2,1024,128]{2,1,0:T(8,128)(2,1)}, bf16[2,2,1024,128]{3,2,1,0:T(8,128)(2,1)}, bf16[2,1024,128]{2,1,0:T(8,128)(2,1)}, bf16[2,1024,128]{2,1,...) custom-call(s32[2]{0:T(128)} %pad_add_fusion.place_ref, s32[8192]{0:T(1024)} %bitcast.21, ...), custom_call_target="tpu_custom_call" | custom-call | flops 22000001024 | bytes 1048576 | tf_op jit(solution)/shard_map/pallas_call | solution.py:754
  128.0 0.1 collective-permute-start.4
  128.1 0.6 collective-permute-start.5
  128.7 1.3 collective-permute-done.5.theirs_ref
  130.0 0.2 collective-permute-done.4.taken_ref
  130.2 0.0 copy-start.19
  130.2 0.0 copy-start.26
  130.2 0.7 shard_map.153
  130.9 0.5 copy-done.28
  131.4 0.1 collective-permute-start.8
  131.6 0.4 collective-permute-start.9
  131.9 1.5 collective-permute-start.6
  133.4 1.7 %collective-permute-start.7 = (bf16[1088,128]{1,0:T(8,128)(2,1)S(1)}, bf16[1088,128]{1,0:T(8,128)(2,1)S(1)}, u32[]{:S(2)}, u32[]{:S(2)}) collective-permute-start(bf16[1088,128]{1,0:T(8,128)(2,1)S(1)} %get-tuple-element.80), channel_id=1, source_target_pairs={{0,6},{1,7},{2,0},{3,1},{4,2},{5,3},{6,4},{7,5},{8,14},{9,15},{10,... | collective-permute-start | bytes 835592 | tf_op jit(solution)/shard_map/ppermute | solution.py:620
  135.2 3.0 %shard_map.154 = f32[128,256]{1,0:T(8,128)} custom-call(bf16[128,512]{1,0:T(8,128)(2,1)S(1)} %copy-done.26, bf16[7,128,512]{2,1,0:T(8,128)(2,1)S(1)} %copy-done.23, bf16[8,128,512]{2,1,0:T(8,128)(2,1)S(1)} %copy-done.19), custom_call_target="tpu_custom_call" | custom-call | flops 4400000000 | bytes 1048576 | tf_op jit(solution)/shard_map/pallas_call | solution.py:791
  138.2 3.6 %collective-permute-done.6.below_ref.before_ref = bf16[1088,128]{1,0:T(8,128)(2,1)S(1)} collective-permute-done((bf16[1088,128]{1,0:T(8,128)(2,1)S(1)}, bf16[1088,128]{1,0:T(8,128)(2,1)S(1)}, u32[]{:S(2)}, u32[]{:S(2)}) %collective-permute-start.6) | collective-permute-done | bytes 278560 | tf_op jit(solution)/shard_map/ppermute | solution.py:620
  141.8 0.0 collective-permute-done.7.above_ref.next_ref
  141.8 0.0 collective-permute-done.9.taken_ref
  141.8 0.0 collective-permute-done.8.taken_ref
  141.9 0.3 shard_map.155
  142.2 1.6 collective-permute-start.10
  143.8 1.8 %collective-permute-start.11 = (bf16[2048,128]{1,0:T(8,128)(2,1)S(1)}, bf16[2048,128]{1,0:T(8,128)(2,1)S(1)}, u32[]{:S(2)}, u32[]{:S(2)}) collective-permute-start(bf16[2048,128]{1,0:T(8,128)(2,1)S(1)} %get-tuple-element.99), channel_id=1, source_target_pairs={{0,6},{1,7},{2,0},{3,1},{4,2},{5,3},{6,4},{7,5},{8,14},{9,15},{10,... | collective-permute-start | bytes 1572872 | tf_op jit(solution)/shard_map/ppermute | solution.py:620
  145.5 0.1 shard_map.156.pair_ref
  145.6 10.7 %collective-permute-done.11.above_ref = bf16[2048,128]{1,0:T(8,128)(2,1)S(1)} collective-permute-done((bf16[2048,128]{1,0:T(8,128)(2,1)S(1)}, bf16[2048,128]{1,0:T(8,128)(2,1)S(1)}, u32[]{:S(2)}, u32[]{:S(2)}) %collective-permute-start.11) | collective-permute-done | bytes 524320 | tf_op jit(solution)/shard_map/ppermute | solution.py:620
  156.3 0.7 collective-permute-done.10.below_ref
  157.0 1.9 %shard_map.157 = (f32[64,4096]{1,0:T(8,128)}, f32[32,512]{1,0:T(8,128)}, f32[8,512]{1,0:T(8,128)}, f32[16,512]{1,0:T(8,128)}) custom-call(s32[2]{0:T(128)S(1)} %copy-done.13, f32[2,1024,128]{2,1,0:T(8,128)S(1)} %shard_map.156.pair_ref, bf16[2112,128]{1,0:T(8,128)(2,1)S(1)} %collective-permute-done.10.below_ref, ...), custom_call_target="tpu_custom_call" | custom-call | flops 2200000000 | bytes 1048576 | tf_op jit(solution)/shard_map/pallas_call | solution.py:813
  (45 shorter events, 0.2 us)
Async XLA Ops:
  0.6 0.7 copy-start.9
  1.3 0.7 copy-start.10
  2.1 21.6 %copy-start.3 = (bf16[32768,64]{0,1:T(8,128)(2,1)S(1)}, bf16[32768,64]{0,1:T(8,128)(2,1)}, u32[]{:S(2)}) copy-start(bf16[32768,64]{0,1:T(8,128)(2,1)} %param.13) | copy-start | bytes 12582916
  3.3 20.3 %copy-start.11 = (s32[28,128]{1,0:T(8,128)}, s32[28,128]{1,0:T(8,128)S(1)}, u32[]{:S(2)}) copy-start(s32[28,128]{1,0:T(8,128)S(1)} %get-tuple-element.56) | copy-start | bytes 43012
  23.6 11.1 %copy-start = (s32[32,1,256]{2,0,1:T(8,128)}, s32[32,1,256]{2,0,1:T(8,128)S(1)}, u32[]{:S(2)}) copy-start(s32[32,1,256]{2,0,1:T(8,128)S(1)} %copy.22) | copy-start | bytes 98308
  23.7 11.0 %copy-start.1 = (s32[32,1,256]{2,1,0:T(1,128)}, s32[32,1,256]{2,1,0:T(1,128)S(1)}, u32[]{:S(2)}) copy-start(s32[32,1,256]{2,1,0:T(1,128)S(1)} %broadcast_and_fusion) | copy-start | bytes 98308
  34.7 6.0 %copy-start.27 = (s32[128,7,4]{0,2,1:T(4,128)S(1)}, s32[128,7,4]{0,2,1:T(4,128)}, u32[]{:S(2)}) copy-start(s32[128,7,4]{0,2,1:T(4,128)} %param.18) | copy-start | bytes 43012
  34.7 6.6 %copy-start.2 = (s32[256]{0:T(256)S(1)}, s32[256]{0:T(256)}, u32[]{:S(2)}) copy-start(s32[256]{0:T(256)} %param.19) | copy-start | bytes 3076
  34.7 7.3 %copy-start.4 = (bf16[1024,512]{1,0:T(8,128)(2,1)S(1)}, bf16[1024,512]{1,0:T(8,128)(2,1)}, u32[]{:S(2)}) copy-start(bf16[1024,512]{1,0:T(8,128)(2,1)} %hot_ref.1) | copy-start | bytes 3145732
  34.7 7.3 %copy-start.5 = (bf16[512,512]{1,0:T(8,128)(2,1)S(1)}, bf16[512,512]{1,0:T(8,128)(2,1)}, u32[]{:S(2)}) copy-start(bf16[512,512]{1,0:T(8,128)(2,1)} %weight_ref.1) | copy-start | bytes 1572868
  34.7 7.3 %copy-start.6 = (f32[128,256]{1,0:T(8,128)S(1)}, f32[128,256]{1,0:T(8,128)}, u32[]{:S(2)}) copy-start(f32[128,256]{1,0:T(8,128)} %grad_ref.1) | copy-start | bytes 393220
  34.7 7.3 %copy-start.7 = (bf16[128,512]{1,0:T(8,128)(2,1)S(1)}, bf16[128,512]{1,0:T(8,128)(2,1)}, u32[]{:S(2)}) copy-start(bf16[128,512]{1,0:T(8,128)(2,1)} %dense_ref.3) | copy-start | bytes 393220
  34.8 7.3 %copy-start.8 = (s32[128,8,4]{0,2,1:T(4,128)S(1)}, s32[128,8,4]{0,2,1:T(4,128)}, u32[]{:S(2)}) copy-start(s32[128,8,4]{0,2,1:T(4,128)} %param.20) | copy-start | bytes 49156
  34.8 28.0 %all-to-all-start.1 = ((bf16[32,112,128]{2,1,0:T(8,128)(2,1)}), bf16[32,112,128]{2,1,0:T(8,128)(2,1)}, u32[]{:S(2)}, u32[]{:S(2)}) async-start(bf16[32,112,128]{2,1,0:T(8,128)(2,1)} %shard_map.147), calls=%async_computation.1 | async-start | bytes 1835008 | tf_op jit(solution)/shard_map/all_to_all | solution.py:624
  44.7 1.0 copy-start.18
  45.6 1.0 copy-start.20
  46.6 1.0 copy-start.21
  47.6 0.9 copy-start.22
  48.5 0.7 copy-start.24
  49.2 0.7 copy-start.25
  74.7 8.1 %copy-start.12 = (s32[2]{0:T(128)S(1)}, s32[2]{0:T(128)}, u32[]{:S(2)}) copy-start(s32[2]{0:T(128)} %pad_add_fusion.place_ref) | copy-start | bytes 28
  74.7 8.1 %copy-start.17 = (bf16[13,128,512]{2,1,0:T(8,128)(2,1)S(1)}, bf16[13,128,512]{2,1,0:T(8,128)(2,1)}, u32[]{:S(2)}) copy-start(bf16[13,128,512]{2,1,0:T(8,128)(2,1)} %get-tuple-element.67.keep_ref) | copy-start | bytes 5111812
  74.7 8.1 %collective-permute-start = (bf16[13,128,512]{2,1,0:T(8,128)(2,1)}, bf16[13,128,512]{2,1,0:T(8,128)(2,1)S(1)}, u32[]{:S(2)}, u32[]{:S(2)}) collective-permute-start(bf16[13,128,512]{2,1,0:T(8,128)(2,1)} %get-tuple-element.68), channel_id=1, source_target_pairs={{0,1},{1,0},{2,3},{3,2},{4,5},{5,4},{6,7},{7,6},{8,9},{9,8},{10,11... | collective-permute-start | bytes 5111816 | tf_op jit(solution)/shard_map/ppermute | solution.py:616
  74.8 31.9 %all-to-all-start.2 = ((bf16[32,112,128]{2,1,0:T(8,128)(2,1)}), bf16[32,112,128]{2,1,0:T(8,128)(2,1)}, u32[]{:S(2)}, u32[]{:S(2)}) async-start(bf16[32,112,128]{2,1,0:T(8,128)(2,1)} %get-tuple-element.66), calls=%async_computation.2 | async-start | bytes 1835008 | tf_op jit(solution)/shard_map/all_to_all | solution.py:624
  85.6 9.5 %collective-permute-start.1 = (bf16[1024,128]{1,0:T(8,128)(2,1)S(1)}, bf16[1024,128]{1,0:T(8,128)(2,1)S(1)}, u32[]{:S(2)}, u32[]{:S(2)}) collective-permute-start(bf16[1024,128]{1,0:T(8,128)(2,1)S(1)} %get-tuple-element.70), channel_id=1, source_target_pairs={{0,2},{1,3},{2,4},{3,5},{4,6},{5,7},{6,0},{7,1},{8,10},{9,11},{10,... | collective-permute-start | bytes 786440 | tf_op jit(solution)/shard_map/ppermute | solution.py:620
  87.2 13.4 %collective-permute-start.2 = (bf16[1024,128]{1,0:T(8,128)(2,1)S(1)}, bf16[1024,128]{1,0:T(8,128)(2,1)S(1)}, u32[]{:S(2)}, u32[]{:S(2)}) collective-permute-start(bf16[1024,128]{1,0:T(8,128)(2,1)S(1)} %get-tuple-element.71), channel_id=1, source_target_pairs={{0,4},{1,5},{2,6},{3,7},{4,0},{5,1},{6,2},{7,3},{8,12},{9,13},{10,... | collective-permute-start | bytes 786440 | tf_op jit(solution)/shard_map/ppermute | solution.py:620
  89.9 10.7 %collective-permute-start.3 = (bf16[1024,128]{1,0:T(8,128)(2,1)S(1)}, bf16[1024,128]{1,0:T(8,128)(2,1)S(1)}, u32[]{:S(2)}, u32[]{:S(2)}) collective-permute-start(bf16[1024,128]{1,0:T(8,128)(2,1)S(1)} %get-tuple-element.72), channel_id=1, source_target_pairs={{0,6},{1,7},{2,0},{3,1},{4,2},{5,3},{6,4},{7,5},{8,14},{9,15},{10,... | collective-permute-start | bytes 786440 | tf_op jit(solution)/shard_map/ppermute | solution.py:620
  106.8 21.2 %all-to-all-start.3 = ((bf16[32,32,128]{2,1,0:T(8,128)(2,1)}), bf16[32,32,128]{2,1,0:T(8,128)(2,1)S(1)}, u32[]{:S(2)}, u32[]{:S(2)}) async-start(bf16[32,32,128]{2,1,0:T(8,128)(2,1)} %bitcast.12), calls=%async_computation.3 | async-start | bytes 524288 | tf_op jit(solution)/shard_map/all_to_all | solution.py:624
  128.0 2.2 %copy-start.13 = (s32[2]{0:T(128)S(1)}, s32[2]{0:T(128)}, u32[]{:S(2)}) copy-start(s32[2]{0:T(128)} %pad_add_fusion.place_ref) | copy-start | bytes 28
  128.0 2.2 %copy-start.15 = (bf16[2,1024,128]{2,1,0:T(8,128)(2,1)S(1)}, bf16[2,1024,128]{2,1,0:T(8,128)(2,1)}, u32[]{:S(2)}) copy-start(bf16[2,1024,128]{2,1,0:T(8,128)(2,1)} %get-tuple-element.74.kept_ref) | copy-start | bytes 1572868
  128.0 2.2 %collective-permute-start.4 = (bf16[2,1024,128]{2,1,0:T(8,128)(2,1)}, bf16[2,1024,128]{2,1,0:T(8,128)(2,1)S(1)}, u32[]{:S(2)}, u32[]{:S(2)}) collective-permute-start(bf16[2,1024,128]{2,1,0:T(8,128)(2,1)} %get-tuple-element.77), channel_id=1, source_target_pairs={{0,1},{1,0},{2,3},{3,2},{4,5},{5,4},{6,7},{7,6},{8,9},{9,8},{10,11... | collective-permute-start | bytes 1572872 | tf_op jit(solution)/shard_map/ppermute | solution.py:616
  128.1 1.9 %collective-permute-start.5 = (bf16[32,128]{1,0:T(8,128)(2,1)S(1)}, bf16[32,128]{1,0:T(8,128)(2,1)S(1)}, u32[]{:S(2)}, u32[]{:S(2)}) collective-permute-start(bf16[32,128]{1,0:T(8,128)(2,1)S(1)} %shard_map.152.mine_ref), channel_id=1, source_target_pairs={{0,1},{1,0},{2,3},{3,2},{4,5},{5,4},{6,7},{7,6},{8,9},{9,8},{10,11... | collective-permute-start | bytes 24584 | tf_op jit(solution)/shard_map/ppermute | solution.py:616
  130.2 1.2 copy-start.28
  130.2 1.4 copy-start.29
  130.2 5.0 %copy-start.19 = (bf16[8,128,512]{2,1,0:T(8,128)(2,1)S(1)}, bf16[8,128,512]{2,1,0:T(8,128)(2,1)}, u32[]{:S(2)}) copy-start(bf16[8,128,512]{2,1,0:T(8,128)(2,1)} %copy-done.18) | copy-start | bytes 3145732
  130.2 5.0 %copy-start.23 = (bf16[7,128,512]{2,1,0:T(8,128)(2,1)S(1)}, bf16[7,128,512]{2,1,0:T(8,128)(2,1)}, u32[]{:S(2)}) copy-start(bf16[7,128,512]{2,1,0:T(8,128)(2,1)} %get-tuple-element.86.cold_ref) | copy-start | bytes 2752516
  130.2 5.0 %copy-start.26 = (bf16[128,512]{1,0:T(8,128)(2,1)S(1)}, bf16[128,512]{1,0:T(8,128)(2,1)}, u32[]{:S(2)}) copy-start(bf16[128,512]{1,0:T(8,128)(2,1)} %copy-done.25) | copy-start | bytes 393220
  131.4 10.4 %copy-start.14 = (bf16[2,2,1024,128]{3,2,1,0:T(8,128)(2,1)S(1)}, bf16[2,2,1024,128]{3,2,1,0:T(8,128)(2,1)}, u32[]{:S(2)}) copy-start(bf16[2,2,1024,128]{3,2,1,0:T(8,128)(2,1)} %get-tuple-element.88.kept_ref) | copy-start | bytes 3145732
  131.4 10.4 %collective-permute-start.8 = (bf16[2,2,1024,128]{3,2,1,0:T(8,128)(2,1)S(1)}, bf16[2,2,1024,128]{3,2,1,0:T(8,128)(2,1)S(1)}, u32[]{:S(2)}, u32[]{:S(2)}) collective-permute-start(bf16[2,2,1024,128]{3,2,1,0:T(8,128)(2,1)S(1)} %copy-done.28), channel_id=1, source_target_pairs={{0,1},{1,0},{2,3},{3,2},{4,5},{5,4},{6,7},{7,6},{8,9},{9,8},{10,11... | collective-permute-start | bytes 3145736 | tf_op jit(solution)/shard_map/ppermute | solution.py:616
  131.6 10.3 %collective-permute-start.9 = (bf16[2,1024,128]{2,1,0:T(8,128)(2,1)S(1)}, bf16[2,1024,128]{2,1,0:T(8,128)(2,1)S(1)}, u32[]{:S(2)}, u32[]{:S(2)}) collective-permute-start(bf16[2,1024,128]{2,1,0:T(8,128)(2,1)S(1)} %copy-done.29), channel_id=1, source_target_pairs={{0,1},{1,0},{2,3},{3,2},{4,5},{5,4},{6,7},{7,6},{8,9},{9,8},{10,11... | collective-permute-start | bytes 1572872 | tf_op jit(solution)/shard_map/ppermute | solution.py:616
  131.9 9.9 %collective-permute-start.6 = (bf16[1088,128]{1,0:T(8,128)(2,1)S(1)}, bf16[1088,128]{1,0:T(8,128)(2,1)S(1)}, u32[]{:S(2)}, u32[]{:S(2)}) collective-permute-start(bf16[1088,128]{1,0:T(8,128)(2,1)S(1)} %get-tuple-element.100.own_ref), channel_id=1, source_target_pairs={{0,2},{1,3},{2,4},{3,5},{4,6},{5,7},{6,0},{7,1},{8,10},{9,11},{10,... | collective-permute-start | bytes 835592 | tf_op jit(solution)/shard_map/ppermute | solution.py:620
  133.4 8.4 %collective-permute-start.7 = (bf16[1088,128]{1,0:T(8,128)(2,1)S(1)}, bf16[1088,128]{1,0:T(8,128)(2,1)S(1)}, u32[]{:S(2)}, u32[]{:S(2)}) collective-permute-start(bf16[1088,128]{1,0:T(8,128)(2,1)S(1)} %get-tuple-element.80), channel_id=1, source_target_pairs={{0,6},{1,7},{2,0},{3,1},{4,2},{5,3},{6,4},{7,5},{8,14},{9,15},{10,... | collective-permute-start | bytes 835592 | tf_op jit(solution)/shard_map/ppermute | solution.py:620
  141.9 3.6 %copy-start.16 = (f32[2,1024,128]{2,1,0:T(8,128)S(1)}, f32[2,1024,128]{2,1,0:T(8,128)}, u32[]{:S(2)}) copy-start(f32[2,1024,128]{2,1,0:T(8,128)} %get-tuple-element.96.kept_ref) | copy-start | bytes 3145732
  142.2 14.8 %collective-permute-start.10 = (bf16[2112,128]{1,0:T(8,128)(2,1)S(1)}, bf16[2112,128]{1,0:T(8,128)(2,1)S(1)}, u32[]{:S(2)}, u32[]{:S(2)}) collective-permute-start(bf16[2112,128]{1,0:T(8,128)(2,1)S(1)} %get-tuple-element.98), channel_id=1, source_target_pairs={{0,2},{1,3},{2,4},{3,5},{4,6},{5,7},{6,0},{7,1},{8,10},{9,11},{10,... | collective-permute-start | bytes 1622024 | tf_op jit(solution)/shard_map/ppermute | solution.py:620
  143.8 12.5 %collective-permute-start.11 = (bf16[2048,128]{1,0:T(8,128)(2,1)S(1)}, bf16[2048,128]{1,0:T(8,128)(2,1)S(1)}, u32[]{:S(2)}, u32[]{:S(2)}) collective-permute-start(bf16[2048,128]{1,0:T(8,128)(2,1)S(1)} %get-tuple-element.99), channel_id=1, source_target_pairs={{0,6},{1,7},{2,0},{3,1},{4,2},{5,3},{6,4},{7,5},{8,14},{9,15},{10,... | collective-permute-start | bytes 1572872 | tf_op jit(solution)/shard_map/ppermute | solution.py:620
